TPU v7x, 128 devices: a whole 4x4x4 slice. The times are simulated.
128 devices in a mesh: px: 8 (over z, core), py: 16 (over y, x).
Axes of the slice: x: 4, y: 4, z: 4, core: 2. Of those that a mesh axis runs over, the one named last changes fastest.
Arguments:
- background_field: float32 [64, 512, 1024], P('px', 'py'), may hold values from -6 to 6
- perturbation: float32 [64, 512, 1024], P('px', 'py'), may hold values from -6 to 6
- permittivity: float32 [64, 512, 1024], P('px', 'py'), may hold values from 0.5 to 2
- probe_nodes: int32 [4, 131072], P(None, ('px', 'py')), may hold values from 0 to 262143
- probe_weights: float32 [4, 131072], P(None, ('px', 'py')), may hold values from 0.1 to 1
- probe_owner: int32 [131072, 1], P(('px', 'py')), may hold values from 0 to 127; in each aligned block of 1024 rows (0 to 1023, 1024 to 2047, ...) at most 16 rows name the same one
- probe_sensor: int32 [131072], P(('px', 'py')), may hold values from 0 to 7
- sensor_weight: float32 [1024], P(('px', 'py')), may hold values from 0.2 to 5
Outputs:
- hess_vec: float32 [64, 512, 1024], P('px', 'py')
Inputs may be any that keep to these rules, and one draw needn't show every extreme that they name: `probe_nodes`: each probe's nodes lie in the block of the device that holds the probe. `probe_owner`: of the probes of one device at most 16 name the same owner, and in every draw some owner is named by exactly 16 of them.
All inputs are finite; a program needn't handle non-finite values.
Results may differ from a plain program's by a relative error of at most 0.00025.
Values sent between devices are 32-bit elements; how exact they have to be, the bound alone decides.
No kernel may reach another device: no remote copies, remote signals or barrier semaphores. Data moves between devices by JAX's collectives and lax.ppermute only.
A program may use at most 64 MiB of HBM per device.

v0:
```python
import jax
import jax.numpy as jnp
from jax import lax
from jax.sharding import PartitionSpec as P

SWEEPS = 4


mass_term = 1.0
bound_low = 1.0
bound_high = 25.0


def padded_2(block, sides, width):
    for axis, dim in sides:
        count = lax.axis_size(axis)
        forward = [(i, i + 1) for i in range(count - 1)]
        backward = [(target, source) for source, target in forward]
        low = lax.ppermute(
            lax.slice_in_dim(block, block.shape[dim] - width, None, axis=dim), axis, forward
        )
        high = lax.ppermute(lax.slice_in_dim(block, 0, width, axis=dim), axis, backward)
        block = jnp.concatenate([low, block, high], axis=dim)
    return block


def crop_rim(array, depth):
    return array[depth : array.shape[0] - depth, depth : array.shape[1] - depth]


def inside_line(count, index, total, depth):
    positions = index * count - depth + jnp.arange(count + 2 * depth, dtype=jnp.int32)
    return ((positions >= 0) & (positions < total)).astype(jnp.float32)


def face_masks(row_inside, col_inside):
    row_faces = (row_inside[1:] * row_inside[:-1])[:, None] * col_inside[None, :]
    col_faces = row_inside[:, None] * (col_inside[1:] * col_inside[:-1])[None, :]
    return (row_faces, col_faces)


def face_coefs(padded, row_inside, col_inside):
    row_faces, col_faces = face_masks(row_inside, col_inside)
    cell_inside = row_inside[:, None] * col_inside[None, :]
    along_rows = 0.5 * (padded[1:] + padded[:-1]) * row_faces[:, :, None]
    along_cols = 0.5 * (padded[:, 1:] + padded[:, :-1]) * col_faces[:, :, None]
    along_depth = 0.5 * (padded[:, :, 1:] + padded[:, :, :-1]) * cell_inside[:, :, None]
    return (along_rows, along_cols, along_depth)


def apply_local(field, coefs, mass_value, depth):
    along_rows = crop_rim(coefs[0], depth)
    along_cols = crop_rim(coefs[1], depth)
    along_depth = crop_rim(coefs[2], depth + 1)
    inner = field[1:-1, 1:-1]
    row_flux = along_rows[:, 1:-1] * (field[1:, 1:-1] - field[:-1, 1:-1])
    col_flux = along_cols[1:-1] * (field[1:-1, 1:] - field[1:-1, :-1])
    depth_flux = along_depth * (inner[:, :, 1:] - inner[:, :, :-1])
    zero_plane = jnp.zeros_like(depth_flux[:, :, :1])
    result = mass_value * inner - row_flux[1:] + row_flux[:-1] - col_flux[:, 1:] + col_flux[:, :-1]
    return (
        result
        - jnp.concatenate([depth_flux, zero_plane], 2)
        + jnp.concatenate([zero_plane, depth_flux], 2)
    )


def cheb_constants():
    centre = 0.5 * (bound_high + bound_low)
    half_width = 0.5 * (bound_high - bound_low)
    return (centre, half_width, centre / half_width)


def solve_faces(source, coefs):
    centre, half_width, spread = cheb_constants()
    iterate = jnp.zeros_like(source)
    remain = source
    search = source / centre
    ratio_now = 1.0 / spread
    for sweep in range(SWEEPS):
        iterate = iterate + search
        if sweep < SWEEPS - 1:
            search_pad = padded_2(search, (("px", 0), ("py", 1)), 1)
            remain = remain - apply_local(search_pad, coefs, mass_term, 0)
            ratio_next = 1.0 / (2.0 * spread - ratio_now)
            search = ratio_next * ratio_now * search + 2.0 * ratio_next / half_width * remain
            ratio_now = ratio_next
    return iterate


def sensitivity(back_pad, adj_pad, row_inside, col_inside):
    row_faces, col_faces = face_masks(row_inside, col_inside)
    row_term = (
        row_faces[:, 1:-1, None]
        * (back_pad[1:, 1:-1] - back_pad[:-1, 1:-1])
        * (adj_pad[1:, 1:-1] - adj_pad[:-1, 1:-1])
    )
    col_term = (
        col_faces[1:-1, :, None]
        * (back_pad[1:-1, 1:] - back_pad[1:-1, :-1])
        * (adj_pad[1:-1, 1:] - adj_pad[1:-1, :-1])
    )
    inner_back = back_pad[1:-1, 1:-1]
    inner_adj = adj_pad[1:-1, 1:-1]
    depth_term = (inner_back[:, :, 1:] - inner_back[:, :, :-1]) * (
        inner_adj[:, :, 1:] - inner_adj[:, :, :-1]
    )
    zero_plane = jnp.zeros_like(depth_term[:, :, :1])
    total = row_term[1:] + row_term[:-1] + col_term[:, 1:] + col_term[:, :-1]
    total = (
        total
        + jnp.concatenate([depth_term, zero_plane], 2)
        + jnp.concatenate([zero_plane, depth_term], 2)
    )
    return -0.5 * total


def body(
    background_field,
    perturbation,
    permittivity,
    probe_nodes,
    probe_weights,
    probe_owner,
    probe_sensor,
    sensor_weight,
):
    rows_dev, cols_dev, depth_dev = background_field.shape
    size_px = lax.axis_size("px")
    size_py = lax.axis_size("py")
    index_px = lax.axis_index("px")
    index_py = lax.axis_index("py")
    rows_one = inside_line(rows_dev, index_px, rows_dev * size_px, 1)
    cols_one = inside_line(cols_dev, index_py, cols_dev * size_py, 1)
    back_pad, perturb_pad, permit_pad = (
        padded_2(background_field, (("px", 0), ("py", 1)), 1),
        padded_2(perturbation, (("px", 0), ("py", 1)), 1),
        padded_2(permittivity, (("px", 0), ("py", 1)), 1),
    )
    permit_coefs = face_coefs(permit_pad, rows_one, cols_one)

    def solve_field(source):
        return solve_faces(source, permit_coefs)

    perturb_coefs = face_coefs(perturb_pad, rows_one, cols_one)
    tangent = solve_field(-apply_local(back_pad, perturb_coefs, 0.0, 0))
    flat = tangent.reshape(-1)
    values = jnp.sum(probe_weights * flat[probe_nodes], axis=0)
    owner_ids = probe_owner[:, 0]
    sensors_dev = sensor_weight.shape[0]
    device_count = size_px * size_py
    probes = probe_sensor.shape[0]
    capacity = max(2, 2 * probes // device_count)
    owner_hot = (owner_ids[:, None] == jnp.arange(device_count, dtype=jnp.int32)[None, :]).astype(
        jnp.int32
    )
    before_count = jnp.sum((jnp.cumsum(owner_hot, axis=0) - owner_hot) * owner_hot, axis=1)
    slot_index = owner_ids * capacity + before_count
    send_values = (
        jnp.zeros((device_count * capacity,), jnp.float32)
        .at[slot_index]
        .set(values)
        .reshape(device_count, capacity)
    )
    send_sensor = (
        jnp.zeros((device_count * capacity,), jnp.int32)
        .at[slot_index]
        .set(probe_sensor)
        .reshape(device_count, capacity)
    )
    got_values, got_sensor = (
        lax.all_to_all(send_values, ("px", "py"), split_axis=0, concat_axis=0, tiled=True),
        lax.all_to_all(send_sensor, ("px", "py"), split_axis=0, concat_axis=0, tiled=True),
    )
    sensor_hot = (
        got_sensor[:, :, None] == jnp.arange(sensors_dev, dtype=jnp.int32)[None, None, :]
    ).astype(jnp.float32)
    readings = jnp.einsum("dcs,dc->s", sensor_hot, got_values, precision=lax.Precision.HIGHEST)
    weighted = readings * sensor_weight
    reply = jnp.einsum("dcs,s->dc", sensor_hot, weighted, precision=lax.Precision.HIGHEST)
    back_values = lax.all_to_all(reply, ("px", "py"), split_axis=0, concat_axis=0, tiled=True)
    returned = back_values.reshape(-1)[slot_index]
    source = (
        jnp.zeros(flat.shape, jnp.float32)
        .at[probe_nodes.reshape(-1)]
        .add((probe_weights * returned[None, :]).reshape(-1))
    )
    adjoint = solve_field(source.reshape(tangent.shape))
    adj_pad = padded_2(adjoint, (("px", 0), ("py", 1)), 1)
    return sensitivity(back_pad, adj_pad, rows_one, cols_one)


def solution(mesh):
    placed = (
        P("px", "py", None),
        P("px", "py", None),
        P("px", "py", None),
        P(None, ("px", "py")),
        P(None, ("px", "py")),
        P(("px", "py"), None),
        P(("px", "py")),
        P(("px", "py")),
    )
    return jax.shard_map(
        body, mesh=mesh, in_specs=placed, out_specs=P("px", "py", None), check_vma=False
    )
```

profile of v0, /device:TPU:1, one launch (start us, length us, event | category | flops | bytes accessed | tf_op | source)
XLA Modules:
  0.0 322.8 jit_solution(16359432580490612976)
XLA Ops:
  0.0 1.7 fusion.107
  1.7 4.9 %collective-permute-start.2 = (f32[1,32,1024]{2,1,0:T(8,128)S(1)}, f32[1,32,1024]{2,1,0:T(8,128)S(1)}, u32[]{:S(2)}, u32[]{:S(2)}) collective-permute-start(f32[1,32,1024]{2,1,0:T(8,128)S(1)} %get-tuple-element.66), channel_id=1, source_target_pairs={{0,16},{16,32},{32,48},{48,64},{64,80},{80,96},{96,112},{1,17},{17... | collective-permute-start | bytes 393224 | tf_op jit(solution)/shard_map/ppermute | solution.py:19
  6.6 1.9 collective-permute-start.3
  9.5 3.6 %collective-permute-start.1 = (f32[1,32,1024]{2,1,0:T(8,128)S(1)}, f32[1,32,1024]{2,1,0:T(8,128)S(1)}, u32[]{:S(2)}, u32[]{:S(2)}) collective-permute-start(f32[1,32,1024]{2,1,0:T(8,128)S(1)} %get-tuple-element.64), channel_id=1, source_target_pairs={{0,16},{16,32},{32,48},{48,64},{64,80},{80,96},{96,112},{1,17},{17... | collective-permute-start | bytes 393224 | tf_op jit(solution)/shard_map/ppermute | solution.py:19
  13.2 1.9 collective-permute-start
  16.1 3.6 %collective-permute-start.8 = (f32[1,32,1024]{2,1,0:T(8,128)S(1)}, f32[1,32,1024]{2,1,0:T(8,128)S(1)}, u32[]{:S(2)}, u32[]{:S(2)}) collective-permute-start(f32[1,32,1024]{2,1,0:T(8,128)S(1)} %get-tuple-element.62), channel_id=1, source_target_pairs={{0,16},{16,32},{32,48},{48,64},{64,80},{80,96},{96,112},{1,17},{17... | collective-permute-start | bytes 393224 | tf_op jit(solution)/shard_map/ppermute | solution.py:19
  20.7 4.5 %scatter_custom_fusion = s32[2048]{0:T(1024)S(1)} fusion(s32[1024]{0:T(1024)S(1)} %bitcast.55, s32[1024]{0:T(1024)} %param.14, s32[]{:T(128)} %constant.26.clone.1), kind=kCustom, calls=%fused_computation.243 | custom fusion | bytes 8704 | tf_op jit(solution)/shard_map/scatter | solution.py:168
  25.9 9.7 %all-to-all-start = ((s32[128,1,16]{2,1,0:T(1,128)}), s32[128,1,16]{2,1,0:T(1,128)S(1)}, u32[]{:S(2)}, u32[]{:S(2)}) async-start(s32[128,1,16]{2,1,0:T(1,128)} %bitcast.11), calls=%async_computation | async-start | bytes 131072 | tf_op jit(solution)/shard_map/all_to_all | solution.py:173
  38.5 3.0 collective-permute-start.9
  43.1 4.0 %collective-permute-start.4 = (f32[10,1,1024]{2,1,0:T(1,128)S(1)}, f32[10,1,1024]{2,1,0:T(1,128)S(1)}, u32[]{:S(2)}, u32[]{:S(2)}) collective-permute-start(f32[10,1,1024]{2,1,0:T(1,128)S(1)} %get-tuple-element.45), channel_id=1, source_target_pairs={{0,1},{1,2},{2,3},{3,4},{4,5},{5,6},{6,7},{7,8},{8,9},{9,10},{10,1... | collective-permute-start | bytes 122888 | tf_op jit(solution)/shard_map/ppermute | solution.py:19
  47.4 2.7 collective-permute-start.7
  53.0 4.6 %collective-permute-start.10 = (f32[10,1,1024]{2,1,0:T(1,128)S(1)}, f32[10,1,1024]{2,1,0:T(1,128)S(1)}, u32[]{:S(2)}, u32[]{:S(2)}) collective-permute-start(f32[10,1,1024]{2,1,0:T(1,128)S(1)} %get-tuple-element.41), channel_id=1, source_target_pairs={{0,1},{1,2},{2,3},{3,4},{4,5},{5,6},{6,7},{7,8},{8,9},{9,10},{10,1... | collective-permute-start | bytes 122888 | tf_op jit(solution)/shard_map/ppermute | solution.py:19
  62.3 3.0 collective-permute-start.12
  65.3 3.9 %collective-permute-start.13 = (f32[1,32,1024]{2,1,0:T(8,128)S(1)}, f32[1,32,1024]{2,1,0:T(8,128)S(1)}, u32[]{:S(2)}, u32[]{:S(2)}) collective-permute-start(f32[1,32,1024]{2,1,0:T(8,128)S(1)} %get-tuple-element.59), channel_id=1, source_target_pairs={{0,16},{16,32},{32,48},{48,64},{64,80},{80,96},{96,112},{1,17},{17... | collective-permute-start | bytes 393224 | tf_op jit(solution)/shard_map/ppermute | solution.py:19
  71.2 4.4 %collective-permute-start.15 = (f32[10,1,1024]{2,1,0:T(1,128)S(1)}, f32[10,1,1024]{2,1,0:T(1,128)S(1)}, u32[]{:S(2)}, u32[]{:S(2)}) collective-permute-start(f32[10,1,1024]{2,1,0:T(1,128)S(1)} %get-tuple-element.40), channel_id=1, source_target_pairs={{0,1},{1,2},{2,3},{3,4},{4,5},{5,6},{6,7},{7,8},{8,9},{9,10},{10,1... | collective-permute-start | bytes 122888 | tf_op jit(solution)/shard_map/ppermute | solution.py:19
  77.3 3.6 %collective-permute-done.14 = f32[10,1,1024]{2,1,0:T(1,128)S(1)} collective-permute-done((f32[10,1,1024]{2,1,0:T(1,128)S(1)}, f32[10,1,1024]{2,1,0:T(1,128)S(1)}, u32[]{:S(2)}, u32[]{:S(2)}) %collective-permute-start.14) | collective-permute-done | bytes 40992 | tf_op jit(solution)/shard_map/ppermute | solution.py:22
  82.2 1.9 collective-permute-start.16
  84.2 5.5 %collective-permute-start.17 = (f32[1,32,1024]{2,1,0:T(8,128)S(1)}, f32[1,32,1024]{2,1,0:T(8,128)S(1)}, u32[]{:S(2)}, u32[]{:S(2)}) collective-permute-start(f32[1,32,1024]{2,1,0:T(8,128)S(1)} %get-tuple-element.57), channel_id=1, source_target_pairs={{0,16},{16,32},{32,48},{48,64},{64,80},{80,96},{96,112},{1,17},{17... | collective-permute-start | bytes 393224 | tf_op jit(solution)/shard_map/ppermute | solution.py:19
  91.7 5.4 %collective-permute-start.19 = (f32[10,1,1024]{2,1,0:T(1,128)S(1)}, f32[10,1,1024]{2,1,0:T(1,128)S(1)}, u32[]{:S(2)}, u32[]{:S(2)}) collective-permute-start(f32[10,1,1024]{2,1,0:T(1,128)S(1)} %get-tuple-element.38), channel_id=1, source_target_pairs={{0,1},{1,2},{2,3},{3,4},{4,5},{5,6},{6,7},{7,8},{8,9},{9,10},{10,1... | collective-permute-start | bytes 122888 | tf_op jit(solution)/shard_map/ppermute | solution.py:19
  98.9 5.7 %collective-permute-done.18 = f32[10,1,1024]{2,1,0:T(1,128)S(1)} collective-permute-done((f32[10,1,1024]{2,1,0:T(1,128)S(1)}, f32[10,1,1024]{2,1,0:T(1,128)S(1)}, u32[]{:S(2)}, u32[]{:S(2)}) %collective-permute-start.18) | collective-permute-done | bytes 40992 | tf_op jit(solution)/shard_map/ppermute | solution.py:22
  106.0 1.9 collective-permute-start.20
  107.9 5.5 %collective-permute-start.21 = (f32[1,32,1024]{2,1,0:T(8,128)S(1)}, f32[1,32,1024]{2,1,0:T(8,128)S(1)}, u32[]{:S(2)}, u32[]{:S(2)}) collective-permute-start(f32[1,32,1024]{2,1,0:T(8,128)S(1)} %get-tuple-element.55), channel_id=1, source_target_pairs={{0,16},{16,32},{32,48},{48,64},{64,80},{80,96},{96,112},{1,17},{17... | collective-permute-start | bytes 393224 | tf_op jit(solution)/shard_map/ppermute | solution.py:19
  115.4 5.7 %collective-permute-start.23 = (f32[10,1,1024]{2,1,0:T(1,128)S(1)}, f32[10,1,1024]{2,1,0:T(1,128)S(1)}, u32[]{:S(2)}, u32[]{:S(2)}) collective-permute-start(f32[10,1,1024]{2,1,0:T(1,128)S(1)} %get-tuple-element.36), channel_id=1, source_target_pairs={{0,1},{1,2},{2,3},{3,4},{4,5},{5,6},{6,7},{7,8},{8,9},{9,10},{10,1... | collective-permute-start | bytes 122888 | tf_op jit(solution)/shard_map/ppermute | solution.py:19
  122.8 3.4 %collective-permute-done.22 = f32[10,1,1024]{2,1,0:T(1,128)S(1)} collective-permute-done((f32[10,1,1024]{2,1,0:T(1,128)S(1)}, f32[10,1,1024]{2,1,0:T(1,128)S(1)}, u32[]{:S(2)}, u32[]{:S(2)}) %collective-permute-start.22) | collective-permute-done | bytes 40992 | tf_op jit(solution)/shard_map/ppermute | solution.py:22
  127.9 40.7 %gather_fusion = f32[4096]{0:T(1024)} fusion(f32[262144]{0:T(1024)S(1)} %bitcast.45, s32[4096]{0:T(1024)} %bitcast_clamp_fusion), kind=kCustom, calls=%fused_computation | custom fusion | bytes 49152 | tf_op jit(solution)/shard_map/gather | solution.py:148
  170.0 4.5 %scatter_custom_fusion.1 = f32[2048]{0:T(1024)S(1)} fusion(s32[1024]{0:T(1024)} %bitcast.56, f32[1024]{0:T(1024)S(1)} %multiply_reduce_fusion, f32[]{:T(128)} %constant.31.clone.1), kind=kCustom, calls=%fused_computation.241 | custom fusion | bytes 8704 | tf_op jit(solution)/shard_map/scatter | solution.py:162
  175.2 13.6 %all-to-all-start.1 = ((f32[128,1,16]{2,1,0:T(1,128)}), f32[128,1,16]{2,1,0:T(1,128)S(1)}, u32[]{:S(2)}, u32[]{:S(2)}) async-start(f32[128,1,16]{2,1,0:T(1,128)} %bitcast.13), calls=%async_computation.1 | async-start | bytes 131072 | tf_op jit(solution)/shard_map/all_to_all | solution.py:172
  189.5 8.8 %all-to-all-done.1 = f32[128,1,16]{2,1,0:T(1,128)S(1)} async-done(((f32[128,1,16]{2,1,0:T(1,128)}), f32[128,1,16]{2,1,0:T(1,128)S(1)}, u32[]{:S(2)}, u32[]{:S(2)}) %all-to-all-start.1) | async-done | bytes 8224 | tf_op jit(solution)/shard_map/all_to_all | solution.py:172
  200.9 4.5 %all-to-all-start.2 = ((f32[128,1,16]{2,1,0:T(1,128)}), f32[128,1,16]{2,1,0:T(1,128)S(1)}, u32[]{:S(2)}, u32[]{:S(2)}) async-start(f32[128,1,16]{2,1,0:T(1,128)} %bitcast.16), calls=%async_computation.2 | async-start | bytes 131072 | tf_op jit(solution)/shard_map/all_to_all | solution.py:181
  207.5 7.4 %all-to-all-done.2 = f32[128,1,16]{2,1,0:T(1,128)S(1)} async-done(((f32[128,1,16]{2,1,0:T(1,128)}), f32[128,1,16]{2,1,0:T(1,128)S(1)}, u32[]{:S(2)}, u32[]{:S(2)}) %all-to-all-start.2) | async-done | bytes 8224 | tf_op jit(solution)/shard_map/all_to_all | solution.py:181
  216.3 6.2 %gather_fusion.1 = f32[1024]{0:T(1024)S(1)} fusion(f32[2048]{0:T(1024)S(1)} %reshape.175, s32[1024]{0:T(1024)S(1)} %broadcast_clamp_fusion), kind=kCustom, calls=%fused_computation.1 | custom fusion | bytes 12288 | tf_op jit(solution)/shard_map/gather | solution.py:182
  222.5 22.9 %scatter_custom_fusion.2 = f32[262144]{0:T(1024)} fusion(s32[4096]{0:T(1024)S(1)} %bitcast.58, f32[4096]{0:T(1024)S(1)} %bitcast.59, f32[]{:T(128)} %constant.31.clone.1), kind=kCustom, calls=%fused_computation.194 | custom fusion | flops 4096 | bytes 1048580 | tf_op jit(solution)/shard_map/scatter-add | solution.py:186
  247.0 3.0 collective-permute-start.24
  250.0 2.7 collective-permute-start.25
  254.7 2.2 collective-permute-start.27
  258.7 3.0 collective-permute-done.26
  262.9 2.1 collective-permute-start.28
  265.0 5.6 %collective-permute-start.29 = (f32[1,32,1024]{2,1,0:T(8,128)S(1)}, f32[1,32,1024]{2,1,0:T(8,128)S(1)}, u32[]{:S(2)}, u32[]{:S(2)}) collective-permute-start(f32[1,32,1024]{2,1,0:T(8,128)S(1)} %get-tuple-element.51), channel_id=1, source_target_pairs={{0,16},{16,32},{32,48},{48,64},{64,80},{80,96},{96,112},{1,17},{17... | collective-permute-start | bytes 393224 | tf_op jit(solution)/shard_map/ppermute | solution.py:19
  272.6 2.3 collective-permute-start.31
  276.4 3.1 collective-permute-done.30
  281.0 1.9 collective-permute-start.32
  282.9 5.8 %collective-permute-start.33 = (f32[1,32,1024]{2,1,0:T(8,128)S(1)}, f32[1,32,1024]{2,1,0:T(8,128)S(1)}, u32[]{:S(2)}, u32[]{:S(2)}) collective-permute-start(f32[1,32,1024]{2,1,0:T(8,128)S(1)} %get-tuple-element.49), channel_id=1, source_target_pairs={{0,16},{16,32},{32,48},{48,64},{64,80},{80,96},{96,112},{1,17},{17... | collective-permute-start | bytes 393224 | tf_op jit(solution)/shard_map/ppermute | solution.py:19
  290.7 5.2 %collective-permute-start.35 = (f32[10,1,1024]{2,1,0:T(1,128)S(1)}, f32[10,1,1024]{2,1,0:T(1,128)S(1)}, u32[]{:S(2)}, u32[]{:S(2)}) collective-permute-start(f32[10,1,1024]{2,1,0:T(1,128)S(1)} %get-tuple-element.30), channel_id=1, source_target_pairs={{0,1},{1,2},{2,3},{3,4},{4,5},{5,6},{6,7},{7,8},{8,9},{9,10},{10,1... | collective-permute-start | bytes 122888 | tf_op jit(solution)/shard_map/ppermute | solution.py:19
  297.5 3.4 %collective-permute-done.34 = f32[10,1,1024]{2,1,0:T(1,128)S(1)} collective-permute-done((f32[10,1,1024]{2,1,0:T(1,128)S(1)}, f32[10,1,1024]{2,1,0:T(1,128)S(1)}, u32[]{:S(2)}, u32[]{:S(2)}) %collective-permute-start.34) | collective-permute-done | bytes 40992 | tf_op jit(solution)/shard_map/ppermute | solution.py:22
  302.4 1.9 collective-permute-start.36
  304.3 5.5 %collective-permute-start.37 = (f32[1,32,1024]{2,1,0:T(8,128)S(1)}, f32[1,32,1024]{2,1,0:T(8,128)S(1)}, u32[]{:S(2)}, u32[]{:S(2)}) collective-permute-start(f32[1,32,1024]{2,1,0:T(8,128)S(1)} %get-tuple-element.47), channel_id=1, source_target_pairs={{0,16},{16,32},{32,48},{48,64},{64,80},{80,96},{96,112},{1,17},{17... | collective-permute-start | bytes 393224 | tf_op jit(solution)/shard_map/ppermute | solution.py:19
  311.8 3.7 %collective-permute-start.39 = (f32[10,1,1024]{2,1,0:T(1,128)S(1)}, f32[10,1,1024]{2,1,0:T(1,128)S(1)}, u32[]{:S(2)}, u32[]{:S(2)}) collective-permute-start(f32[10,1,1024]{2,1,0:T(1,128)S(1)} %get-tuple-element.28), channel_id=1, source_target_pairs={{0,1},{1,2},{2,3},{3,4},{4,5},{5,6},{6,7},{7,8},{8,9},{9,10},{10,1... | collective-permute-start | bytes 122888 | tf_op jit(solution)/shard_map/ppermute | solution.py:19
  317.4 3.4 %collective-permute-done.38 = f32[10,1,1024]{2,1,0:T(1,128)S(1)} collective-permute-done((f32[10,1,1024]{2,1,0:T(1,128)S(1)}, f32[10,1,1024]{2,1,0:T(1,128)S(1)}, u32[]{:S(2)}, u32[]{:S(2)}) %collective-permute-start.38) | collective-permute-done | bytes 40992 | tf_op jit(solution)/shard_map/ppermute | solution.py:22
  (197 shorter events, 62.0 us)
Async XLA Ops:
  0.0 19.7 %copy-start.21 = (s32[1024,1]{0,1:T(1,128)S(1)}, s32[1024,1]{0,1:T(1,128)}, u32[]{:S(2)}) copy-start(s32[1024,1]{0,1:T(1,128)} %param.13) | copy-start | bytes 12292
  1.7 36.8 %collective-permute-start.2 = (f32[1,32,1024]{2,1,0:T(8,128)S(1)}, f32[1,32,1024]{2,1,0:T(8,128)S(1)}, u32[]{:S(2)}, u32[]{:S(2)}) collective-permute-start(f32[1,32,1024]{2,1,0:T(8,128)S(1)} %get-tuple-element.66), channel_id=1, source_target_pairs={{0,16},{16,32},{32,48},{48,64},{64,80},{80,96},{96,112},{1,17},{17... | collective-permute-start | bytes 393224 | tf_op jit(solution)/shard_map/ppermute | solution.py:19
  6.6 35.0 %collective-permute-start.3 = (f32[1,32,1024]{2,1,0:T(8,128)}, f32[1,32,1024]{2,1,0:T(8,128)S(1)}, u32[]{:S(2)}, u32[]{:S(2)}) collective-permute-start(f32[1,32,1024]{2,1,0:T(8,128)} %get-tuple-element.65), channel_id=1, source_target_pairs={{16,0},{32,16},{48,32},{64,48},{80,64},{96,80},{112,96},{17,1},{33... | collective-permute-start | bytes 393224 | tf_op jit(solution)/shard_map/ppermute | solution.py:22
  9.5 33.6 %collective-permute-start.1 = (f32[1,32,1024]{2,1,0:T(8,128)S(1)}, f32[1,32,1024]{2,1,0:T(8,128)S(1)}, u32[]{:S(2)}, u32[]{:S(2)}) collective-permute-start(f32[1,32,1024]{2,1,0:T(8,128)S(1)} %get-tuple-element.64), channel_id=1, source_target_pairs={{0,16},{16,32},{32,48},{48,64},{64,80},{80,96},{96,112},{1,17},{17... | collective-permute-start | bytes 393224 | tf_op jit(solution)/shard_map/ppermute | solution.py:19
  13.2 34.1 %collective-permute-start = (f32[1,32,1024]{2,1,0:T(8,128)S(1)}, f32[1,32,1024]{2,1,0:T(8,128)S(1)}, u32[]{:S(2)}, u32[]{:S(2)}) collective-permute-start(f32[1,32,1024]{2,1,0:T(8,128)S(1)} %get-tuple-element.63), channel_id=1, source_target_pairs={{16,0},{32,16},{48,32},{64,48},{80,64},{96,80},{112,96},{17,1},{33... | collective-permute-start | bytes 393224 | tf_op jit(solution)/shard_map/ppermute | solution.py:22
  16.1 34.0 %collective-permute-start.8 = (f32[1,32,1024]{2,1,0:T(8,128)S(1)}, f32[1,32,1024]{2,1,0:T(8,128)S(1)}, u32[]{:S(2)}, u32[]{:S(2)}) collective-permute-start(f32[1,32,1024]{2,1,0:T(8,128)S(1)} %get-tuple-element.62), channel_id=1, source_target_pairs={{0,16},{16,32},{32,48},{48,64},{64,80},{80,96},{96,112},{1,17},{17... | collective-permute-start | bytes 393224 | tf_op jit(solution)/shard_map/ppermute | solution.py:19
  20.1 21.3 %copy-start.7 = (f32[8,32,1024]{2,1,0:T(8,128)S(1)}, f32[8,32,1024]{2,1,0:T(8,128)}, u32[]{:S(2)}) copy-start(f32[8,32,1024]{2,1,0:T(8,128)} %param.9) | copy-start | bytes 3145732
  25.9 149.3 %all-to-all-start = ((s32[128,1,16]{2,1,0:T(1,128)}), s32[128,1,16]{2,1,0:T(1,128)S(1)}, u32[]{:S(2)}, u32[]{:S(2)}) async-start(s32[128,1,16]{2,1,0:T(1,128)} %bitcast.11), calls=%async_computation | async-start | bytes 131072 | tf_op jit(solution)/shard_map/all_to_all | solution.py:173
  37.2 89.1 %copy-start.13 = (f32[8,33]{1,0:T(8,128)}, f32[8,33]{1,0:T(8,128)S(1)}, u32[]{:S(2)}) copy-start(f32[8,33]{1,0:T(8,128)S(1)} %slice.605) | copy-start | bytes 3172
  38.5 13.1 %collective-permute-start.9 = (f32[1,32,1024]{2,1,0:T(8,128)S(1)}, f32[1,32,1024]{2,1,0:T(8,128)S(1)}, u32[]{:S(2)}, u32[]{:S(2)}) collective-permute-start(f32[1,32,1024]{2,1,0:T(8,128)S(1)} %get-tuple-element.61), channel_id=1, source_target_pairs={{16,0},{32,16},{48,32},{64,48},{80,64},{96,80},{112,96},{17,1},{33... | collective-permute-start | bytes 393224 | tf_op jit(solution)/shard_map/ppermute | solution.py:22
  41.7 11.3 %collective-permute-start.5 = (f32[10,1,1024]{2,1,0:T(1,128)S(1)}, f32[10,1,1024]{2,1,0:T(1,128)S(1)}, u32[]{:S(2)}, u32[]{:S(2)}) collective-permute-start(f32[10,1,1024]{2,1,0:T(1,128)S(1)} %get-tuple-element.46), channel_id=1, source_target_pairs={{1,0},{2,1},{3,2},{4,3},{5,4},{6,5},{7,6},{8,7},{9,8},{10,9},{11,1... | collective-permute-start | bytes 122888 | tf_op jit(solution)/shard_map/ppermute | solution.py:22
  43.1 14.4 %collective-permute-start.4 = (f32[10,1,1024]{2,1,0:T(1,128)S(1)}, f32[10,1,1024]{2,1,0:T(1,128)S(1)}, u32[]{:S(2)}, u32[]{:S(2)}) collective-permute-start(f32[10,1,1024]{2,1,0:T(1,128)S(1)} %get-tuple-element.45), channel_id=1, source_target_pairs={{0,1},{1,2},{2,3},{3,4},{4,5},{5,6},{6,7},{7,8},{8,9},{9,10},{10,1... | collective-permute-start | bytes 122888 | tf_op jit(solution)/shard_map/ppermute | solution.py:19
  47.4 13.1 %collective-permute-start.7 = (f32[10,1,1024]{2,1,0:T(1,128)S(1)}, f32[10,1,1024]{2,1,0:T(1,128)S(1)}, u32[]{:S(2)}, u32[]{:S(2)}) collective-permute-start(f32[10,1,1024]{2,1,0:T(1,128)S(1)} %get-tuple-element.44), channel_id=1, source_target_pairs={{0,1},{1,2},{2,3},{3,4},{4,5},{5,6},{6,7},{7,8},{8,9},{9,10},{10,1... | collective-permute-start | bytes 122888 | tf_op jit(solution)/shard_map/ppermute | solution.py:19
  50.1 10.4 %collective-permute-start.6 = (f32[10,1,1024]{2,1,0:T(1,128)S(1)}, f32[10,1,1024]{2,1,0:T(1,128)S(1)}, u32[]{:S(2)}, u32[]{:S(2)}) collective-permute-start(f32[10,1,1024]{2,1,0:T(1,128)S(1)} %get-tuple-element.43), channel_id=1, source_target_pairs={{1,0},{2,1},{3,2},{4,3},{5,4},{6,5},{7,6},{8,7},{9,8},{10,9},{11,1... | collective-permute-start | bytes 122888 | tf_op jit(solution)/shard_map/ppermute | solution.py:22
  51.6 7.3 %collective-permute-start.11 = (f32[10,1,1024]{2,1,0:T(1,128)S(1)}, f32[10,1,1024]{2,1,0:T(1,128)S(1)}, u32[]{:S(2)}, u32[]{:S(2)}) collective-permute-start(f32[10,1,1024]{2,1,0:T(1,128)S(1)} %get-tuple-element.42), channel_id=1, source_target_pairs={{1,0},{2,1},{3,2},{4,3},{5,4},{6,5},{7,6},{8,7},{9,8},{10,9},{11,1... | collective-permute-start | bytes 122888 | tf_op jit(solution)/shard_map/ppermute | solution.py:22
  53.0 6.0 %collective-permute-start.10 = (f32[10,1,1024]{2,1,0:T(1,128)S(1)}, f32[10,1,1024]{2,1,0:T(1,128)S(1)}, u32[]{:S(2)}, u32[]{:S(2)}) collective-permute-start(f32[10,1,1024]{2,1,0:T(1,128)S(1)} %get-tuple-element.41), channel_id=1, source_target_pairs={{0,1},{1,2},{2,3},{3,4},{4,5},{5,6},{6,7},{7,8},{8,9},{9,10},{10,1... | collective-permute-start | bytes 122888 | tf_op jit(solution)/shard_map/ppermute | solution.py:19
  62.3 7.9 %collective-permute-start.12 = (f32[1,32,1024]{2,1,0:T(8,128)S(1)}, f32[1,32,1024]{2,1,0:T(8,128)S(1)}, u32[]{:S(2)}, u32[]{:S(2)}) collective-permute-start(f32[1,32,1024]{2,1,0:T(8,128)S(1)} %get-tuple-element.60), channel_id=1, source_target_pairs={{16,0},{32,16},{48,32},{64,48},{80,64},{96,80},{112,96},{17,1},{33... | collective-permute-start | bytes 393224 | tf_op jit(solution)/shard_map/ppermute | solution.py:22
  65.3 5.9 %collective-permute-start.13 = (f32[1,32,1024]{2,1,0:T(8,128)S(1)}, f32[1,32,1024]{2,1,0:T(8,128)S(1)}, u32[]{:S(2)}, u32[]{:S(2)}) collective-permute-start(f32[1,32,1024]{2,1,0:T(8,128)S(1)} %get-tuple-element.59), channel_id=1, source_target_pairs={{0,16},{16,32},{32,48},{48,64},{64,80},{80,96},{96,112},{1,17},{17... | collective-permute-start | bytes 393224 | tf_op jit(solution)/shard_map/ppermute | solution.py:19
  69.8 43.6 %copy-start.3 = (f32[8,32,1023]{2,1,0:T(8,128)}, f32[8,32,1023]{2,1,0:T(8,128)S(1)}, u32[]{:S(2)}) copy-start(f32[8,32,1023]{2,1,0:T(8,128)S(1)} %get-tuple-element.14) | copy-start | bytes 3142660
  71.2 6.1 %collective-permute-start.15 = (f32[10,1,1024]{2,1,0:T(1,128)S(1)}, f32[10,1,1024]{2,1,0:T(1,128)S(1)}, u32[]{:S(2)}, u32[]{:S(2)}) collective-permute-start(f32[10,1,1024]{2,1,0:T(1,128)S(1)} %get-tuple-element.40), channel_id=1, source_target_pairs={{0,1},{1,2},{2,3},{3,4},{4,5},{5,6},{6,7},{7,8},{8,9},{9,10},{10,1... | collective-permute-start | bytes 122888 | tf_op jit(solution)/shard_map/ppermute | solution.py:19
  75.6 5.3 %collective-permute-start.14 = (f32[10,1,1024]{2,1,0:T(1,128)S(1)}, f32[10,1,1024]{2,1,0:T(1,128)S(1)}, u32[]{:S(2)}, u32[]{:S(2)}) collective-permute-start(f32[10,1,1024]{2,1,0:T(1,128)S(1)} %get-tuple-element.39), channel_id=1, source_target_pairs={{1,0},{2,1},{3,2},{4,3},{5,4},{6,5},{7,6},{8,7},{9,8},{10,9},{11,1... | collective-permute-start | bytes 122888 | tf_op jit(solution)/shard_map/ppermute | solution.py:22
  77.3 45.2 %copy-start.1 = (f32[9,32,1024]{2,1,0:T(8,128)}, f32[9,32,1024]{2,1,0:T(8,128)S(1)}, u32[]{:S(2)}) copy-start(f32[9,32,1024]{2,1,0:T(8,128)S(1)} %get-tuple-element.16) | copy-start | bytes 3538948
  82.2 8.1 %collective-permute-start.16 = (f32[1,32,1024]{2,1,0:T(8,128)S(1)}, f32[1,32,1024]{2,1,0:T(8,128)S(1)}, u32[]{:S(2)}, u32[]{:S(2)}) collective-permute-start(f32[1,32,1024]{2,1,0:T(8,128)S(1)} %get-tuple-element.58), channel_id=1, source_target_pairs={{16,0},{32,16},{48,32},{64,48},{80,64},{96,80},{112,96},{17,1},{33... | collective-permute-start | bytes 393224 | tf_op jit(solution)/shard_map/ppermute | solution.py:22
  84.2 7.4 %collective-permute-start.17 = (f32[1,32,1024]{2,1,0:T(8,128)S(1)}, f32[1,32,1024]{2,1,0:T(8,128)S(1)}, u32[]{:S(2)}, u32[]{:S(2)}) collective-permute-start(f32[1,32,1024]{2,1,0:T(8,128)S(1)} %get-tuple-element.57), channel_id=1, source_target_pairs={{0,16},{16,32},{32,48},{48,64},{64,80},{80,96},{96,112},{1,17},{17... | collective-permute-start | bytes 393224 | tf_op jit(solution)/shard_map/ppermute | solution.py:19
  91.7 7.2 %collective-permute-start.19 = (f32[10,1,1024]{2,1,0:T(1,128)S(1)}, f32[10,1,1024]{2,1,0:T(1,128)S(1)}, u32[]{:S(2)}, u32[]{:S(2)}) collective-permute-start(f32[10,1,1024]{2,1,0:T(1,128)S(1)} %get-tuple-element.38), channel_id=1, source_target_pairs={{0,1},{1,2},{2,3},{3,4},{4,5},{5,6},{6,7},{7,8},{8,9},{9,10},{10,1... | collective-permute-start | bytes 122888 | tf_op jit(solution)/shard_map/ppermute | solution.py:19
  97.1 7.5 %collective-permute-start.18 = (f32[10,1,1024]{2,1,0:T(1,128)S(1)}, f32[10,1,1024]{2,1,0:T(1,128)S(1)}, u32[]{:S(2)}, u32[]{:S(2)}) collective-permute-start(f32[10,1,1024]{2,1,0:T(1,128)S(1)} %get-tuple-element.37), channel_id=1, source_target_pairs={{1,0},{2,1},{3,2},{4,3},{5,4},{6,5},{7,6},{8,7},{9,8},{10,9},{11,1... | collective-permute-start | bytes 122888 | tf_op jit(solution)/shard_map/ppermute | solution.py:22
  106.0 8.1 %collective-permute-start.20 = (f32[1,32,1024]{2,1,0:T(8,128)S(1)}, f32[1,32,1024]{2,1,0:T(8,128)S(1)}, u32[]{:S(2)}, u32[]{:S(2)}) collective-permute-start(f32[1,32,1024]{2,1,0:T(8,128)S(1)} %get-tuple-element.56), channel_id=1, source_target_pairs={{16,0},{32,16},{48,32},{64,48},{80,64},{96,80},{112,96},{17,1},{33... | collective-permute-start | bytes 393224 | tf_op jit(solution)/shard_map/ppermute | solution.py:22
  107.9 7.4 %collective-permute-start.21 = (f32[1,32,1024]{2,1,0:T(8,128)S(1)}, f32[1,32,1024]{2,1,0:T(8,128)S(1)}, u32[]{:S(2)}, u32[]{:S(2)}) collective-permute-start(f32[1,32,1024]{2,1,0:T(8,128)S(1)} %get-tuple-element.55), channel_id=1, source_target_pairs={{0,16},{16,32},{32,48},{48,64},{64,80},{80,96},{96,112},{1,17},{17... | collective-permute-start | bytes 393224 | tf_op jit(solution)/shard_map/ppermute | solution.py:19
  115.4 7.3 %collective-permute-start.23 = (f32[10,1,1024]{2,1,0:T(1,128)S(1)}, f32[10,1,1024]{2,1,0:T(1,128)S(1)}, u32[]{:S(2)}, u32[]{:S(2)}) collective-permute-start(f32[10,1,1024]{2,1,0:T(1,128)S(1)} %get-tuple-element.36), channel_id=1, source_target_pairs={{0,1},{1,2},{2,3},{3,4},{4,5},{5,6},{6,7},{7,8},{8,9},{9,10},{10,1... | collective-permute-start | bytes 122888 | tf_op jit(solution)/shard_map/ppermute | solution.py:19
  121.2 5.0 %collective-permute-start.22 = (f32[10,1,1024]{2,1,0:T(1,128)S(1)}, f32[10,1,1024]{2,1,0:T(1,128)S(1)}, u32[]{:S(2)}, u32[]{:S(2)}) collective-permute-start(f32[10,1,1024]{2,1,0:T(1,128)S(1)} %get-tuple-element.35), channel_id=1, source_target_pairs={{1,0},{2,1},{3,2},{4,3},{5,4},{6,5},{7,6},{8,7},{9,8},{10,9},{11,1... | collective-permute-start | bytes 122888 | tf_op jit(solution)/shard_map/ppermute | solution.py:22
  175.2 23.1 %all-to-all-start.1 = ((f32[128,1,16]{2,1,0:T(1,128)}), f32[128,1,16]{2,1,0:T(1,128)S(1)}, u32[]{:S(2)}, u32[]{:S(2)}) async-start(f32[128,1,16]{2,1,0:T(1,128)} %bitcast.13), calls=%async_computation.1 | async-start | bytes 131072 | tf_op jit(solution)/shard_map/all_to_all | solution.py:172
  200.9 14.0 %all-to-all-start.2 = ((f32[128,1,16]{2,1,0:T(1,128)}), f32[128,1,16]{2,1,0:T(1,128)S(1)}, u32[]{:S(2)}, u32[]{:S(2)}) async-start(f32[128,1,16]{2,1,0:T(1,128)} %bitcast.16), calls=%async_computation.2 | async-start | bytes 131072 | tf_op jit(solution)/shard_map/all_to_all | solution.py:181
  247.0 6.4 %collective-permute-start.24 = (f32[1,32,1024]{2,1,0:T(8,128)S(1)}, f32[1,32,1024]{2,1,0:T(8,128)S(1)}, u32[]{:S(2)}, u32[]{:S(2)}) collective-permute-start(f32[1,32,1024]{2,1,0:T(8,128)S(1)} %get-tuple-element.54), channel_id=1, source_target_pairs={{16,0},{32,16},{48,32},{64,48},{80,64},{96,80},{112,96},{17,1},{33... | collective-permute-start | bytes 393224 | tf_op jit(solution)/shard_map/ppermute | solution.py:22
  250.0 4.6 %collective-permute-start.25 = (f32[1,32,1024]{2,1,0:T(8,128)S(1)}, f32[1,32,1024]{2,1,0:T(8,128)S(1)}, u32[]{:S(2)}, u32[]{:S(2)}) collective-permute-start(f32[1,32,1024]{2,1,0:T(8,128)S(1)} %get-tuple-element.53), channel_id=1, source_target_pairs={{0,16},{16,32},{32,48},{48,64},{64,80},{80,96},{96,112},{1,17},{17... | collective-permute-start | bytes 393224 | tf_op jit(solution)/shard_map/ppermute | solution.py:19
  254.7 4.0 %collective-permute-start.27 = (f32[10,1,1024]{2,1,0:T(1,128)S(1)}, f32[10,1,1024]{2,1,0:T(1,128)S(1)}, u32[]{:S(2)}, u32[]{:S(2)}) collective-permute-start(f32[10,1,1024]{2,1,0:T(1,128)S(1)} %get-tuple-element.34), channel_id=1, source_target_pairs={{0,1},{1,2},{2,3},{3,4},{4,5},{5,6},{6,7},{7,8},{8,9},{9,10},{10,1... | collective-permute-start | bytes 122888 | tf_op jit(solution)/shard_map/ppermute | solution.py:19
  256.9 4.7 %collective-permute-start.26 = (f32[10,1,1024]{2,1,0:T(1,128)S(1)}, f32[10,1,1024]{2,1,0:T(1,128)S(1)}, u32[]{:S(2)}, u32[]{:S(2)}) collective-permute-start(f32[10,1,1024]{2,1,0:T(1,128)S(1)} %get-tuple-element.33), channel_id=1, source_target_pairs={{1,0},{2,1},{3,2},{4,3},{5,4},{6,5},{7,6},{8,7},{9,8},{10,9},{11,1... | collective-permute-start | bytes 122888 | tf_op jit(solution)/shard_map/ppermute | solution.py:22
  262.9 8.4 %collective-permute-start.28 = (f32[1,32,1024]{2,1,0:T(8,128)S(1)}, f32[1,32,1024]{2,1,0:T(8,128)S(1)}, u32[]{:S(2)}, u32[]{:S(2)}) collective-permute-start(f32[1,32,1024]{2,1,0:T(8,128)S(1)} %get-tuple-element.52), channel_id=1, source_target_pairs={{16,0},{32,16},{48,32},{64,48},{80,64},{96,80},{112,96},{17,1},{33... | collective-permute-start | bytes 393224 | tf_op jit(solution)/shard_map/ppermute | solution.py:22
  265.0 7.5 %collective-permute-start.29 = (f32[1,32,1024]{2,1,0:T(8,128)S(1)}, f32[1,32,1024]{2,1,0:T(8,128)S(1)}, u32[]{:S(2)}, u32[]{:S(2)}) collective-permute-start(f32[1,32,1024]{2,1,0:T(8,128)S(1)} %get-tuple-element.51), channel_id=1, source_target_pairs={{0,16},{16,32},{32,48},{48,64},{64,80},{80,96},{96,112},{1,17},{17... | collective-permute-start | bytes 393224 | tf_op jit(solution)/shard_map/ppermute | solution.py:19
  272.6 3.9 %collective-permute-start.31 = (f32[10,1,1024]{2,1,0:T(1,128)S(1)}, f32[10,1,1024]{2,1,0:T(1,128)S(1)}, u32[]{:S(2)}, u32[]{:S(2)}) collective-permute-start(f32[10,1,1024]{2,1,0:T(1,128)S(1)} %get-tuple-element.32), channel_id=1, source_target_pairs={{0,1},{1,2},{2,3},{3,4},{4,5},{5,6},{6,7},{7,8},{8,9},{9,10},{10,1... | collective-permute-start | bytes 122888 | tf_op jit(solution)/shard_map/ppermute | solution.py:19
  274.8 4.7 %collective-permute-start.30 = (f32[10,1,1024]{2,1,0:T(1,128)S(1)}, f32[10,1,1024]{2,1,0:T(1,128)S(1)}, u32[]{:S(2)}, u32[]{:S(2)}) collective-permute-start(f32[10,1,1024]{2,1,0:T(1,128)S(1)} %get-tuple-element.31), channel_id=1, source_target_pairs={{1,0},{2,1},{3,2},{4,3},{5,4},{6,5},{7,6},{8,7},{9,8},{10,9},{11,1... | collective-permute-start | bytes 122888 | tf_op jit(solution)/shard_map/ppermute | solution.py:22
  281.0 8.4 %collective-permute-start.32 = (f32[1,32,1024]{2,1,0:T(8,128)S(1)}, f32[1,32,1024]{2,1,0:T(8,128)S(1)}, u32[]{:S(2)}, u32[]{:S(2)}) collective-permute-start(f32[1,32,1024]{2,1,0:T(8,128)S(1)} %get-tuple-element.50), channel_id=1, source_target_pairs={{16,0},{32,16},{48,32},{64,48},{80,64},{96,80},{112,96},{17,1},{33... | collective-permute-start | bytes 393224 | tf_op jit(solution)/shard_map/ppermute | solution.py:22
  282.9 7.7 %collective-permute-start.33 = (f32[1,32,1024]{2,1,0:T(8,128)S(1)}, f32[1,32,1024]{2,1,0:T(8,128)S(1)}, u32[]{:S(2)}, u32[]{:S(2)}) collective-permute-start(f32[1,32,1024]{2,1,0:T(8,128)S(1)} %get-tuple-element.49), channel_id=1, source_target_pairs={{0,16},{16,32},{32,48},{48,64},{64,80},{80,96},{96,112},{1,17},{17... | collective-permute-start | bytes 393224 | tf_op jit(solution)/shard_map/ppermute | solution.py:19
  290.7 6.8 %collective-permute-start.35 = (f32[10,1,1024]{2,1,0:T(1,128)S(1)}, f32[10,1,1024]{2,1,0:T(1,128)S(1)}, u32[]{:S(2)}, u32[]{:S(2)}) collective-permute-start(f32[10,1,1024]{2,1,0:T(1,128)S(1)} %get-tuple-element.30), channel_id=1, source_target_pairs={{0,1},{1,2},{2,3},{3,4},{4,5},{5,6},{6,7},{7,8},{8,9},{9,10},{10,1... | collective-permute-start | bytes 122888 | tf_op jit(solution)/shard_map/ppermute | solution.py:19
  295.9 5.0 %collective-permute-start.34 = (f32[10,1,1024]{2,1,0:T(1,128)S(1)}, f32[10,1,1024]{2,1,0:T(1,128)S(1)}, u32[]{:S(2)}, u32[]{:S(2)}) collective-permute-start(f32[10,1,1024]{2,1,0:T(1,128)S(1)} %get-tuple-element.29), channel_id=1, source_target_pairs={{1,0},{2,1},{3,2},{4,3},{5,4},{6,5},{7,6},{8,7},{9,8},{10,9},{11,1... | collective-permute-start | bytes 122888 | tf_op jit(solution)/shard_map/ppermute | solution.py:22
  302.4 8.1 %collective-permute-start.36 = (f32[1,32,1024]{2,1,0:T(8,128)S(1)}, f32[1,32,1024]{2,1,0:T(8,128)S(1)}, u32[]{:S(2)}, u32[]{:S(2)}) collective-permute-start(f32[1,32,1024]{2,1,0:T(8,128)S(1)} %get-tuple-element.48), channel_id=1, source_target_pairs={{16,0},{32,16},{48,32},{64,48},{80,64},{96,80},{112,96},{17,1},{33... | collective-permute-start | bytes 393224 | tf_op jit(solution)/shard_map/ppermute | solution.py:22
  304.3 7.4 %collective-permute-start.37 = (f32[1,32,1024]{2,1,0:T(8,128)S(1)}, f32[1,32,1024]{2,1,0:T(8,128)S(1)}, u32[]{:S(2)}, u32[]{:S(2)}) collective-permute-start(f32[1,32,1024]{2,1,0:T(8,128)S(1)} %get-tuple-element.47), channel_id=1, source_target_pairs={{0,16},{16,32},{32,48},{48,64},{64,80},{80,96},{96,112},{1,17},{17... | collective-permute-start | bytes 393224 | tf_op jit(solution)/shard_map/ppermute | solution.py:19
  311.8 5.5 %collective-permute-start.39 = (f32[10,1,1024]{2,1,0:T(1,128)S(1)}, f32[10,1,1024]{2,1,0:T(1,128)S(1)}, u32[]{:S(2)}, u32[]{:S(2)}) collective-permute-start(f32[10,1,1024]{2,1,0:T(1,128)S(1)} %get-tuple-element.28), channel_id=1, source_target_pairs={{0,1},{1,2},{2,3},{3,4},{4,5},{5,6},{6,7},{7,8},{8,9},{9,10},{10,1... | collective-permute-start | bytes 122888 | tf_op jit(solution)/shard_map/ppermute | solution.py:19
  315.6 5.2 %collective-permute-start.38 = (f32[10,1,1024]{2,1,0:T(1,128)S(1)}, f32[10,1,1024]{2,1,0:T(1,128)S(1)}, u32[]{:S(2)}, u32[]{:S(2)}) collective-permute-start(f32[10,1,1024]{2,1,0:T(1,128)S(1)} %get-tuple-element.27), channel_id=1, source_target_pairs={{1,0},{2,1},{3,2},{4,3},{5,4},{6,5},{7,6},{8,7},{9,8},{10,9},{11,1... | collective-permute-start | bytes 122888 | tf_op jit(solution)/shard_map/ppermute | solution.py:22
  (18 other events, 137.9 us)
where the time goes:
time: 327 us; the launch traced here: 323 us
  starting transfers between devices  151 us (46%)
  local copies, waits for them, and re-layouts  69.1 us (21%)
  waiting for transfers between devices  51.6 us (16%)
  other arithmetic  49.8 us (15%)
    ppermute x20, starting transfers between devices, padded_2(): lax.ppermute(lax.slice_in_dim(block, block.shape[dim] - width, None, axis...  87 us
    gather x2, local copies, waits for them, and re-layouts, body(): values = jnp.sum(probe_weights * flat[probe_nodes], axis=0)  41.4 us
    ppermute x20, starting transfers between devices, padded_2(): lax.ppermute(lax.slice_in_dim(block, 0, width, axis=dim), axis, backward)  36.1 us
    ppermute x20, waiting for transfers between devices, padded_2(): lax.ppermute(lax.slice_in_dim(block, 0, width, axis=dim), axis, backward)  27.2 us
    scatter-add x1, other arithmetic, body(): source = jnp.zeros(flat.shape, jnp.float32).at[probe_nodes.reshape(-1)].a...  22.9 us
    all_to_all x1, starting transfers between devices, body(): lax.all_to_all(send_values, ('px', 'py'), split_axis=0, concat_axis=0, ti...  13.6 us
    all_to_all x1, starting transfers between devices, body(): lax.all_to_all(send_sensor, ('px', 'py'), split_axis=0, concat_axis=0, ti...  9.65 us
    all_to_all x1, waiting for transfers between devices, body(): lax.all_to_all(send_values, ('px', 'py'), split_axis=0, concat_axis=0, ti...  8.77 us
  transfers between devices with their start and end apart: 43, of which 22 were waited for; matrix products, arithmetic and copies ran while one was open for 23% of the time, Pallas kernels for 0%

commit v1 on v0

v1 whole, which is shorter than its diff:
```python
import jax
import jax.numpy as jnp
import numpy as np
from jax import lax
from jax.experimental import pallas as pl
from jax.experimental.pallas import tpu as pltpu
from jax.sharding import PartitionSpec as P

SWEEPS = 4
MASS = 1.0
LOW = 1.0
HIGH = 25.0
CENTRE = 0.5 * (HIGH + LOW)
HALF = 0.5 * (HIGH - LOW)

CX, CY, CZ = 8, 32, 1024
D = 4
EX, EY = CX + 2 * D, CY + 2 * D
ROWS = CX * CY * 8
HALO_X = D * CY * 8
HALO_Y = CX * D * 8
DC = 3
HALO_C = DC * D * 8
META = 128
F32 = jnp.float32
BF16 = jnp.bfloat16


def horner_terms():
    spread = CENTRE / HALF
    size = SWEEPS
    iterate = np.zeros(size)
    remain = np.eye(size)[0]
    search = remain / CENTRE
    ratio = 1.0 / spread
    for sweep in range(SWEEPS):
        iterate = iterate + search
        if sweep < SWEEPS - 1:
            shifted = np.concatenate([[0.0], search[:-1]])
            remain = remain - (CENTRE * search + HALF * shifted)
            following = 1.0 / (2.0 * spread - ratio)
            search = following * ratio * search + 2.0 * following / HALF * remain
            ratio = following
    return [float(v) for v in iterate]


A0, A1, A2, A3 = horner_terms()


def lane_of(n):
    return lax.broadcasted_iota(jnp.int32, (n, 8, 128), 2)


def z_up(f):
    r = pltpu.roll(f, 127, 2)
    return jnp.where(lane_of(f.shape[0]) == 127, pltpu.roll(r, 7, 1), r)


def z_down(f):
    r = pltpu.roll(f, 1, 2)
    return jnp.where(lane_of(f.shape[0]) == 0, pltpu.roll(r, 1, 1), r)


def z_face(q):
    n = q.shape[0]
    sub = lax.broadcasted_iota(jnp.int32, (n, 8, 128), 1)
    last = (sub == 7) & (lane_of(n) == 127)
    return jnp.where(last, 0.0, q + z_up(q))


def fluxes(src, q, cz, x, y, n):
    fe, qe = src[x, pl.ds(y - 1, n + 2)], q[x, pl.ds(y - 1, n + 2)]
    f, qc = fe[1:-1], qe[1:-1]
    fy = (fe[1:] - fe[:-1]) * (qe[1:] + qe[:-1])
    acc = fy[1:] - fy[:-1]
    acc += (src[x + 1, pl.ds(y, n)] - f) * (q[x + 1, pl.ds(y, n)] + qc)
    acc += (src[x - 1, pl.ds(y, n)] - f) * (q[x - 1, pl.ds(y, n)] + qc)
    fz = (z_up(f) - f) * (z_face(qc) if cz is None else cz[x, pl.ds(y, n)])
    return f, acc + (fz - z_down(fz))


def cover(low, high, n):
    starts = list(range(low, high - n + 1, n))
    if starts[-1] + n < high:
        starts.append(high - n)
    return starts


def sweep(margin, n, step):
    def plane(x, carry):
        for y in cover(margin, EY - margin, n):
            step(x, y, n)
        return carry

    lax.fori_loop(margin, EX - margin, plane, 0)


def own_rows(ref, out, scale):
    def plane(x, carry):
        for yt in range(CY // 8):
            for ys in range(8):
                v = ref[pl.ds((x * (CY // 8) + yt) * 64 + ys, 8, stride=8), :]
                out[x + D, D + yt * 8 + ys] = v * scale if scale != 1.0 else v
        return carry

    lax.fori_loop(0, CX, plane, 0)


def extend(field, own, px_low, px_high, py_low, py_high, c_low, c_high, out, scale):
    own_rows(own, out, scale)
    for ref, at in ((px_low, 0), (px_high, D + CX)):

        def plane(x, carry, ref=ref, at=at):
            for yt in range(CY // 8):
                for ys in range(8):
                    v = ref[
                        pl.ds(field * HALO_X + (x * (CY // 8) + yt) * 64 + ys, 8, stride=8), :
                    ]
                    out[x + at, D + yt * 8 + ys] = v * scale
            return carry

        lax.fori_loop(0, D, plane, 0)
    for ref, at in ((py_low, 0), (py_high, D + CY)):
        for x in range(CX):
            v = ref[pl.ds(field * HALO_Y + x * D * 8, D * 8), :]
            out[x + D, pl.ds(at, D)] = v.reshape(D, 8, 128) * scale
    part = 3 * HALO_C + META
    for ref, at, gap in ((c_low, 1, 0), (c_high, D + CX, D + CX + DC)):
        for side, to in ((0, 0), (1, D + CY)):
            out[gap, pl.ds(to, D)] = jnp.zeros((D, 8, 128), F32)
            for x in range(DC):
                v = ref[pl.ds(side * part + field * HALO_C + x * D * 8, D * 8), :]
                out[at + x, pl.ds(to, D)] = v.reshape(D, 8, 128) * scale


def close_edges(pos, out, sign):
    @pl.when(pos[0] == 0)
    def _():
        out[D - 1] = out[D] * sign

    @pl.when(pos[0] == pos[2])
    def _():
        out[D + CX] = out[D + CX - 1] * sign

    @pl.when(pos[1] == 0)
    def _():
        out[:, D - 1] = out[:, D] * sign

    @pl.when(pos[1] == pos[3])
    def _():
        out[:, D + CY] = out[:, D + CY - 1] * sign


def take_meta(ref, base, out):
    for half in range(2):
        for c in range(8):
            out[half * 8 : half * 8 + 8, c * 128 : (c + 1) * 128] = ref[
                pl.ds(base + half * 64 + c * 8, 8), :
            ]


def two_parts(v):
    high = v.astype(BF16)
    return high, (v - high.astype(F32)).astype(BF16)


def three_parts(v):
    high = v.astype(BF16)
    rest = v - high.astype(F32)
    mid = rest.astype(BF16)
    return high, mid, (rest - mid.astype(F32)).astype(BF16)


def one_hot(index, count):
    at = lax.broadcasted_iota(jnp.int32, (count, index.shape[1]), 0)
    return jnp.where(at == index, 1.0, 0.0).astype(BF16)


def dot(a, b, over):
    return lax.dot_general(a, b, (over, ((), ())), preferred_element_type=F32)


def tangent_kernel(
    pos,
    permit,
    back,
    perturb,
    px_low,
    px_high,
    py_low,
    py_high,
    c_low,
    c_high,
    meta,
    weights,
    out,
    q,
    qp,
    bg,
    cz,
    b,
    y1,
    y2,
    table,
    vals,
):
    sides = (px_low, px_high, py_low, py_high, c_low, c_high)
    extend(0, permit, *sides, q, 0.5 / HALF)
    extend(1, back, *sides, bg, 1.0)
    extend(2, perturb, *sides, qp, 0.5)
    close_edges(pos, q, -1.0)
    close_edges(pos, qp, -1.0)

    def first(x, y, n):
        _, acc = fluxes(bg, qp, None, x, y, n)
        b[x, pl.ds(y, n)] = acc
        cz[x, pl.ds(y, n)] = z_face(q[x, pl.ds(y, n)])

    def second(x, y, n):
        f, acc = fluxes(b, q, cz, x, y, n)
        y1[x, pl.ds(y, n)] = (A2 - A3) * f - A3 * acc

    def third(x, y, n):
        f, acc = fluxes(y1, q, cz, x, y, n)
        y2[x, pl.ds(y, n)] = A1 * b[x, pl.ds(y, n)] - f - acc

    def fourth(x, y, n):
        f, acc = fluxes(y2, q, cz, x, y, n)
        y1[x, pl.ds(y, n)] = A0 * b[x, pl.ds(y, n)] - f - acc

    sweep(1, 4, first)
    sweep(2, 4, second)
    sweep(3, 4, third)
    sweep(4, 4, fourth)

    flat = y1.reshape(EX * EY * 8, 128)
    for x in range(CX):
        for c in range(8):
            v = flat[pl.ds(((x + D) * EY + D) * 8 + c, CY, stride=8), :]
            high, low = two_parts(v)
            table[x * CY : (x + 1) * CY, c * 128 : (c + 1) * 128] = high
            table[CX * CY + x * CY : CX * CY + (x + 1) * CY, c * 128 : (c + 1) * 128] = low

    vals[...] = jnp.zeros_like(vals)
    wide = 512

    def gather(i, carry):
        k, lanes = i // 2, pl.ds(pl.multiple_of((i % 2) * wide, wide), wide)
        node = meta[pl.ds(k, 1), lanes].astype(jnp.int32)
        found = dot(table[...], one_hot(node & (CZ - 1), CZ), ((1,), (0,)))
        found = found[: CX * CY] + found[CX * CY :]
        at = lax.broadcasted_iota(jnp.int32, found.shape, 0)
        found = jnp.sum(jnp.where(at == node >> 10, found, 0.0), axis=0, keepdims=True)
        vals[0:1, lanes] += meta[pl.ds(k + 4, 1), lanes] * found
        return carry

    lax.fori_loop(0, 8, gather, 0)

    key = meta[8:9, :].astype(jnp.int32)
    at = lax.broadcasted_iota(jnp.int32, (8, 1024), 0)
    owned = jnp.where(at == key >> 7, vals[0:1, :], 0.0)
    parts = jnp.concatenate(three_parts(owned), axis=0)
    sums = dot(parts, one_hot(key & 127, 128), ((1,), (1,)))
    readings = sums[0:8] + sums[8:16] + sums[16:24]
    both = jnp.concatenate([readings, weights[...]], axis=0)
    out[...] = jnp.broadcast_to(both[None], out.shape)


def scatter(meta, values, rows, cols, per, tiles, lhs, keep):
    for k in range(4):
        node = meta[k : k + 1, :].astype(jnp.int32)
        high, low = two_parts(values[k : k + 1, :])
        hit = lax.broadcasted_iota(jnp.int32, (per, 1024), 0) == rows(node)
        lanes = slice(k * 1024, (k + 1) * 1024)
        lhs[0:per, lanes] = jnp.where(hit, high.astype(F32), 0.0).astype(BF16)
        lhs[per : 2 * per, lanes] = jnp.where(hit, low.astype(F32), 0.0).astype(BF16)

    def tile(t, carry):
        total = None
        for k in range(4):
            node = meta[k : k + 1, :].astype(jnp.int32)
            lanes = slice(k * 1024, (k + 1) * 1024)
            part = dot(lhs[0 : 2 * per, lanes], one_hot(cols(node) - t * 256, 256), ((1,), (1,)))
            total = part if total is None else total + part
        keep(t, total[0:per] + total[per : 2 * per])
        return carry

    if tiles == 1:
        tile(0, 0)
    else:
        lax.fori_loop(0, tiles, tile, 0)


def adjoint_kernel(
    pos,
    got,
    permit,
    back,
    px_low,
    px_high,
    py_low,
    py_high,
    c_low,
    c_high,
    meta,
    out,
    q,
    bg,
    cz,
    src,
    y1,
    y2,
    lhs,
    near,
    values,
):
    sides = (px_low, px_high, py_low, py_high, c_low, c_high)
    extend(0, permit, *sides, q, 0.5 / HALF)
    extend(1, back, *sides, bg, 1.0)
    close_edges(pos, q, -1.0)
    close_edges(pos, bg, 1.0)

    both = jnp.sum(got[...], axis=0)
    weighted = jnp.concatenate(three_parts(both[0:8] * both[8:16]), axis=0)

    def returned(table):
        key = table[8:9, :].astype(jnp.int32)
        found = dot(weighted, one_hot(key & 127, 128), ((1,), (0,)))
        found = found[0:8] + found[8:16] + found[16:24]
        at = lax.broadcasted_iota(jnp.int32, found.shape, 0)
        found = jnp.sum(jnp.where(at == key >> 7, found, 0.0), axis=0, keepdims=True)
        values[0:4, :] = table[4:8, :] * found

    flat = src.reshape(EX * EY * 8, 128)

    def xy(node):
        return node >> 15, (node >> 10) & (CY - 1)

    def put_planes(x0, planes):
        def keep(t, sums):
            for x in range(planes):
                for half in range(2):
                    flat[pl.ds(((x + x0) * EY + D) * 8 + t * 2 + half, CY, stride=8), :] = sums[
                        x * CY : (x + 1) * CY, half * 128 : (half + 1) * 128
                    ]

        return keep

    def put_strip(x0, planes, y0):
        def keep(t, sums):
            for zq in range(4):
                for x in range(0, planes):
                    block = sums[zq * planes * D + x * D : zq * planes * D + (x + 1) * D]
                    for half in range(2):
                        flat[
                            pl.ds(((x + x0) * EY + y0) * 8 + zq * 2 + half, D, stride=8), :
                        ] = block[:, half * 128 : (half + 1) * 128]

        return keep

    def column(node):
        return node & (CZ - 1)

    def low_column(node):
        return node & 255

    returned(meta)
    scatter(meta, values, lambda n: n >> 10, column, CX * CY, 4, lhs, put_planes(D, CX))

    for ref, x0, first in ((px_low, 0, CX - D), (px_high, D + CX, 0)):
        take_meta(ref, 3 * HALO_X, near)
        returned(near)
        scatter(
            near,
            values,
            lambda n, first=first: (n >> 10) - first * CY,
            column,
            D * CY,
            4,
            lhs,
            put_planes(x0, D),
        )

    def strip(first_x, planes, first_y):
        def rows(node):
            x, y = xy(node)
            x, y = x - first_x, y - first_y
            good = (x >= 0) & (x < planes) & (y >= 0) & (y < D)
            return jnp.where(good, ((node >> 8) & 3) * (planes * D) + x * D + y, -1)

        return rows

    for ref, y0, first in ((py_low, 0, CY - D), (py_high, D + CY, 0)):
        take_meta(ref, 3 * HALO_Y, near)
        returned(near)
        scatter(
            near, values, strip(0, CX, first), low_column, 4 * CX * D, 1, lhs, put_strip(D, CX, y0)
        )

    part = 3 * HALO_C + META
    for ref, x0, first_x in ((c_low, 0, CX - D), (c_high, D + CX, 0)):
        for side, y0, first_y in ((0, 0, CY - D), (1, D + CY, 0)):
            take_meta(ref, side * part + 3 * HALO_C, near)
            returned(near)
            scatter(
                near,
                values,
                strip(first_x, D, first_y),
                low_column,
                4 * D * D,
                1,
                lhs,
                put_strip(x0, D, y0),
            )

    def first(x, y, n):
        cz[x, pl.ds(y, n)] = z_face(q[x, pl.ds(y, n)])
        f, acc = fluxes(src, q, cz, x, y, n)
        y1[x, pl.ds(y, n)] = (A2 - A3) * f - A3 * acc

    def second(x, y, n):
        f, acc = fluxes(y1, q, cz, x, y, n)
        y2[x, pl.ds(y, n)] = A1 * src[x, pl.ds(y, n)] - f - acc

    def third(x, y, n):
        f, acc = fluxes(y2, q, cz, x, y, n)
        y1[x, pl.ds(y, n)] = A0 * src[x, pl.ds(y, n)] - f - acc

    sweep(1, 4, first)
    sweep(2, 4, second)
    sweep(3, 4, third)

    def last(x, y, n):
        ae, be = y1[x, pl.ds(y - 1, n + 2)], bg[x, pl.ds(y - 1, n + 2)]
        a, k = ae[1:-1], be[1:-1]
        sy = (ae[1:] - ae[:-1]) * (be[1:] - be[:-1])
        total = sy[1:] + sy[:-1]
        total += (y1[x + 1, pl.ds(y, n)] - a) * (bg[x + 1, pl.ds(y, n)] - k)
        total += (y1[x - 1, pl.ds(y, n)] - a) * (bg[x - 1, pl.ds(y, n)] - k)
        sub = lax.broadcasted_iota(jnp.int32, (n, 8, 128), 1)
        end = (sub == 7) & (lane_of(n) == 127)
        sz = jnp.where(end, 0.0, (z_up(a) - a) * (z_up(k) - k))
        total = -0.5 * (total + (sz + z_down(sz)))
        yy = y - D
        for i in range(n):
            row = (x - D) * (CY // 8) + (yy + i) // 8
            out[pl.ds(row * 64 + (yy + i) % 8, 8, stride=8), :] = total[i]

    sweep(4, 4, last)


def by_tiles(block):
    lead = block.shape[:-2]
    rows, cols = block.shape[-2:]
    split = block.reshape(*lead, rows // 8, 8, cols // 128, 128)
    return jnp.swapaxes(split, -3, -2).reshape(-1, 128)


def from_tiles(rows):
    split = rows.reshape(CX, CY // 8, CZ // 128, 8, 128)
    return jnp.swapaxes(split, -3, -2).reshape(CX, CY, CZ)


def pack_kernel(permit, back, perturb, meta, low, high):
    for field, ref in enumerate((permit, back, perturb)):
        for x in range(CX):
            for y in range(D):
                at = pl.ds(field * HALO_Y + (x * D + y) * 8, 8)
                low[at, :] = ref[pl.ds(x * (CY // 8) * 64 + y, 8, stride=8), :]
                last = x * (CY // 8) + CY // 8 - 1
                high[at, :] = ref[pl.ds(last * 64 + 8 - D + y, 8, stride=8), :]
    low[3 * HALO_Y :, :] = meta[...]
    high[3 * HALO_Y :, :] = meta[...]


def vmem(count):
    return [pl.BlockSpec(memory_space=pltpu.VMEM)] * count


def shift(x, axis, by):
    count = lax.axis_size(axis)
    return lax.ppermute(x, axis, [(i, (i + by) % count) for i in range(count)])


def body(
    background_field,
    perturbation,
    permittivity,
    probe_nodes,
    probe_weights,
    probe_owner,
    probe_sensor,
    sensor_weight,
):
    count_x, count_y = lax.axis_size("px"), lax.axis_size("py")
    px, py = lax.axis_index("px"), lax.axis_index("py")
    owned = sensor_weight.shape[0]
    devices = count_x * count_y
    pos = jnp.stack([px, py, jnp.int32(count_x - 1), jnp.int32(count_y - 1)]).astype(jnp.int32)
    key = probe_owner.reshape(1, -1) * owned + probe_sensor[None, :]
    meta = jnp.concatenate(
        [
            probe_nodes.astype(F32),
            probe_weights,
            key.astype(F32),
            jnp.zeros((7, key.shape[1]), F32),
        ],
        axis=0,
    )
    weights = lax.dynamic_update_slice(
        jnp.zeros((8, 128), F32), sensor_weight[None, :], (px, py * owned)
    )
    fields = [by_tiles(f) for f in (permittivity, background_field, perturbation)]
    meta_rows = by_tiles(meta)

    low_x = jnp.concatenate([f[:HALO_X] for f in fields] + [meta_rows], axis=0)
    high_x = jnp.concatenate([f[ROWS - HALO_X :] for f in fields] + [meta_rows], axis=0)
    px_low, px_high = shift(high_x, "px", 1), shift(low_x, "px", -1)
    strip = jax.ShapeDtypeStruct((3 * HALO_Y + META, 128), F32)
    low_y, high_y = pl.pallas_call(
        pack_kernel,
        out_shape=(strip, strip),
        in_specs=vmem(4),
        out_specs=tuple(vmem(2)),
    )(*fields, meta_rows)
    py_low, py_high = shift(high_y, "py", 1), shift(low_y, "py", -1)
    low_c, high_c = [], []
    for arrived in (py_low, py_high):
        for field in range(3):
            strip = arrived[field * HALO_Y : (field + 1) * HALO_Y]
            low_c.append(strip[:HALO_C])
            high_c.append(strip[HALO_Y - HALO_C :])
        low_c.append(arrived[3 * HALO_Y :])
        high_c.append(arrived[3 * HALO_Y :])
    c_low = shift(jnp.concatenate(high_c, axis=0), "px", 1)
    c_high = shift(jnp.concatenate(low_c, axis=0), "px", -1)
    sides = (px_low, px_high, py_low, py_high, c_low, c_high)

    block = pltpu.VMEM((EX, EY, 8, 128), F32)
    smem = pl.BlockSpec(memory_space=pltpu.SMEM)
    readings = pl.pallas_call(
        tangent_kernel,
        out_shape=jax.ShapeDtypeStruct((devices, 16, 128), F32),
        in_specs=[smem] + vmem(11),
        out_specs=vmem(1)[0],
        scratch_shapes=[block] * 7
        + [pltpu.VMEM((2 * CX * CY, CZ), BF16), pltpu.VMEM((8, 1024), F32)],
        compiler_params=pltpu.CompilerParams(vmem_limit_bytes=56 * 2**20),
    )(pos, *fields, *sides, meta, weights)
    got = lax.all_to_all(readings, ("px", "py"), split_axis=0, concat_axis=0, tiled=True)
    result = pl.pallas_call(
        adjoint_kernel,
        out_shape=jax.ShapeDtypeStruct((ROWS, 128), F32),
        in_specs=[smem] + vmem(10),
        out_specs=vmem(1)[0],
        scratch_shapes=[block] * 6
        + [
            pltpu.VMEM((2 * CX * CY, 4096), BF16),
            pltpu.VMEM((16, 1024), F32),
            pltpu.VMEM((8, 1024), F32),
        ],
        compiler_params=pltpu.CompilerParams(vmem_limit_bytes=56 * 2**20),
    )(pos, got, *fields[:2], *sides, meta)
    return from_tiles(result)


def solution(mesh):
    placed = (
        P("px", "py", None),
        P("px", "py", None),
        P("px", "py", None),
        P(None, ("px", "py")),
        P(None, ("px", "py")),
        P(("px", "py"), None),
        P(("px", "py")),
        P(("px", "py")),
    )
    return jax.shard_map(
        body, mesh=mesh, in_specs=placed, out_specs=P("px", "py", None), check_vma=False
    )
```

time: 327 us -> 130 us (0.40); the launches traced: 323 us -> 130 us
  starting transfers between devices: 151 us -> 13.2 us
  Pallas kernels: 0 us -> 60.3 us
  local copies, waits for them, and re-layouts: 69.1 us -> 10.4 us
  other arithmetic: 49.8 us -> 6.08 us
  waiting for transfers between devices: 51.6 us -> 12.4 us
  blocking collectives: 0 us -> 27.7 us
    ppermute x40 -> x6, starting transfers between devices: 123 us -> 13.2 us  [shift(): return lax.ppermute(x, axis, [(i, (i + by) % count) for i in range(count)])]
    pallas_call x0 -> x3, Pallas kernels: none -> 60.3 us  [the longest x1 34.8 us: body(): pl.pallas_call(adjoint_kernel, out_shape=jax.ShapeDtypeStruct((ROWS, 128)...]
    gather x3 -> x0, local copies, waits for them, and re-layouts: 47.6 us -> none  [the longest x2 41.4 us: body(): values = jnp.sum(probe_weights * flat[probe_nodes], axis=0)]
    all_to_all x3 -> x0, starting transfers between devices: 27.7 us -> none  [the longest x1 13.6 us: body(): lax.all_to_all(send_values, ('px', 'py'), split_axis=0, concat_axis=0, ti...]
    all_to_all x0 -> x1, blocking collectives: none -> 27.7 us  [body(): lax.all_to_all(readings, ('px', 'py'), split_axis=0, concat_axis=0, tiled...]
    ppermute x40 -> x6, waiting for transfers between devices: 35.5 us -> 12.4 us  [shift(): return lax.ppermute(x, axis, [(i, (i + by) % count) for i in range(count)])]
    scatter-add x1 -> x0, other arithmetic: 22.9 us -> none  [body(): source = jnp.zeros(flat.shape, jnp.float32).at[probe_nodes.reshape(-1)].a...]
    all_to_all x3 -> x0, waiting for transfers between devices: 16.1 us -> none  [the longest x1 8.77 us: body(): lax.all_to_all(send_values, ('px', 'py'), split_axis=0, concat_axis=0, ti...]
  transfers between devices with their start and end apart: 43 -> 6, of which waited for: 22 -> 4; matrix products, arithmetic and copies ran while one was open for 23% -> 7% of each run, Pallas kernels for 0% -> 0%
where the time goes in v1:
time: 130 us
  Pallas kernels  60.3 us (46%)
  blocking collectives  27.7 us (21%)
  starting transfers between devices  13.2 us (10%)
  waiting for transfers between devices  12.4 us (10%)
  local copies, waits for them, and re-layouts  10.4 us (8%)
  other arithmetic  6.08 us (5%)
    pallas_call x1, Pallas kernels, body(): pl.pallas_call(adjoint_kernel, out_shape=jax.ShapeDtypeStruct((ROWS, 128)...  34.8 us
    all_to_all x1, blocking collectives, body(): lax.all_to_all(readings, ('px', 'py'), split_axis=0, concat_axis=0, tiled...  27.7 us
    pallas_call x1, Pallas kernels, body(): pl.pallas_call(tangent_kernel, out_shape=jax.ShapeDtypeStruct((devices, 1...  22.6 us
    ppermute x6, starting transfers between devices, shift(): return lax.ppermute(x, axis, [(i, (i + by) % count) for i in range(count)])  13.2 us
    ppermute x6, waiting for transfers between devices, shift(): return lax.ppermute(x, axis, [(i, (i + by) % count) for i in range(count)])  12.4 us
    unnamed x30, local copies, waits for them, and re-layouts  8.59 us
    pallas_call x1, Pallas kernels, body(): pl.pallas_call(pack_kernel, out_shape=(strip, strip), in_specs=vmem(4), o...  2.95 us
  transfers between devices with their start and end apart: 6, of which 4 were waited for; matrix products, arithmetic and copies ran while one was open for 7% of the time, Pallas kernels for 0%

profile of v1, /device:TPU:1, one launch (start us, length us, event | category | flops | bytes accessed | tf_op | source)
XLA Modules:
  0.0 130.1 jit_solution(9828499795060862994)
XLA Ops:
  0.0 0.7 broadcast_multiply_fusion
  0.7 0.7 convert_element_type.9
  1.4 0.7 add_convert_fusion
  2.1 0.1 pad.11.clone
  2.2 1.5 %maximum_maximum_fusion.meta = f32[16,1024]{1,0:T(8,128)} fusion(f32[1,1024]{1,0:T(1,128)S(1)} %bitcast.55, f32[4,1024]{1,0:T(4,128)} %param.12, f32[4,1024]{1,0:T(4,128)S(1)} %convert_element_type.9, f32[16]{0:T(128)S(1)} %pad.11.clone), kind=kLoop, calls=%fused_computation.6 | loop fusion | flops 49152 | bytes 102464 | tf_op jit(solution)/shard_map/concatenate | solution.py:501
  3.7 3.0 %shard_map.82 = (f32[896,128]{1,0:T(8,128)}, f32[896,128]{1,0:T(8,128)}) custom-call(f32[2048,128]{1,0:T(8,128)} %bitcast.36, f32[2048,128]{1,0:T(8,128)} %bitcast.40, f32[2048,128]{1,0:T(8,128)} %bitcast.44, f32[128,128]{1,0:T(8,128)} %bitcast.53), custom_call_target="tpu_custom_call" | custom-call | tf_op jit(solution)/shard_map/pallas_call | solution.py:520
  6.6 2.0 %collective-permute-start.2 = (f32[896,128]{1,0:T(8,128)}, f32[896,128]{1,0:T(8,128)S(1)}, u32[]{:S(2)}, u32[]{:S(2)}) collective-permute-start(f32[896,128]{1,0:T(8,128)} %get-tuple-element.7), channel_id=1, source_target_pairs={{0,1},{1,2},{2,3},{3,4},{4,5},{5,6},{6,7},{7,8},{8,9},{9,10},{10,1... | collective-permute-start | bytes 1376264 | tf_op jit(solution)/shard_map/ppermute | solution.py:482
  8.7 0.0 copy-done.2
  8.7 0.1 fusion.2
  8.8 0.0 copy-done.1
  8.8 0.0 copy-start.7
  8.8 0.1 fusion.1
  8.9 1.1 copy-done
  9.9 0.1 fusion
  10.0 0.0 copy-done.7
  10.0 0.0 copy-start.10
  10.0 1.9 %pad_maximum_fusion = (f32[3200,128]{1,0:T(8,128)}, f32[3200,128]{1,0:T(8,128)}) fusion(f32[128,128]{1,0:T(8,128)S(1)} %bitcast.54, f32[1024,128]{1,0:T(8,128)S(1)} %bitcast.47, f32[1024,128]{1,0:T(8,128)S(1)} %bitcast.49, f32[1024,128]{1,0:T(8,128)S(1)} %bitcast.51, f32[1024,128]{1,0:T(8,128)S(1)} %bitcast.48, f32[1024,128]{1,0:T(8,128)S(1)} %bitcast.50, ...), kind=kLoop, calls=%fused_computation | loop fusion | flops 2457600 | bytes 6488064 | tf_op jit(solution)/shard_map/concatenate | solution.py:516
  11.9 2.5 %collective-permute-start = (f32[3200,128]{1,0:T(8,128)}, f32[3200,128]{1,0:T(8,128)S(1)}, u32[]{:S(2)}, u32[]{:S(2)}) collective-permute-start(f32[3200,128]{1,0:T(8,128)} %get-tuple-element.24), channel_id=1, source_target_pairs={{0,16},{16,32},{32,48},{48,64},{64,80},{80,96},{96,112},{112,0},{1... | collective-permute-start | bytes 4915208 | tf_op jit(solution)/shard_map/ppermute | solution.py:482
  14.4 0.0 collective-permute-start.1
  14.4 0.0 copy-done.10
  14.4 4.3 %collective-permute-start.3 = (f32[896,128]{1,0:T(8,128)S(1)}, f32[896,128]{1,0:T(8,128)S(1)}, u32[]{:S(2)}, u32[]{:S(2)}) collective-permute-start(f32[896,128]{1,0:T(8,128)S(1)} %copy-done.10), channel_id=1, source_target_pairs={{0,15},{1,0},{2,1},{3,2},{4,3},{5,4},{6,5},{7,6},{8,7},{9,8},{10,9... | collective-permute-start | bytes 1376264 | tf_op jit(solution)/shard_map/ppermute | solution.py:482
  18.6 4.2 %collective-permute-done.2.py_low = f32[896,128]{1,0:T(8,128)S(1)} collective-permute-done((f32[896,128]{1,0:T(8,128)}, f32[896,128]{1,0:T(8,128)S(1)}, u32[]{:S(2)}, u32[]{:S(2)}) %collective-permute-start.2) | collective-permute-done | bytes 458784 | tf_op jit(solution)/shard_map/ppermute | solution.py:482
  22.8 0.7 slice_dynamic-update-slice_fusion.9
  23.4 0.6 slice_dynamic-update-slice_fusion.8
  24.1 0.6 slice_dynamic-update-slice_fusion.7
  24.7 0.6 slice_dynamic-update-slice_fusion.3
  25.4 1.1 collective-permute-done.3.py_high
  26.5 0.7 slice_dynamic-update-slice_fusion.6
  27.2 0.0 copy-done.5
  27.2 0.6 slice_dynamic-update-slice_fusion.1
  27.8 0.6 slice_dynamic-update-slice_fusion.5
  28.4 0.6 slice_dynamic-update-slice_fusion.4
  29.1 0.7 slice_dynamic-update-slice_fusion
  29.7 4.4 %collective-permute-start.4 = (f32[832,128]{1,0:T(8,128)}, f32[832,128]{1,0:T(8,128)}, u32[]{:S(2)}, u32[]{:S(2)}) collective-permute-start(f32[832,128]{1,0:T(8,128)} %slice_dynamic-update-slice_fusion), channel_id=1, source_target_pairs={{0,16},{16,32},{32,48},{48,64},{64,80},{80,96},{96,112},{112,0},{1... | collective-permute-start | bytes 1277960 | tf_op jit(solution)/shard_map/ppermute | solution.py:482
  34.1 0.6 slice_dynamic-update-slice_fusion.2
  34.8 0.0 collective-permute-start.5
  34.8 0.0 copy-done.9
  34.8 0.2 dynamic_update_slice.3.weights
  35.0 0.6 pad_add_fusion.pos
  35.6 3.9 %collective-permute-done.4.c_low = f32[832,128]{1,0:T(8,128)} collective-permute-done((f32[832,128]{1,0:T(8,128)}, f32[832,128]{1,0:T(8,128)}, u32[]{:S(2)}, u32[]{:S(2)}) %collective-permute-start.4) | collective-permute-done | bytes 426016 | tf_op jit(solution)/shard_map/ppermute | solution.py:482
  39.5 3.1 %collective-permute-done.5.c_high = f32[832,128]{1,0:T(8,128)} collective-permute-done((f32[832,128]{1,0:T(8,128)}, f32[832,128]{1,0:T(8,128)}, u32[]{:S(2)}, u32[]{:S(2)}) %collective-permute-start.5) | collective-permute-done | bytes 426016 | tf_op jit(solution)/shard_map/ppermute | solution.py:482
  42.6 0.0 collective-permute-done.px_low
  42.7 0.0 collective-permute-done.1.px_high
  42.7 1.1 copy-done.3
  43.8 1.2 copy-done.4
  45.0 22.6 %shard_map.83 = f32[128,16,128]{2,1,0:T(8,128)} custom-call(s32[4]{0:T(128)} %pad_add_fusion.pos, f32[2048,128]{1,0:T(8,128)} %bitcast.37, f32[2048,128]{1,0:T(8,128)} %bitcast.41, f32[2048,128]{1,0:T(8,128)} %bitcast.45, f32[3200,128]{1,0:T(8,128)} %copy-done.3, f32[3200,128]{1,0:T(8,128)} %copy-done.4, f32[896,128]{1,0:T(8,128)} %copy-done.5, ...), custom_call_target="tpu_custom_call" | custom-call | tf_op jit(solution)/shard_map/pallas_call | solution.py:541
  67.6 27.7 %all_to_all.5.got = f32[128,16,128]{2,1,0:T(8,128)} all-to-all(f32[128,16,128]{2,1,0:T(8,128)} %shard_map.83), channel_id=1, replica_groups=mesh['px'=8,'py'=16] {'px','py'}, dimensions={0} | all-to-all | bytes 2097152 | tf_op jit(solution)/shard_map/all_to_all | solution.py:550
  95.3 34.8 %shard_map.84 = f32[2048,128]{1,0:T(8,128)} custom-call(s32[4]{0:T(128)} %pad_add_fusion.pos, f32[128,16,128]{2,1,0:T(8,128)} %all_to_all.5.got, f32[2048,128]{1,0:T(8,128)} %bitcast.38, f32[2048,128]{1,0:T(8,128)} %bitcast.42, f32[3200,128]{1,0:T(8,128)} %copy-done.3, f32[3200,128]{1,0:T(8,128)} %copy-done.4, f32[896,128]{1,0:T(8,128)} %copy-done.5, ...), custom_call_target="tpu_custom_call" | custom-call | tf_op jit(solution)/shard_map/pallas_call | solution.py:551
  (13 shorter events, 0.0 us)
Async XLA Ops:
  2.2 6.5 %copy-start.2 = (f32[8,32,1024]{2,1,0:T(8,128)S(1)}, f32[8,32,1024]{2,1,0:T(8,128)}, u32[]{:S(2)}) copy-start(f32[8,32,1024]{2,1,0:T(8,128)} %param.9) | copy-start | bytes 3145732
  6.6 2.1 %copy-start.1 = (f32[8,32,1024]{2,1,0:T(8,128)S(1)}, f32[8,32,1024]{2,1,0:T(8,128)}, u32[]{:S(2)}) copy-start(f32[8,32,1024]{2,1,0:T(8,128)} %param.8) | copy-start | bytes 3145732
  6.6 16.2 %collective-permute-start.2 = (f32[896,128]{1,0:T(8,128)}, f32[896,128]{1,0:T(8,128)S(1)}, u32[]{:S(2)}, u32[]{:S(2)}) collective-permute-start(f32[896,128]{1,0:T(8,128)} %get-tuple-element.7), channel_id=1, source_target_pairs={{0,1},{1,2},{2,3},{3,4},{4,5},{5,6},{6,7},{7,8},{8,9},{9,10},{10,1... | collective-permute-start | bytes 1376264 | tf_op jit(solution)/shard_map/ppermute | solution.py:482
  8.7 1.2 copy-start
  8.8 1.2 copy-start.7
  10.0 4.4 %copy-start.10 = (f32[896,128]{1,0:T(8,128)S(1)}, f32[896,128]{1,0:T(8,128)}, u32[]{:S(2)}) copy-start(f32[896,128]{1,0:T(8,128)} %get-tuple-element.8) | copy-start | bytes 1376260
  11.9 22.9 %copy-start.9 = (f32[8]{0:T(128)S(1)}, f32[8]{0:T(128)}, u32[]{:S(2)}) copy-start(f32[8]{0:T(128)} %param.15) | copy-start | bytes 100
  11.9 30.8 %collective-permute-start = (f32[3200,128]{1,0:T(8,128)}, f32[3200,128]{1,0:T(8,128)S(1)}, u32[]{:S(2)}, u32[]{:S(2)}) collective-permute-start(f32[3200,128]{1,0:T(8,128)} %get-tuple-element.24), channel_id=1, source_target_pairs={{0,16},{16,32},{32,48},{48,64},{64,80},{80,96},{96,112},{112,0},{1... | collective-permute-start | bytes 4915208 | tf_op jit(solution)/shard_map/ppermute | solution.py:482
  14.4 28.3 %collective-permute-start.1 = (f32[3200,128]{1,0:T(8,128)}, f32[3200,128]{1,0:T(8,128)S(1)}, u32[]{:S(2)}, u32[]{:S(2)}) collective-permute-start(f32[3200,128]{1,0:T(8,128)} %get-tuple-element.23), channel_id=1, source_target_pairs={{0,112},{16,0},{32,16},{48,32},{64,48},{80,64},{96,80},{112,96},{1... | collective-permute-start | bytes 4915208 | tf_op jit(solution)/shard_map/ppermute | solution.py:482
  14.4 12.1 %collective-permute-start.3 = (f32[896,128]{1,0:T(8,128)S(1)}, f32[896,128]{1,0:T(8,128)S(1)}, u32[]{:S(2)}, u32[]{:S(2)}) collective-permute-start(f32[896,128]{1,0:T(8,128)S(1)} %copy-done.10), channel_id=1, source_target_pairs={{0,15},{1,0},{2,1},{3,2},{4,3},{5,4},{6,5},{7,6},{8,7},{9,8},{10,9... | collective-permute-start | bytes 1376264 | tf_op jit(solution)/shard_map/ppermute | solution.py:482
  22.8 4.4 %copy-start.5 = (f32[896,128]{1,0:T(8,128)}, f32[896,128]{1,0:T(8,128)S(1)}, u32[]{:S(2)}) copy-start(f32[896,128]{1,0:T(8,128)S(1)} %collective-permute-done.2.py_low) | copy-start | bytes 1376260
  26.5 7.7 %copy-start.6 = (f32[896,128]{1,0:T(8,128)}, f32[896,128]{1,0:T(8,128)S(1)}, u32[]{:S(2)}) copy-start(f32[896,128]{1,0:T(8,128)S(1)} %collective-permute-done.3.py_high) | copy-start | bytes 1376260
  29.7 9.8 %collective-permute-start.4 = (f32[832,128]{1,0:T(8,128)}, f32[832,128]{1,0:T(8,128)}, u32[]{:S(2)}, u32[]{:S(2)}) collective-permute-start(f32[832,128]{1,0:T(8,128)} %slice_dynamic-update-slice_fusion), channel_id=1, source_target_pairs={{0,16},{16,32},{32,48},{48,64},{64,80},{80,96},{96,112},{112,0},{1... | collective-permute-start | bytes 1277960 | tf_op jit(solution)/shard_map/ppermute | solution.py:482
  34.8 7.9 %collective-permute-start.5 = (f32[832,128]{1,0:T(8,128)}, f32[832,128]{1,0:T(8,128)}, u32[]{:S(2)}, u32[]{:S(2)}) collective-permute-start(f32[832,128]{1,0:T(8,128)} %slice_dynamic-update-slice_fusion.2), channel_id=1, source_target_pairs={{0,112},{16,0},{32,16},{48,32},{64,48},{80,64},{96,80},{112,96},{1... | collective-permute-start | bytes 1277960 | tf_op jit(solution)/shard_map/ppermute | solution.py:482
  35.0 7.7 %copy-start.8 = (f32[8,128]{1,0:T(8,128)}, f32[8,128]{1,0:T(8,128)S(1)}, u32[]{:S(2)}) copy-start(f32[8,128]{1,0:T(8,128)S(1)} %dynamic_update_slice.3.weights) | copy-start | bytes 12292
  42.6 1.2 copy-start.3
  43.8 1.2 copy-start.4

commit v2 on v1

--- a/solution.py
+++ b/solution.py
@@ -95,58 +95,41 @@
     lax.fori_loop(margin, EX - margin, plane, 0)
 
 
-def own_rows(ref, out, scale):
-    def plane(x, carry):
-        for yt in range(CY // 8):
-            for ys in range(8):
-                v = ref[pl.ds((x * (CY // 8) + yt) * 64 + ys, 8, stride=8), :]
-                out[x + D, D + yt * 8 + ys] = v * scale if scale != 1.0 else v
-        return carry
-
-    lax.fori_loop(0, CX, plane, 0)
-
-
-def extend(field, own, px_low, px_high, py_low, py_high, c_low, c_high, out, scale):
-    own_rows(own, out, scale)
+def extend(field, own, sides, out, scale):
+    px_low, px_high, py_low, py_high, c_low, c_high = sides
+    middle_x, middle_y = slice(D, D + CX), slice(D, D + CY)
+    out[middle_x, middle_y] = own[...]
     for ref, at in ((px_low, 0), (px_high, D + CX)):
-
-        def plane(x, carry, ref=ref, at=at):
-            for yt in range(CY // 8):
-                for ys in range(8):
-                    v = ref[
-                        pl.ds(field * HALO_X + (x * (CY // 8) + yt) * 64 + ys, 8, stride=8), :
-                    ]
-                    out[x + at, D + yt * 8 + ys] = v * scale
-            return carry
-
-        lax.fori_loop(0, D, plane, 0)
+        v = ref[field * HALO_X : (field + 1) * HALO_X, :]
+        out[at : at + D, middle_y] = v.reshape(D, CY, 8, 128) * scale
     for ref, at in ((py_low, 0), (py_high, D + CY)):
-        for x in range(CX):
-            v = ref[pl.ds(field * HALO_Y + x * D * 8, D * 8), :]
-            out[x + D, pl.ds(at, D)] = v.reshape(D, 8, 128) * scale
+        v = ref[field * HALO_Y : (field + 1) * HALO_Y, :]
+        out[middle_x, at : at + D] = v.reshape(CX, D, 8, 128) * scale
     part = 3 * HALO_C + META
     for ref, at, gap in ((c_low, 1, 0), (c_high, D + CX, D + CX + DC)):
         for side, to in ((0, 0), (1, D + CY)):
-            out[gap, pl.ds(to, D)] = jnp.zeros((D, 8, 128), F32)
-            for x in range(DC):
-                v = ref[pl.ds(side * part + field * HALO_C + x * D * 8, D * 8), :]
-                out[at + x, pl.ds(to, D)] = v.reshape(D, 8, 128) * scale
-
-
-def close_edges(pos, out, sign):
-    @pl.when(pos[0] == 0)
+            out[gap, to : to + D] = jnp.zeros((D, 8, 128), F32)
+            v = ref[side * part + field * HALO_C : side * part + (field + 1) * HALO_C, :]
+            out[at : at + DC, to : to + D] = v.reshape(DC, D, 8, 128) * scale
+
+
+def close_edges(out, sign):
+    px, py = lax.axis_index("px"), lax.axis_index("py")
+    last_x, last_y = lax.axis_size("px") - 1, lax.axis_size("py") - 1
+
+    @pl.when(px == 0)
     def _():
         out[D - 1] = out[D] * sign
 
-    @pl.when(pos[0] == pos[2])
+    @pl.when(px == last_x)
     def _():
         out[D + CX] = out[D + CX - 1] * sign
 
-    @pl.when(pos[1] == 0)
+    @pl.when(py == 0)
     def _():
         out[:, D - 1] = out[:, D] * sign
 
-    @pl.when(pos[1] == pos[3])
+    @pl.when(py == last_y)
     def _():
         out[:, D + CY] = out[:, D + CY - 1] * sign
 
@@ -181,7 +164,6 @@
 
 
 def tangent_kernel(
-    pos,
     permit,
     back,
     perturb,
@@ -192,12 +174,13 @@
     c_low,
     c_high,
     meta,
+    hot,
     weights,
     out,
     q,
-    qp,
     bg,
     cz,
+    qp,
     b,
     y1,
     y2,
@@ -205,11 +188,12 @@
     vals,
 ):
     sides = (px_low, px_high, py_low, py_high, c_low, c_high)
-    extend(0, permit, *sides, q, 0.5 / HALF)
-    extend(1, back, *sides, bg, 1.0)
-    extend(2, perturb, *sides, qp, 0.5)
-    close_edges(pos, q, -1.0)
-    close_edges(pos, qp, -1.0)
+    extend(0, permit, sides, q, 0.5 / HALF)
+    extend(1, back, sides, bg, 1.0)
+    extend(2, perturb, sides, qp, 0.5)
+    close_edges(q, -1.0)
+    close_edges(qp, -1.0)
+    close_edges(bg, 1.0)
 
     def first(x, y, n):
         _, acc = fluxes(bg, qp, None, x, y, n)
@@ -247,7 +231,7 @@
     def gather(i, carry):
         k, lanes = i // 2, pl.ds(pl.multiple_of((i % 2) * wide, wide), wide)
         node = meta[pl.ds(k, 1), lanes].astype(jnp.int32)
-        found = dot(table[...], one_hot(node & (CZ - 1), CZ), ((1,), (0,)))
+        found = dot(table[...], hot[:, pl.ds(pl.multiple_of(i * wide, wide), wide)], ((1,), (0,)))
         found = found[: CX * CY] + found[CX * CY :]
         at = lax.broadcasted_iota(jnp.int32, found.shape, 0)
         found = jnp.sum(jnp.where(at == node >> 10, found, 0.0), axis=0, keepdims=True)
@@ -256,17 +240,18 @@
 
     lax.fori_loop(0, 8, gather, 0)
 
-    key = meta[8:9, :].astype(jnp.int32)
+    owner, sensor = meta[8:9, :].astype(jnp.int32), meta[9:10, :].astype(jnp.int32)
     at = lax.broadcasted_iota(jnp.int32, (8, 1024), 0)
-    owned = jnp.where(at == key >> 7, vals[0:1, :], 0.0)
+    owned = jnp.where(at == sensor, vals[0:1, :], 0.0)
     parts = jnp.concatenate(three_parts(owned), axis=0)
-    sums = dot(parts, one_hot(key & 127, 128), ((1,), (1,)))
+    sums = dot(parts, one_hot(owner, 128), ((1,), (1,)))
     readings = sums[0:8] + sums[8:16] + sums[16:24]
-    both = jnp.concatenate([readings, weights[...]], axis=0)
-    out[...] = jnp.broadcast_to(both[None], out.shape)
-
-
-def scatter(meta, values, rows, cols, per, tiles, lhs, keep):
+    block = jnp.concatenate([readings, weights[...]] * 8, axis=0)
+    for i in range(out.shape[0] // 72):
+        out[i * 72 : (i + 1) * 72, :] = block
+
+
+def scatter(meta, values, rows, cols, per, tiles, lhs, keep, hot=None):
     for k in range(4):
         node = meta[k : k + 1, :].astype(jnp.int32)
         high, low = two_parts(values[k : k + 1, :])
@@ -278,9 +263,13 @@
     def tile(t, carry):
         total = None
         for k in range(4):
-            node = meta[k : k + 1, :].astype(jnp.int32)
             lanes = slice(k * 1024, (k + 1) * 1024)
-            part = dot(lhs[0 : 2 * per, lanes], one_hot(cols(node) - t * 256, 256), ((1,), (1,)))
+            if hot is None:
+                node = meta[k : k + 1, :].astype(jnp.int32)
+                hits = one_hot(cols(node) - t * 256, 256)
+            else:
+                hits = hot[pl.ds(pl.multiple_of(t * 256, 256), 256), lanes]
+            part = dot(lhs[0 : 2 * per, lanes], hits, ((1,), (1,)))
             total = part if total is None else total + part
         keep(t, total[0:per] + total[per : 2 * per])
         return carry
@@ -292,10 +281,7 @@
 
 
 def adjoint_kernel(
-    pos,
     got,
-    permit,
-    back,
     px_low,
     px_high,
     py_low,
@@ -303,10 +289,11 @@
     c_low,
     c_high,
     meta,
-    out,
+    hot,
     q,
     bg,
     cz,
+    out,
     src,
     y1,
     y2,
@@ -314,21 +301,18 @@
     near,
     values,
 ):
-    sides = (px_low, px_high, py_low, py_high, c_low, c_high)
-    extend(0, permit, *sides, q, 0.5 / HALF)
-    extend(1, back, *sides, bg, 1.0)
-    close_edges(pos, q, -1.0)
-    close_edges(pos, bg, 1.0)
-
-    both = jnp.sum(got[...], axis=0)
-    weighted = jnp.concatenate(three_parts(both[0:8] * both[8:16]), axis=0)
+    count = got.shape[0] // 9
+    sums = [jnp.sum(got[pl.ds(i, count, stride=9), :], axis=0, keepdims=True) for i in range(8)]
+    readings = jnp.concatenate(sums, axis=0)
+    weights = jnp.transpose(got[pl.ds(8, count, stride=9), :])[0:8]
+    weighted = jnp.concatenate(three_parts(readings * weights), axis=0)
 
     def returned(table):
-        key = table[8:9, :].astype(jnp.int32)
-        found = dot(weighted, one_hot(key & 127, 128), ((1,), (0,)))
+        owner, sensor = table[8:9, :].astype(jnp.int32), table[9:10, :].astype(jnp.int32)
+        found = dot(weighted, one_hot(owner, 128), ((1,), (0,)))
         found = found[0:8] + found[8:16] + found[16:24]
         at = lax.broadcasted_iota(jnp.int32, found.shape, 0)
-        found = jnp.sum(jnp.where(at == key >> 7, found, 0.0), axis=0, keepdims=True)
+        found = jnp.sum(jnp.where(at == sensor, found, 0.0), axis=0, keepdims=True)
         values[0:4, :] = table[4:8, :] * found
 
     flat = src.reshape(EX * EY * 8, 128)
@@ -365,7 +349,7 @@
         return node & 255
 
     returned(meta)
-    scatter(meta, values, lambda n: n >> 10, column, CX * CY, 4, lhs, put_planes(D, CX))
+    scatter(meta, values, lambda n: n >> 10, column, CX * CY, 4, lhs, put_planes(D, CX), hot)
 
     for ref, x0, first in ((px_low, 0, CX - D), (px_high, D + CX, 0)):
         take_meta(ref, 3 * HALO_X, near)
@@ -414,7 +398,6 @@
             )
 
     def first(x, y, n):
-        cz[x, pl.ds(y, n)] = z_face(q[x, pl.ds(y, n)])
         f, acc = fluxes(src, q, cz, x, y, n)
         y1[x, pl.ds(y, n)] = (A2 - A3) * f - A3 * acc
 
@@ -461,16 +444,83 @@
     return jnp.swapaxes(split, -3, -2).reshape(CX, CY, CZ)
 
 
-def pack_kernel(permit, back, perturb, meta, low, high):
+def row_of(ref, x, y):
+    return ref[pl.ds((x * (CY // 8) + y // 8) * 64 + y % 8, 8, stride=8), :]
+
+
+def pack_kernel(
+    permit,
+    back,
+    perturb,
+    nodes,
+    probe_weights,
+    owner,
+    sensor,
+    low_x,
+    high_x,
+    low_y,
+    high_y,
+    meta,
+):
+    meta[0:4, :] = nodes[...].astype(F32)
+    meta[4:8, :] = probe_weights[...]
+    meta[8:9, :] = owner[...].astype(F32)
+    meta[9:10, :] = sensor[...].astype(F32)
+    meta[10:16, :] = jnp.zeros((6, 1024), F32)
     for field, ref in enumerate((permit, back, perturb)):
+
+        def plane(x, carry, field=field, ref=ref):
+            for y in range(CY):
+                at = pl.ds(field * HALO_X + (x * CY + y) * 8, 8)
+                low_x[at, :] = row_of(ref, x, y)
+                high_x[at, :] = row_of(ref, x + CX - D, y)
+            return carry
+
+        lax.fori_loop(0, D, plane, 0)
         for x in range(CX):
             for y in range(D):
                 at = pl.ds(field * HALO_Y + (x * D + y) * 8, 8)
-                low[at, :] = ref[pl.ds(x * (CY // 8) * 64 + y, 8, stride=8), :]
-                last = x * (CY // 8) + CY // 8 - 1
-                high[at, :] = ref[pl.ds(last * 64 + 8 - D + y, 8, stride=8), :]
-    low[3 * HALO_Y :, :] = meta[...]
-    high[3 * HALO_Y :, :] = meta[...]
+                low_y[at, :] = row_of(ref, x, y)
+                high_y[at, :] = row_of(ref, x, y + CY - D)
+    for half in range(2):
+        for c in range(8):
+            v = meta[half * 8 : half * 8 + 8, c * 128 : (c + 1) * 128]
+            at = half * 64 + c * 8
+            low_x[3 * HALO_X + at : 3 * HALO_X + at + 8, :] = v
+            high_x[3 * HALO_X + at : 3 * HALO_X + at + 8, :] = v
+            low_y[3 * HALO_Y + at : 3 * HALO_Y + at + 8, :] = v
+            high_y[3 * HALO_Y + at : 3 * HALO_Y + at + 8, :] = v
+
+
+def own_kernel(permit, back, perturb, meta, q, bg, qp, hot):
+    def plane(x, carry):
+        for y in range(CY):
+            q[x, y] = row_of(permit, x, y) * (0.5 / HALF)
+            bg[x, y] = row_of(back, x, y)
+            qp[x, y] = row_of(perturb, x, y) * 0.5
+        return carry
+
+    lax.fori_loop(0, CX, plane, 0)
+
+    def entries(i, carry):
+        k, lanes = i // 2, pl.ds(pl.multiple_of((i % 2) * 512, 512), 512)
+        node = meta[pl.ds(k, 1), lanes].astype(jnp.int32)
+        hot[:, pl.ds(pl.multiple_of(i * 512, 512), 512)] = one_hot(node & (CZ - 1), CZ)
+        return carry
+
+    lax.fori_loop(0, 8, entries, 0)
+
+
+def corner_kernel(py_low, py_high, low, high):
+    part = 3 * HALO_C + META
+    for side, ref in enumerate((py_low, py_high)):
+        for field in range(3):
+            at, first = side * part + field * HALO_C, field * HALO_Y
+            low[at : at + HALO_C, :] = ref[first : first + HALO_C, :]
+            high[at : at + HALO_C, :] = ref[first + HALO_Y - HALO_C : first + HALO_Y, :]
+        at = side * part + 3 * HALO_C
+        low[at : at + META, :] = ref[3 * HALO_Y :, :]
+        high[at : at + META, :] = ref[3 * HALO_Y :, :]
 
 
 def vmem(count):
@@ -492,75 +542,94 @@
     probe_sensor,
     sensor_weight,
 ):
-    count_x, count_y = lax.axis_size("px"), lax.axis_size("py")
-    px, py = lax.axis_index("px"), lax.axis_index("py")
-    owned = sensor_weight.shape[0]
-    devices = count_x * count_y
-    pos = jnp.stack([px, py, jnp.int32(count_x - 1), jnp.int32(count_y - 1)]).astype(jnp.int32)
-    key = probe_owner.reshape(1, -1) * owned + probe_sensor[None, :]
-    meta = jnp.concatenate(
-        [
-            probe_nodes.astype(F32),
-            probe_weights,
-            key.astype(F32),
-            jnp.zeros((7, key.shape[1]), F32),
-        ],
-        axis=0,
+    devices = lax.axis_size("px") * lax.axis_size("py")
+    fields = [by_tiles(f) for f in (permittivity, background_field, perturbation)]
+    weights = jnp.pad(sensor_weight, (0, 128 - sensor_weight.shape[0]))[None, :]
+
+    def rows(*counts):
+        return [jax.ShapeDtypeStruct((n, 128), F32) for n in counts]
+
+    def call(kernel, outs, *args, scratch=(), limit, bytes_accessed=0):
+        return pl.pallas_call(
+            kernel,
+            out_shape=tuple(outs),
+            in_specs=vmem(len(args)),
+            out_specs=tuple(vmem(len(outs))),
+            scratch_shapes=scratch,
+            compiler_params=pltpu.CompilerParams(vmem_limit_bytes=limit * 2**20),
+            cost_estimate=pl.CostEstimate(
+                flops=0, bytes_accessed=bytes_accessed, transcendentals=0
+            ),
+        )(*args)
+
+    size_x, size_y, size_c = 3 * HALO_X + META, 3 * HALO_Y + META, 2 * (3 * HALO_C + META)
+    table = jax.ShapeDtypeStruct((16, 1024), F32)
+    low_x, high_x, low_y, high_y, meta = call(
+        pack_kernel,
+        rows(size_x, size_x, size_y, size_y) + [table],
+        *fields,
+        probe_nodes,
+        probe_weights,
+        probe_owner.reshape(1, -1),
+        probe_sensor.reshape(1, -1),
+        limit=4,
     )
-    weights = lax.dynamic_update_slice(
-        jnp.zeros((8, 128), F32), sensor_weight[None, :], (px, py * owned)
+    px_low, px_high = shift(high_x, "px", 1), shift(low_x, "px", -1)
+    py_low, py_high = shift(high_y, "py", 1), shift(low_y, "py", -1)
+    compact = jax.ShapeDtypeStruct((CX, CY, 8, 128), F32)
+    full = jax.ShapeDtypeStruct((EX, EY, 8, 128), F32)
+    own_q, own_bg, own_qp, hot = call(
+        own_kernel,
+        [compact] * 3 + [jax.ShapeDtypeStruct((CZ, 4096), BF16)],
+        *fields,
+        meta,
+        limit=8,
+        bytes_accessed=8 * 2**20,
     )
-    fields = [by_tiles(f) for f in (permittivity, background_field, perturbation)]
-    meta_rows = by_tiles(meta)
-
-    low_x = jnp.concatenate([f[:HALO_X] for f in fields] + [meta_rows], axis=0)
-    high_x = jnp.concatenate([f[ROWS - HALO_X :] for f in fields] + [meta_rows], axis=0)
-    px_low, px_high = shift(high_x, "px", 1), shift(low_x, "px", -1)
-    strip = jax.ShapeDtypeStruct((3 * HALO_Y + META, 128), F32)
-    low_y, high_y = pl.pallas_call(
-        pack_kernel,
-        out_shape=(strip, strip),
-        in_specs=vmem(4),
-        out_specs=tuple(vmem(2)),
-    )(*fields, meta_rows)
-    py_low, py_high = shift(high_y, "py", 1), shift(low_y, "py", -1)
-    low_c, high_c = [], []
-    for arrived in (py_low, py_high):
-        for field in range(3):
-            strip = arrived[field * HALO_Y : (field + 1) * HALO_Y]
-            low_c.append(strip[:HALO_C])
-            high_c.append(strip[HALO_Y - HALO_C :])
-        low_c.append(arrived[3 * HALO_Y :])
-        high_c.append(arrived[3 * HALO_Y :])
-    c_low = shift(jnp.concatenate(high_c, axis=0), "px", 1)
-    c_high = shift(jnp.concatenate(low_c, axis=0), "px", -1)
+    low_c, high_c = call(corner_kernel, rows(size_c, size_c), py_low, py_high, limit=4)
+    c_low, c_high = shift(high_c, "px", 1), shift(low_c, "px", -1)
     sides = (px_low, px_high, py_low, py_high, c_low, c_high)
 
     block = pltpu.VMEM((EX, EY, 8, 128), F32)
-    smem = pl.BlockSpec(memory_space=pltpu.SMEM)
-    readings = pl.pallas_call(
+    readings, q, bg, cz = call(
         tangent_kernel,
-        out_shape=jax.ShapeDtypeStruct((devices, 16, 128), F32),
-        in_specs=[smem] + vmem(11),
-        out_specs=vmem(1)[0],
-        scratch_shapes=[block] * 7
+        rows(devices * 9) + [full] * 3,
+        own_q,
+        own_bg,
+        own_qp,
+        *sides,
+        meta,
+        hot,
+        weights,
+        scratch=[block] * 4
         + [pltpu.VMEM((2 * CX * CY, CZ), BF16), pltpu.VMEM((8, 1024), F32)],
-        compiler_params=pltpu.CompilerParams(vmem_limit_bytes=56 * 2**20),
-    )(pos, *fields, *sides, meta, weights)
-    got = lax.all_to_all(readings, ("px", "py"), split_axis=0, concat_axis=0, tiled=True)
-    result = pl.pallas_call(
+        limit=18,
+    )
+    got = lax.all_to_all(
+        readings.reshape(devices, 1, 9 * 128),
+        ("px", "py"),
+        split_axis=0,
+        concat_axis=0,
+        tiled=True,
+    ).reshape(devices * 9, 128)
+    (result,) = call(
         adjoint_kernel,
-        out_shape=jax.ShapeDtypeStruct((ROWS, 128), F32),
-        in_specs=[smem] + vmem(10),
-        out_specs=vmem(1)[0],
-        scratch_shapes=[block] * 6
+        rows(ROWS),
+        got,
+        *sides,
+        meta,
+        hot,
+        q,
+        bg,
+        cz,
+        scratch=[block] * 3
         + [
             pltpu.VMEM((2 * CX * CY, 4096), BF16),
             pltpu.VMEM((16, 1024), F32),
             pltpu.VMEM((8, 1024), F32),
         ],
-        compiler_params=pltpu.CompilerParams(vmem_limit_bytes=56 * 2**20),
-    )(pos, got, *fields[:2], *sides, meta)
+        limit=24,
+    )
     return from_tiles(result)
 
 

time: 130 us -> 106 us (0.82)
  Pallas kernels: 60.3 us -> 49.6 us
  other arithmetic: 6.08 us -> 0 us
  blocking collectives: 27.7 us -> 23.6 us
  local copies, waits for them, and re-layouts: 10.4 us -> 6.5 us
  waiting for transfers between devices: 12.4 us -> 14 us
    pallas_call x3 -> x5, Pallas kernels: 60.3 us -> 49.6 us  [call(): pl.pallas_call(kernel, out_shape=tuple(outs), in_specs=vmem(len(args)), o...]
    all_to_all x1, blocking collectives: 27.7 us -> 23.6 us  [body(): lax.all_to_all(readings.reshape(devices, 1, 9 * 128), ('px', 'py'), split...]
    concatenate x2 -> x0, other arithmetic: 3.38 us -> none  [the longest x1 1.88 us: body(): low_x = jnp.concatenate([f[:HALO_X] for f in fields] + [meta_rows], axis=0)]
    unnamed x30 -> x22, local copies, waits for them, and re-layouts: 8.59 us -> 6.5 us
    ppermute x6, waiting for transfers between devices: 12.4 us -> 14 us  [shift(): return lax.ppermute(x, axis, [(i, (i + by) % count) for i in range(count)])]
    convert_element_type x2 -> x0, other arithmetic: 1.41 us -> none  [the longest x1 0.72 us: body(): probe_nodes.astype(F32)]
    concatenate x3 -> x0, local copies, waits for them, and re-layouts: 1.37 us -> none  [the longest x1 0.66 us: body(): c_low = shift(jnp.concatenate(high_c, axis=0), 'px', 1)]
  transfers between devices with their start and end apart: 6 -> 6, of which waited for: 4 -> 3; matrix products, arithmetic and copies ran while one was open for 7% -> 0% of each run, Pallas kernels for 0% -> 2%
where the time goes in v2:
time: 106 us
  Pallas kernels  49.6 us (47%)
  blocking collectives  23.6 us (22%)
  waiting for transfers between devices  14 us (13%)
  starting transfers between devices  12.3 us (12%)
  local copies, waits for them, and re-layouts  6.5 us (6%)
    pallas_call x5, Pallas kernels, call(): pl.pallas_call(kernel, out_shape=tuple(outs), in_specs=vmem(len(args)), o...  49.6 us
    all_to_all x1, blocking collectives, body(): lax.all_to_all(readings.reshape(devices, 1, 9 * 128), ('px', 'py'), split...  23.6 us
    ppermute x6, waiting for transfers between devices, shift(): return lax.ppermute(x, axis, [(i, (i + by) % count) for i in range(count)])  14 us
    ppermute x6, starting transfers between devices, shift(): return lax.ppermute(x, axis, [(i, (i + by) % count) for i in range(count)])  12.3 us
    unnamed x22, local copies, waits for them, and re-layouts  6.5 us
  transfers between devices with their start and end apart: 6, of which 3 were waited for; matrix products, arithmetic and copies ran while one was open for 0% of the time, Pallas kernels for 2%

profile of v2, /device:TPU:1, one launch (start us, length us, event | category | flops | bytes accessed | tf_op | source)
XLA Modules:
  0.0 106.0 jit_solution(8250653043217112937)
XLA Ops:
  0.0 0.0 copy-start
  0.0 1.2 %copy-done = f32[8,32,1024]{2,1,0:T(8,128)S(1)} copy-done((f32[8,32,1024]{2,1,0:T(8,128)S(1)}, f32[8,32,1024]{2,1,0:T(8,128)}, u32[]{:S(2)}) %copy-start) | copy-done | bytes 1048600
  1.2 0.0 copy-start.2
  1.2 1.2 %copy-done.2 = f32[8,32,1024]{2,1,0:T(8,128)S(1)} copy-done((f32[8,32,1024]{2,1,0:T(8,128)S(1)}, f32[8,32,1024]{2,1,0:T(8,128)}, u32[]{:S(2)}) %copy-start.2) | copy-done | bytes 1048600
  2.5 0.0 copy-start.4
  2.5 1.2 %copy-done.4 = f32[8,32,1024]{2,1,0:T(8,128)S(1)} copy-done((f32[8,32,1024]{2,1,0:T(8,128)S(1)}, f32[8,32,1024]{2,1,0:T(8,128)}, u32[]{:S(2)}) %copy-start.4) | copy-done | bytes 1048600
  3.7 0.0 copy-start.6
  3.7 0.7 copy-done.6
  4.4 0.0 copy-start.7
  4.4 0.7 copy-done.7
  5.1 0.0 copy-start.8
  5.1 0.7 copy-done.8
  5.8 0.0 copy-start.9
  5.8 0.7 copy-done.9
  6.5 0.0 copy-start.1
  6.5 0.0 copy-start.3
  6.5 0.0 copy-start.5
  6.5 0.8 shard_map.82
  7.3 0.0 copy-start.10
  7.3 3.0 %collective-permute-start = (f32[3200,128]{1,0:T(8,128)S(1)}, f32[3200,128]{1,0:T(8,128)S(1)}, u32[]{:S(2)}, u32[]{:S(2)}) collective-permute-start(f32[3200,128]{1,0:T(8,128)S(1)} %get-tuple-element.24), channel_id=1, source_target_pairs={{0,16},{16,32},{32,48},{48,64},{64,80},{80,96},{96,112},{112,0},{1... | collective-permute-start | bytes 4915208 | tf_op jit(solution)/shard_map/ppermute | solution.py:532
  10.3 0.0 collective-permute-start.1
  10.4 1.2 %collective-permute-start.2 = (f32[896,128]{1,0:T(8,128)S(1)}, f32[896,128]{1,0:T(8,128)S(1)}, u32[]{:S(2)}, u32[]{:S(2)}) collective-permute-start(f32[896,128]{1,0:T(8,128)S(1)} %get-tuple-element.26), channel_id=1, source_target_pairs={{0,1},{1,2},{2,3},{3,4},{4,5},{5,6},{6,7},{7,8},{8,9},{9,10},{10,1... | collective-permute-start | bytes 1376264 | tf_op jit(solution)/shard_map/ppermute | solution.py:532
  11.6 3.7 %collective-permute-start.3 = (f32[896,128]{1,0:T(8,128)S(1)}, f32[896,128]{1,0:T(8,128)S(1)}, u32[]{:S(2)}, u32[]{:S(2)}) collective-permute-start(f32[896,128]{1,0:T(8,128)S(1)} %get-tuple-element.27), channel_id=1, source_target_pairs={{0,15},{1,0},{2,1},{3,2},{4,3},{5,4},{6,5},{7,6},{8,7},{9,8},{10,9... | collective-permute-start | bytes 1376264 | tf_op jit(solution)/shard_map/ppermute | solution.py:532
  15.3 8.7 %collective-permute-done.2.py_low = f32[896,128]{1,0:T(8,128)S(1)} collective-permute-done((f32[896,128]{1,0:T(8,128)S(1)}, f32[896,128]{1,0:T(8,128)S(1)}, u32[]{:S(2)}, u32[]{:S(2)}) %collective-permute-start.2) | collective-permute-done | bytes 458784 | tf_op jit(solution)/shard_map/ppermute | solution.py:532
  24.0 0.0 collective-permute-done.3.py_high
  24.0 0.1 shard_map.84
  24.1 4.3 %collective-permute-start.4 = (f32[832,128]{1,0:T(8,128)S(1)}, f32[832,128]{1,0:T(8,128)S(1)}, u32[]{:S(2)}, u32[]{:S(2)}) collective-permute-start(f32[832,128]{1,0:T(8,128)S(1)} %get-tuple-element.28), channel_id=1, source_target_pairs={{0,16},{16,32},{32,48},{48,64},{64,80},{80,96},{96,112},{112,0},{1... | collective-permute-start | bytes 1277960 | tf_op jit(solution)/shard_map/ppermute | solution.py:532
  28.4 0.0 collective-permute-start.5
  28.4 0.0 copy-done.1
  28.4 0.0 copy-done.3
  28.4 0.0 copy-done.5
  28.4 2.2 %shard_map.83 = (f32[8,32,8,128]{3,2,1,0:T(8,128)S(1)}, f32[8,32,8,128]{3,2,1,0:T(8,128)S(1)}, f32[8,32,8,128]{3,2,1,0:T(8,128)S(1)}, bf16[1024,4096]{1,0:T(8,128)(2,1)S(1)}) custom-call(f32[2048,128]{1,0:T(8,128)S(1)} %bitcast.27, f32[2048,128]{1,0:T(8,128)S(1)} %bitcast.29, f32[2048,128]{1,0:T(8,128)S(1)} %bitcast.31, f32[16,1024]{1,0:T(8,128)S(1)} %get-tuple-element.20.meta), custom_call_target="tpu_custom_call" | custom-call | bytes 8388608 | tf_op jit(solution)/shard_map/pallas_call | solution.py:553
  30.6 0.0 copy-done.10
  30.6 2.8 %collective-permute-done.4.c_low = f32[832,128]{1,0:T(8,128)S(1)} collective-permute-done((f32[832,128]{1,0:T(8,128)S(1)}, f32[832,128]{1,0:T(8,128)S(1)}, u32[]{:S(2)}, u32[]{:S(2)}) %collective-permute-start.4) | collective-permute-done | bytes 426016 | tf_op jit(solution)/shard_map/ppermute | solution.py:532
  33.4 2.5 %collective-permute-done.5.c_high = f32[832,128]{1,0:T(8,128)S(1)} collective-permute-done((f32[832,128]{1,0:T(8,128)S(1)}, f32[832,128]{1,0:T(8,128)S(1)}, u32[]{:S(2)}, u32[]{:S(2)}) %collective-permute-start.5) | collective-permute-done | bytes 426016 | tf_op jit(solution)/shard_map/ppermute | solution.py:532
  35.9 0.0 collective-permute-done.px_low
  35.9 0.0 collective-permute-done.1.px_high
  35.9 17.2 %shard_map.85 = (f32[1152,128]{1,0:T(8,128)S(1)}, f32[16,40,8,128]{3,2,1,0:T(8,128)S(1)}, f32[16,40,8,128]{3,2,1,0:T(8,128)S(1)}, f32[16,40,8,128]{3,2,1,0:T(8,128)S(1)}) custom-call(f32[8,32,8,128]{3,2,1,0:T(8,128)S(1)} %get-tuple-element.21.permit, f32[8,32,8,128]{3,2,1,0:T(8,128)S(1)} %get-tuple-element.22.back, ...), custom_call_target="tpu_custom_call" | custom-call | tf_op jit(solution)/shard_map/pallas_call | solution.py:553
  53.2 23.6 %all_to_all.5 = f32[128,1,1152]{2,1,0:T(1,128)S(1)} all-to-all(f32[128,1,1152]{2,1,0:T(1,128)S(1)} %bitcast.33), channel_id=1, replica_groups=mesh['px'=8,'py'=16] {'px','py'}, dimensions={0} | all-to-all | bytes 1179648 | tf_op jit(solution)/shard_map/all_to_all | solution.py:608
  76.7 29.3 %shard_map.86 = f32[2048,128]{1,0:T(8,128)} custom-call(f32[1152,128]{1,0:T(8,128)S(1)} %bitcast.32, f32[3200,128]{1,0:T(8,128)S(1)} %collective-permute-done.px_low, f32[3200,128]{1,0:T(8,128)S(1)} %collective-permute-done.1.px_high, f32[896,128]{1,0:T(8,128)S(1)} %collective-permute-done.2.py_low, f32[896,128]{1,0:T(8,128)S(1)} %collective-permute-done.3.py_high, ...), custom_call_target="tpu_custom_call" | custom-call | tf_op jit(solution)/shard_map/pallas_call | solution.py:553
  (1 shorter events, 0.0 us)
Async XLA Ops:
  0.0 1.2 %copy-start = (f32[8,32,1024]{2,1,0:T(8,128)S(1)}, f32[8,32,1024]{2,1,0:T(8,128)}, u32[]{:S(2)}) copy-start(f32[8,32,1024]{2,1,0:T(8,128)} %param.10) | copy-start | bytes 3145732
  1.2 1.2 %copy-start.2 = (f32[8,32,1024]{2,1,0:T(8,128)S(1)}, f32[8,32,1024]{2,1,0:T(8,128)}, u32[]{:S(2)}) copy-start(f32[8,32,1024]{2,1,0:T(8,128)} %param.8) | copy-start | bytes 3145732
  2.5 1.2 %copy-start.4 = (f32[8,32,1024]{2,1,0:T(8,128)S(1)}, f32[8,32,1024]{2,1,0:T(8,128)}, u32[]{:S(2)}) copy-start(f32[8,32,1024]{2,1,0:T(8,128)} %param.9) | copy-start | bytes 3145732
  3.7 0.7 copy-start.6
  4.4 0.7 copy-start.7
  5.1 0.7 copy-start.8
  5.8 0.7 copy-start.9
  6.5 21.9 %copy-start.1 = (f32[8,32,1024]{2,1,0:T(8,128)S(1)}, f32[8,32,1024]{2,1,0:T(8,128)}, u32[]{:S(2)}) copy-start(f32[8,32,1024]{2,1,0:T(8,128)} %param.10) | copy-start | bytes 3145732
  6.5 21.9 %copy-start.3 = (f32[8,32,1024]{2,1,0:T(8,128)S(1)}, f32[8,32,1024]{2,1,0:T(8,128)}, u32[]{:S(2)}) copy-start(f32[8,32,1024]{2,1,0:T(8,128)} %param.8) | copy-start | bytes 3145732
  6.5 21.9 %copy-start.5 = (f32[8,32,1024]{2,1,0:T(8,128)S(1)}, f32[8,32,1024]{2,1,0:T(8,128)}, u32[]{:S(2)}) copy-start(f32[8,32,1024]{2,1,0:T(8,128)} %param.9) | copy-start | bytes 3145732
  7.3 23.3 %copy-start.10 = (f32[8]{0:T(128)S(1)}, f32[8]{0:T(128)}, u32[]{:S(2)}) copy-start(f32[8]{0:T(128)} %param.15) | copy-start | bytes 100
  7.3 28.6 %collective-permute-start = (f32[3200,128]{1,0:T(8,128)S(1)}, f32[3200,128]{1,0:T(8,128)S(1)}, u32[]{:S(2)}, u32[]{:S(2)}) collective-permute-start(f32[3200,128]{1,0:T(8,128)S(1)} %get-tuple-element.24), channel_id=1, source_target_pairs={{0,16},{16,32},{32,48},{48,64},{64,80},{80,96},{96,112},{112,0},{1... | collective-permute-start | bytes 4915208 | tf_op jit(solution)/shard_map/ppermute | solution.py:532
  10.3 25.6 %collective-permute-start.1 = (f32[3200,128]{1,0:T(8,128)S(1)}, f32[3200,128]{1,0:T(8,128)S(1)}, u32[]{:S(2)}, u32[]{:S(2)}) collective-permute-start(f32[3200,128]{1,0:T(8,128)S(1)} %get-tuple-element.25), channel_id=1, source_target_pairs={{0,112},{16,0},{32,16},{48,32},{64,48},{80,64},{96,80},{112,96},{1... | collective-permute-start | bytes 4915208 | tf_op jit(solution)/shard_map/ppermute | solution.py:532
  10.4 13.6 %collective-permute-start.2 = (f32[896,128]{1,0:T(8,128)S(1)}, f32[896,128]{1,0:T(8,128)S(1)}, u32[]{:S(2)}, u32[]{:S(2)}) collective-permute-start(f32[896,128]{1,0:T(8,128)S(1)} %get-tuple-element.26), channel_id=1, source_target_pairs={{0,1},{1,2},{2,3},{3,4},{4,5},{5,6},{6,7},{7,8},{8,9},{9,10},{10,1... | collective-permute-start | bytes 1376264 | tf_op jit(solution)/shard_map/ppermute | solution.py:532
  11.6 12.4 %collective-permute-start.3 = (f32[896,128]{1,0:T(8,128)S(1)}, f32[896,128]{1,0:T(8,128)S(1)}, u32[]{:S(2)}, u32[]{:S(2)}) collective-permute-start(f32[896,128]{1,0:T(8,128)S(1)} %get-tuple-element.27), channel_id=1, source_target_pairs={{0,15},{1,0},{2,1},{3,2},{4,3},{5,4},{6,5},{7,6},{8,7},{9,8},{10,9... | collective-permute-start | bytes 1376264 | tf_op jit(solution)/shard_map/ppermute | solution.py:532
  24.1 9.4 %collective-permute-start.4 = (f32[832,128]{1,0:T(8,128)S(1)}, f32[832,128]{1,0:T(8,128)S(1)}, u32[]{:S(2)}, u32[]{:S(2)}) collective-permute-start(f32[832,128]{1,0:T(8,128)S(1)} %get-tuple-element.28), channel_id=1, source_target_pairs={{0,16},{16,32},{32,48},{48,64},{64,80},{80,96},{96,112},{112,0},{1... | collective-permute-start | bytes 1277960 | tf_op jit(solution)/shard_map/ppermute | solution.py:532
  28.4 7.6 %collective-permute-start.5 = (f32[832,128]{1,0:T(8,128)S(1)}, f32[832,128]{1,0:T(8,128)S(1)}, u32[]{:S(2)}, u32[]{:S(2)}) collective-permute-start(f32[832,128]{1,0:T(8,128)S(1)} %get-tuple-element.29), channel_id=1, source_target_pairs={{0,112},{16,0},{32,16},{48,32},{64,48},{80,64},{96,80},{112,96},{1... | collective-permute-start | bytes 1277960 | tf_op jit(solution)/shard_map/ppermute | solution.py:532

commit v3 on v2

--- a/solution.py
+++ b/solution.py
@@ -17,11 +17,15 @@
 D = 4
 EX, EY = CX + 2 * D, CY + 2 * D
 ROWS = CX * CY * 8
-HALO_X = D * CY * 8
+PLANE = CY * 8
+PX_AT = (0, D * PLANE, (2 * D - 1) * PLANE)
+PX_FLUX = (3 * D - 2) * PLANE
+PX_META = (3 * D - 1) * PLANE
 HALO_Y = CX * D * 8
-DC = 3
-HALO_C = DC * D * 8
-META = 128
+CELLS = tuple((dx, dy) for dx in range(1, D) for dy in range(1, D) if dx + dy <= D)
+HALO_C = len(CELLS) * 8
+META = 80
+PART = 3 * HALO_C + META
 F32 = jnp.float32
 BF16 = jnp.bfloat16
 
@@ -99,18 +103,30 @@
     px_low, px_high, py_low, py_high, c_low, c_high = sides
     middle_x, middle_y = slice(D, D + CX), slice(D, D + CY)
     out[middle_x, middle_y] = own[...]
-    for ref, at in ((px_low, 0), (px_high, D + CX)):
-        v = ref[field * HALO_X : (field + 1) * HALO_X, :]
-        out[at : at + D, middle_y] = v.reshape(D, CY, 8, 128) * scale
+    planes = D if field == 0 else D - 1
+    for ref, at in ((px_low, D - planes), (px_high, D + CX)):
+        v = ref[PX_AT[field] : PX_AT[field] + planes * PLANE, :]
+        out[at : at + planes, middle_y] = v.reshape(planes, CY, 8, 128) * scale
     for ref, at in ((py_low, 0), (py_high, D + CY)):
         v = ref[field * HALO_Y : (field + 1) * HALO_Y, :]
         out[middle_x, at : at + D] = v.reshape(CX, D, 8, 128) * scale
-    part = 3 * HALO_C + META
-    for ref, at, gap in ((c_low, 1, 0), (c_high, D + CX, D + CX + DC)):
-        for side, to in ((0, 0), (1, D + CY)):
-            out[gap, to : to + D] = jnp.zeros((D, 8, 128), F32)
-            v = ref[side * part + field * HALO_C : side * part + (field + 1) * HALO_C, :]
-            out[at : at + DC, to : to + D] = v.reshape(DC, D, 8, 128) * scale
+    blank = jnp.zeros((D, D, 8, 128), F32)
+    for x, ref in ((0, c_low), (D + CX, c_high)):
+        for side, y in enumerate((0, D + CY)):
+            out[x : x + D, y : y + D] = blank
+            for i, (dx, dy) in enumerate(CELLS):
+                at = side * PART + field * HALO_C + i * 8
+                cell_x = x + D - dx if x == 0 else x + dx - 1
+                cell_y = y + D - dy if y == 0 else y + dy - 1
+                out[cell_x, cell_y] = ref[at : at + 8, :] * scale
+
+
+def far_planes(sides, bg, qp):
+    middle_y = slice(D, D + CY)
+    for ref, at, beside in ((sides[0], 0, 1), (sides[1], EX - 1, EX - 2)):
+        flux = ref[PX_FLUX : PX_FLUX + PLANE, :].reshape(CY, 8, 128)
+        bg[at, middle_y] = bg[beside, middle_y] + flux
+        qp[at, middle_y] = 1.0 - qp[beside, middle_y]
 
 
 def close_edges(out, sign):
@@ -135,11 +151,12 @@
 
 
 def take_meta(ref, base, out):
-    for half in range(2):
-        for c in range(8):
-            out[half * 8 : half * 8 + 8, c * 128 : (c + 1) * 128] = ref[
-                pl.ds(base + half * 64 + c * 8, 8), :
-            ]
+    for c in range(8):
+        lanes = slice(c * 128, (c + 1) * 128)
+        out[0:8, lanes] = ref[base + c * 8 : base + c * 8 + 8, :]
+        for i in range(2):
+            at = base + 64 + i * 8 + c
+            out[8 + i : 9 + i, lanes] = ref[at : at + 1, :]
 
 
 def two_parts(v):
@@ -191,6 +208,7 @@
     extend(0, permit, sides, q, 0.5 / HALF)
     extend(1, back, sides, bg, 1.0)
     extend(2, perturb, sides, qp, 0.5)
+    far_planes(sides, bg, qp)
     close_edges(q, -1.0)
     close_edges(qp, -1.0)
     close_edges(bg, 1.0)
@@ -352,7 +370,7 @@
     scatter(meta, values, lambda n: n >> 10, column, CX * CY, 4, lhs, put_planes(D, CX), hot)
 
     for ref, x0, first in ((px_low, 0, CX - D), (px_high, D + CX, 0)):
-        take_meta(ref, 3 * HALO_X, near)
+        take_meta(ref, PX_META, near)
         returned(near)
         scatter(
             near,
@@ -381,10 +399,9 @@
             near, values, strip(0, CX, first), low_column, 4 * CX * D, 1, lhs, put_strip(D, CX, y0)
         )
 
-    part = 3 * HALO_C + META
     for ref, x0, first_x in ((c_low, 0, CX - D), (c_high, D + CX, 0)):
         for side, y0, first_y in ((0, 0, CY - D), (1, D + CY, 0)):
-            take_meta(ref, side * part + 3 * HALO_C, near)
+            take_meta(ref, side * PART + 3 * HALO_C, near)
             returned(near)
             scatter(
                 near,
@@ -448,51 +465,102 @@
     return ref[pl.ds((x * (CY // 8) + y // 8) * 64 + y % 8, 8, stride=8), :]
 
 
+def line_of(ref, x, y):
+    return ref[pl.ds((x * (CY // 8) + y // 8) * 64 + y % 8, 8, stride=8), :]
+
+
 def pack_kernel(
-    permit,
-    back,
-    perturb,
-    nodes,
-    probe_weights,
-    owner,
-    sensor,
+    permit_hbm,
+    back_hbm,
+    perturb_hbm,
+    nodes_hbm,
+    weights_hbm,
+    owner_hbm,
+    sensor_hbm,
     low_x,
     high_x,
     low_y,
     high_y,
     meta,
+    permit,
+    back,
+    perturb,
+    nodes,
+    weights,
+    owner,
+    sensor,
+    sems,
 ):
+    pairs = (
+        (nodes_hbm, nodes),
+        (weights_hbm, weights),
+        (owner_hbm, owner),
+        (sensor_hbm, sensor),
+        (permit_hbm, permit),
+        (back_hbm, back),
+        (perturb_hbm, perturb),
+    )
+    copies = [pltpu.make_async_copy(a, b, sems.at[i]) for i, (a, b) in enumerate(pairs)]
+    for copy in copies:
+        copy.start()
+    for copy in copies[:4]:
+        copy.wait()
     meta[0:4, :] = nodes[...].astype(F32)
-    meta[4:8, :] = probe_weights[...]
+    meta[4:8, :] = weights[...]
     meta[8:9, :] = owner[...].astype(F32)
     meta[9:10, :] = sensor[...].astype(F32)
     meta[10:16, :] = jnp.zeros((6, 1024), F32)
+    for out, at in ((low_x, PX_META), (high_x, PX_META), (low_y, 3 * HALO_Y), (high_y, 3 * HALO_Y)):
+        for c in range(8):
+            lanes = slice(c * 128, (c + 1) * 128)
+            out[at + c * 8 : at + c * 8 + 8, :] = meta[0:8, lanes]
+            for i in range(2):
+                out[at + 64 + i * 8 + c : at + 65 + i * 8 + c, :] = meta[8 + i : 9 + i, lanes]
+
     for field, ref in enumerate((permit, back, perturb)):
-
-        def plane(x, carry, field=field, ref=ref):
+        copies[4 + field].wait()
+        planes = D if field == 0 else D - 1
+
+        def plane(x, carry, field=field, ref=ref, planes=planes):
             for y in range(CY):
-                at = pl.ds(field * HALO_X + (x * CY + y) * 8, 8)
+                at = pl.ds(PX_AT[field] + (x * CY + y) * 8, 8)
                 low_x[at, :] = row_of(ref, x, y)
-                high_x[at, :] = row_of(ref, x + CX - D, y)
+                high_x[at, :] = row_of(ref, x + CX - planes, y)
             return carry
 
-        lax.fori_loop(0, D, plane, 0)
+        lax.fori_loop(0, planes, plane, 0)
         for x in range(CX):
             for y in range(D):
                 at = pl.ds(field * HALO_Y + (x * D + y) * 8, 8)
                 low_y[at, :] = row_of(ref, x, y)
                 high_y[at, :] = row_of(ref, x, y + CY - D)
-    for half in range(2):
-        for c in range(8):
-            v = meta[half * 8 : half * 8 + 8, c * 128 : (c + 1) * 128]
-            at = half * 64 + c * 8
-            low_x[3 * HALO_X + at : 3 * HALO_X + at + 8, :] = v
-            high_x[3 * HALO_X + at : 3 * HALO_X + at + 8, :] = v
-            low_y[3 * HALO_Y + at : 3 * HALO_Y + at + 8, :] = v
-            high_y[3 * HALO_Y + at : 3 * HALO_Y + at + 8, :] = v
-
-
-def own_kernel(permit, back, perturb, meta, q, bg, qp, hot):
+
+    def flux(y, carry):
+        for out, near, far in ((low_x, D - 2, D - 1), (high_x, CX - D + 1, CX - D)):
+            face = 0.5 * (line_of(perturb, near, y) + line_of(perturb, far, y))
+            at = pl.ds(pl.multiple_of(PX_FLUX + y * 8, 8), 8)
+            out[at, :] = face * (line_of(back, far, y) - line_of(back, near, y))
+        return carry
+
+    lax.fori_loop(0, CY, flux, 0)
+
+
+def own_kernel(permit_hbm, back_hbm, perturb_hbm, meta, q, bg, qp, hot, permit, back, perturb, sems):
+    pairs = ((permit_hbm, permit), (back_hbm, back), (perturb_hbm, perturb))
+    copies = [pltpu.make_async_copy(a, b, sems.at[i]) for i, (a, b) in enumerate(pairs)]
+    for copy in copies:
+        copy.start()
+
+    def entries(i, carry):
+        k, lanes = i // 2, pl.ds(pl.multiple_of((i % 2) * 512, 512), 512)
+        node = meta[pl.ds(k, 1), lanes].astype(jnp.int32)
+        hot[:, pl.ds(pl.multiple_of(i * 512, 512), 512)] = one_hot(node & (CZ - 1), CZ)
+        return carry
+
+    lax.fori_loop(0, 8, entries, 0)
+    for copy in copies:
+        copy.wait()
+
     def plane(x, carry):
         for y in range(CY):
             q[x, y] = row_of(permit, x, y) * (0.5 / HALF)
@@ -502,23 +570,17 @@
 
     lax.fori_loop(0, CX, plane, 0)
 
-    def entries(i, carry):
-        k, lanes = i // 2, pl.ds(pl.multiple_of((i % 2) * 512, 512), 512)
-        node = meta[pl.ds(k, 1), lanes].astype(jnp.int32)
-        hot[:, pl.ds(pl.multiple_of(i * 512, 512), 512)] = one_hot(node & (CZ - 1), CZ)
-        return carry
-
-    lax.fori_loop(0, 8, entries, 0)
-
 
 def corner_kernel(py_low, py_high, low, high):
-    part = 3 * HALO_C + META
     for side, ref in enumerate((py_low, py_high)):
         for field in range(3):
-            at, first = side * part + field * HALO_C, field * HALO_Y
-            low[at : at + HALO_C, :] = ref[first : first + HALO_C, :]
-            high[at : at + HALO_C, :] = ref[first + HALO_Y - HALO_C : first + HALO_Y, :]
-        at = side * part + 3 * HALO_C
+            for i, (dx, dy) in enumerate(CELLS):
+                y = D - dy if side == 0 else dy - 1
+                at = side * PART + field * HALO_C + i * 8
+                for out, x in ((low, dx - 1), (high, CX - dx)):
+                    first = field * HALO_Y + (x * D + y) * 8
+                    out[at : at + 8, :] = ref[first : first + 8, :]
+        at = side * PART + 3 * HALO_C
         low[at : at + META, :] = ref[3 * HALO_Y :, :]
         high[at : at + META, :] = ref[3 * HALO_Y :, :]
 
@@ -549,11 +611,13 @@
     def rows(*counts):
         return [jax.ShapeDtypeStruct((n, 128), F32) for n in counts]
 
-    def call(kernel, outs, *args, scratch=(), limit, bytes_accessed=0):
+    def call(kernel, outs, *args, hbm=0, scratch=(), limit, bytes_accessed=0):
+        held = [pltpu.with_memory_space_constraint(a, pltpu.HBM) for a in args[:hbm]]
+        args = held + list(args[hbm:])
         return pl.pallas_call(
             kernel,
             out_shape=tuple(outs),
-            in_specs=vmem(len(args)),
+            in_specs=[pl.BlockSpec(memory_space=pltpu.HBM)] * hbm + vmem(len(args) - hbm),
             out_specs=tuple(vmem(len(outs))),
             scratch_shapes=scratch,
             compiler_params=pltpu.CompilerParams(vmem_limit_bytes=limit * 2**20),
@@ -562,7 +626,8 @@
             ),
         )(*args)
 
-    size_x, size_y, size_c = 3 * HALO_X + META, 3 * HALO_Y + META, 2 * (3 * HALO_C + META)
+    size_x, size_y, size_c = PX_META + META, 3 * HALO_Y + META, 2 * PART
+    raw = [pltpu.VMEM((ROWS, 128), F32)] * 3
     table = jax.ShapeDtypeStruct((16, 1024), F32)
     low_x, high_x, low_y, high_y, meta = call(
         pack_kernel,
@@ -572,7 +637,16 @@
         probe_weights,
         probe_owner.reshape(1, -1),
         probe_sensor.reshape(1, -1),
-        limit=4,
+        hbm=7,
+        scratch=raw
+        + [
+            pltpu.VMEM((4, 1024), jnp.int32),
+            pltpu.VMEM((4, 1024), F32),
+            pltpu.VMEM((1, 1024), jnp.int32),
+            pltpu.VMEM((1, 1024), jnp.int32),
+            pltpu.SemaphoreType.DMA((7,)),
+        ],
+        limit=6,
     )
     px_low, px_high = shift(high_x, "px", 1), shift(low_x, "px", -1)
     py_low, py_high = shift(high_y, "py", 1), shift(low_y, "py", -1)
@@ -583,7 +657,9 @@
         [compact] * 3 + [jax.ShapeDtypeStruct((CZ, 4096), BF16)],
         *fields,
         meta,
-        limit=8,
+        hbm=3,
+        scratch=raw + [pltpu.SemaphoreType.DMA((3,))],
+        limit=10,
         bytes_accessed=8 * 2**20,
     )
     low_c, high_c = call(corner_kernel, rows(size_c, size_c), py_low, py_high, limit=4)

time: 106 us -> 98.9 us (0.933)
  local copies, waits for them, and re-layouts: 6.5 us -> 0.01 us
  Pallas kernels: 49.6 us -> 52.9 us
  waiting for transfers between devices: 14 us -> 11 us
  blocking collectives: 23.6 us -> 22.5 us
    unnamed x22 -> x2, local copies, waits for them, and re-layouts: 6.5 us -> 0.01 us
    pallas_call x5, Pallas kernels: 49.6 us -> 52.9 us  [call(): pl.pallas_call(kernel, out_shape=tuple(outs), in_specs=[pl.BlockSpec(memo...]
    ppermute x6, waiting for transfers between devices: 14 us -> 11 us  [shift(): return lax.ppermute(x, axis, [(i, (i + by) % count) for i in range(count)])]
    all_to_all x1, blocking collectives: 23.6 us -> 22.5 us  [body(): lax.all_to_all(readings.reshape(devices, 1, 9 * 128), ('px', 'py'), split...]
  transfers between devices with their start and end apart: 6 -> 6, of which waited for: 3 -> 3; matrix products, arithmetic and copies ran while one was open for 0% -> 0% of each run, Pallas kernels for 2% -> 3%
where the time goes in v3:
time: 98.9 us; the launch traced here: 98.7 us
  Pallas kernels  52.9 us (53%)
  blocking collectives  22.5 us (23%)
  starting transfers between devices  12.3 us (12%)
  waiting for transfers between devices  11 us (11%)
    pallas_call x5, Pallas kernels, call(): pl.pallas_call(kernel, out_shape=tuple(outs), in_specs=[pl.BlockSpec(memo...  52.9 us
    all_to_all x1, blocking collectives, body(): lax.all_to_all(readings.reshape(devices, 1, 9 * 128), ('px', 'py'), split...  22.5 us
    ppermute x6, starting transfers between devices, shift(): return lax.ppermute(x, axis, [(i, (i + by) % count) for i in range(count)])  12.3 us
    ppermute x6, waiting for transfers between devices, shift(): return lax.ppermute(x, axis, [(i, (i + by) % count) for i in range(count)])  11 us
  transfers between devices with their start and end apart: 6, of which 3 were waited for; matrix products, arithmetic and copies ran while one was open for 0% of the time, Pallas kernels for 3%

profile of v3, /device:TPU:1, one launch (start us, length us, event | category | flops | bytes accessed | tf_op | source)
XLA Modules:
  0.0 98.7 jit_solution(17379476613381058052)
XLA Ops:
  0.0 2.8 %shard_map.82 = (f32[2896,128]{1,0:T(8,128)S(1)}, f32[2896,128]{1,0:T(8,128)S(1)}, f32[848,128]{1,0:T(8,128)S(1)}, f32[848,128]{1,0:T(8,128)S(1)}, f32[16,1024]{1,0:T(8,128)S(1)}) custom-call(f32[2048,128]{1,0:T(8,128)} %bitcast.28, f32[2048,128]{1,0:T(8,128)} %bitcast.30, f32[2048,128]{1,0:T(8,128)} %bitcast.32, s32[4,1024]{1,0:T(4,128)} %nodes_hbm.1, ...), custom_call_target="tpu_custom_call" | custom-call | tf_op jit(solution)/shard_map/pallas_call | solution.py:617
  2.8 0.0 copy-start
  2.8 3.0 %collective-permute-start = (f32[2896,128]{1,0:T(8,128)S(1)}, f32[2896,128]{1,0:T(8,128)S(1)}, u32[]{:S(2)}, u32[]{:S(2)}) collective-permute-start(f32[2896,128]{1,0:T(8,128)S(1)} %get-tuple-element.24), channel_id=1, source_target_pairs={{0,16},{16,32},{32,48},{48,64},{64,80},{80,96},{96,112},{112,0},{1... | collective-permute-start | bytes 4448264 | tf_op jit(solution)/shard_map/ppermute | solution.py:594
  5.9 0.0 collective-permute-start.1
  5.9 1.2 %collective-permute-start.2 = (f32[848,128]{1,0:T(8,128)S(1)}, f32[848,128]{1,0:T(8,128)S(1)}, u32[]{:S(2)}, u32[]{:S(2)}) collective-permute-start(f32[848,128]{1,0:T(8,128)S(1)} %get-tuple-element.26), channel_id=1, source_target_pairs={{0,1},{1,2},{2,3},{3,4},{4,5},{5,6},{6,7},{7,8},{8,9},{9,10},{10,1... | collective-permute-start | bytes 1302536 | tf_op jit(solution)/shard_map/ppermute | solution.py:594
  7.1 3.7 %collective-permute-start.3 = (f32[848,128]{1,0:T(8,128)S(1)}, f32[848,128]{1,0:T(8,128)S(1)}, u32[]{:S(2)}, u32[]{:S(2)}) collective-permute-start(f32[848,128]{1,0:T(8,128)S(1)} %get-tuple-element.27), channel_id=1, source_target_pairs={{0,15},{1,0},{2,1},{3,2},{4,3},{5,4},{6,5},{7,6},{8,7},{9,8},{10,9... | collective-permute-start | bytes 1302536 | tf_op jit(solution)/shard_map/ppermute | solution.py:594
  10.8 8.2 %collective-permute-done.2.py_low = f32[848,128]{1,0:T(8,128)S(1)} collective-permute-done((f32[848,128]{1,0:T(8,128)S(1)}, f32[848,128]{1,0:T(8,128)S(1)}, u32[]{:S(2)}, u32[]{:S(2)}) %collective-permute-start.2) | collective-permute-done | bytes 434208 | tf_op jit(solution)/shard_map/ppermute | solution.py:594
  19.0 0.0 collective-permute-done.3.py_high
  19.0 4.3 %collective-permute-start.4 = (f32[448,128]{1,0:T(8,128)S(1)}, f32[448,128]{1,0:T(8,128)S(1)}, u32[]{:S(2)}, u32[]{:S(2)}) collective-permute-start(f32[448,128]{1,0:T(8,128)S(1)} %get-tuple-element.28), channel_id=1, source_target_pairs={{0,16},{16,32},{32,48},{48,64},{64,80},{80,96},{96,112},{112,0},{1... | collective-permute-start | bytes 688136 | tf_op jit(solution)/shard_map/ppermute | solution.py:594
  23.3 0.0 collective-permute-start.5
  23.3 2.6 %shard_map.83 = (f32[8,32,8,128]{3,2,1,0:T(8,128)S(1)}, f32[8,32,8,128]{3,2,1,0:T(8,128)S(1)}, f32[8,32,8,128]{3,2,1,0:T(8,128)S(1)}, bf16[1024,4096]{1,0:T(8,128)(2,1)S(1)}) custom-call(f32[2048,128]{1,0:T(8,128)} %bitcast.29, f32[2048,128]{1,0:T(8,128)} %bitcast.31, f32[2048,128]{1,0:T(8,128)} %bitcast.33, f32[16,1024]{1,0:T(8,128)S(1)} %get-tuple-element.20.meta), custom_call_target="tpu_custom_call" | custom-call | bytes 8388608 | tf_op jit(solution)/shard_map/pallas_call | solution.py:617
  25.9 0.0 copy-done
  25.9 0.4 collective-permute-done.4.c_low
  26.3 2.5 %collective-permute-done.5.c_high = f32[448,128]{1,0:T(8,128)S(1)} collective-permute-done((f32[448,128]{1,0:T(8,128)S(1)}, f32[448,128]{1,0:T(8,128)S(1)}, u32[]{:S(2)}, u32[]{:S(2)}) %collective-permute-start.5) | collective-permute-done | bytes 229408 | tf_op jit(solution)/shard_map/ppermute | solution.py:594
  28.8 0.0 collective-permute-done.px_low
  28.8 0.0 collective-permute-done.1.px_high
  28.8 17.7 %shard_map.85 = (f32[1152,128]{1,0:T(8,128)S(1)}, f32[16,40,8,128]{3,2,1,0:T(8,128)S(1)}, f32[16,40,8,128]{3,2,1,0:T(8,128)S(1)}, f32[16,40,8,128]{3,2,1,0:T(8,128)S(1)}) custom-call(f32[8,32,8,128]{3,2,1,0:T(8,128)S(1)} %get-tuple-element.21.permit, f32[8,32,8,128]{3,2,1,0:T(8,128)S(1)} %get-tuple-element.22.back, ...), custom_call_target="tpu_custom_call" | custom-call | tf_op jit(solution)/shard_map/pallas_call | solution.py:617
  46.5 22.5 %all_to_all.5 = f32[128,1,1152]{2,1,0:T(1,128)S(1)} all-to-all(f32[128,1,1152]{2,1,0:T(1,128)S(1)} %bitcast.27), channel_id=1, replica_groups=mesh['px'=8,'py'=16] {'px','py'}, dimensions={0} | all-to-all | bytes 1179648 | tf_op jit(solution)/shard_map/all_to_all | solution.py:684
  68.9 29.8 %shard_map.86 = f32[2048,128]{1,0:T(8,128)} custom-call(f32[1152,128]{1,0:T(8,128)S(1)} %bitcast.26, f32[2896,128]{1,0:T(8,128)S(1)} %collective-permute-done.px_low, f32[2896,128]{1,0:T(8,128)S(1)} %collective-permute-done.1.px_high, f32[848,128]{1,0:T(8,128)S(1)} %collective-permute-done.2.py_low, f32[848,128]{1,0:T(8,128)S(1)} %collective-permute-done.3.py_high, ...), custom_call_target="tpu_custom_call" | custom-call | tf_op jit(solution)/shard_map/pallas_call | solution.py:617
  (2 shorter events, 0.0 us)
Async XLA Ops:
  2.8 23.1 %copy-start = (f32[8]{0:T(128)S(1)}, f32[8]{0:T(128)}, u32[]{:S(2)}) copy-start(f32[8]{0:T(128)} %param.15) | copy-start | bytes 100
  2.8 25.9 %collective-permute-start = (f32[2896,128]{1,0:T(8,128)S(1)}, f32[2896,128]{1,0:T(8,128)S(1)}, u32[]{:S(2)}, u32[]{:S(2)}) collective-permute-start(f32[2896,128]{1,0:T(8,128)S(1)} %get-tuple-element.24), channel_id=1, source_target_pairs={{0,16},{16,32},{32,48},{48,64},{64,80},{80,96},{96,112},{112,0},{1... | collective-permute-start | bytes 4448264 | tf_op jit(solution)/shard_map/ppermute | solution.py:594
  5.9 22.9 %collective-permute-start.1 = (f32[2896,128]{1,0:T(8,128)S(1)}, f32[2896,128]{1,0:T(8,128)S(1)}, u32[]{:S(2)}, u32[]{:S(2)}) collective-permute-start(f32[2896,128]{1,0:T(8,128)S(1)} %get-tuple-element.25), channel_id=1, source_target_pairs={{0,112},{16,0},{32,16},{48,32},{64,48},{80,64},{96,80},{112,96},{1... | collective-permute-start | bytes 4448264 | tf_op jit(solution)/shard_map/ppermute | solution.py:594
  5.9 13.1 %collective-permute-start.2 = (f32[848,128]{1,0:T(8,128)S(1)}, f32[848,128]{1,0:T(8,128)S(1)}, u32[]{:S(2)}, u32[]{:S(2)}) collective-permute-start(f32[848,128]{1,0:T(8,128)S(1)} %get-tuple-element.26), channel_id=1, source_target_pairs={{0,1},{1,2},{2,3},{3,4},{4,5},{5,6},{6,7},{7,8},{8,9},{9,10},{10,1... | collective-permute-start | bytes 1302536 | tf_op jit(solution)/shard_map/ppermute | solution.py:594
  7.1 11.9 %collective-permute-start.3 = (f32[848,128]{1,0:T(8,128)S(1)}, f32[848,128]{1,0:T(8,128)S(1)}, u32[]{:S(2)}, u32[]{:S(2)}) collective-permute-start(f32[848,128]{1,0:T(8,128)S(1)} %get-tuple-element.27), channel_id=1, source_target_pairs={{0,15},{1,0},{2,1},{3,2},{4,3},{5,4},{6,5},{7,6},{8,7},{9,8},{10,9... | collective-permute-start | bytes 1302536 | tf_op jit(solution)/shard_map/ppermute | solution.py:594
  19.0 7.3 %collective-permute-start.4 = (f32[448,128]{1,0:T(8,128)S(1)}, f32[448,128]{1,0:T(8,128)S(1)}, u32[]{:S(2)}, u32[]{:S(2)}) collective-permute-start(f32[448,128]{1,0:T(8,128)S(1)} %get-tuple-element.28), channel_id=1, source_target_pairs={{0,16},{16,32},{32,48},{48,64},{64,80},{80,96},{96,112},{112,0},{1... | collective-permute-start | bytes 688136 | tf_op jit(solution)/shard_map/ppermute | solution.py:594
  23.3 5.4 %collective-permute-start.5 = (f32[448,128]{1,0:T(8,128)S(1)}, f32[448,128]{1,0:T(8,128)S(1)}, u32[]{:S(2)}, u32[]{:S(2)}) collective-permute-start(f32[448,128]{1,0:T(8,128)S(1)} %get-tuple-element.29), channel_id=1, source_target_pairs={{0,112},{16,0},{32,16},{48,32},{64,48},{80,64},{96,80},{112,96},{1... | collective-permute-start | bytes 688136 | tf_op jit(solution)/shard_map/ppermute | solution.py:594

commit v4 on v3

--- a/solution.py
+++ b/solution.py
@@ -72,15 +72,24 @@
     return jnp.where(last, 0.0, q + z_up(q))
 
 
-def fluxes(src, q, cz, x, y, n):
+def side_fluxes(src, q, x, y, n):
     fe, qe = src[x, pl.ds(y - 1, n + 2)], q[x, pl.ds(y - 1, n + 2)]
     f, qc = fe[1:-1], qe[1:-1]
     fy = (fe[1:] - fe[:-1]) * (qe[1:] + qe[:-1])
     acc = fy[1:] - fy[:-1]
     acc += (src[x + 1, pl.ds(y, n)] - f) * (q[x + 1, pl.ds(y, n)] + qc)
     acc += (src[x - 1, pl.ds(y, n)] - f) * (q[x - 1, pl.ds(y, n)] + qc)
-    fz = (z_up(f) - f) * (z_face(qc) if cz is None else cz[x, pl.ds(y, n)])
-    return f, acc + (fz - z_down(fz))
+    return f, acc
+
+
+def z_fluxes(f, faces):
+    fz = (z_up(f) - f) * faces
+    return fz - z_down(fz)
+
+
+def fluxes(src, q, cz, x, y, n):
+    f, acc = side_fluxes(src, q, x, y, n)
+    return f, acc + z_fluxes(f, cz[x, pl.ds(y, n)])
 
 
 def cover(low, high, n):
@@ -176,6 +185,20 @@
     return jnp.where(at == index, 1.0, 0.0).astype(BF16)
 
 
+def rows16(index):
+    shape = (16, index.shape[1])
+    numbers = lax.broadcasted_iota(jnp.int32, shape, 0).astype(jnp.int16)
+    return jnp.broadcast_to(index, shape).astype(jnp.int16), numbers
+
+
+def put_one_hot(index, count, out, first, lanes):
+    wanted, numbers = rows16(index)
+    one, zero = jnp.ones(wanted.shape, BF16), jnp.zeros(wanted.shape, BF16)
+    for r in range(count // 16):
+        hit = numbers + jnp.int16(r * 16) == wanted
+        out[first + r * 16 : first + (r + 1) * 16, lanes] = jnp.where(hit, one, zero)
+
+
 def dot(a, b, over):
     return lax.dot_general(a, b, (over, ((), ())), preferred_element_type=F32)
 
@@ -184,6 +207,8 @@
     permit,
     back,
     perturb,
+    own_cz,
+    own_bz,
     px_low,
     px_high,
     py_low,
@@ -213,10 +238,29 @@
     close_edges(qp, -1.0)
     close_edges(bg, 1.0)
 
-    def first(x, y, n):
-        _, acc = fluxes(bg, qp, None, x, y, n)
-        b[x, pl.ds(y, n)] = acc
+    cz[D : D + CX, D : D + CY] = own_cz[...]
+
+    def outer(x, y, n):
+        f, acc = side_fluxes(bg, qp, x, y, n)
+        b[x, pl.ds(y, n)] = acc + z_fluxes(f, z_face(qp[x, pl.ds(y, n)]))
         cz[x, pl.ds(y, n)] = z_face(q[x, pl.ds(y, n)])
+
+    def outer_planes(i, carry):
+        for x in (1 + i, D + CX + i):
+            for y in cover(1, EY - 1, 4):
+                outer(x, y, 4)
+        return carry
+
+    def own_planes(x, carry):
+        outer(x, 1, D - 1)
+        outer(x, D + CY, D - 1)
+        for y in cover(D, D + CY, 4):
+            _, acc = side_fluxes(bg, qp, x, y, 4)
+            b[x, pl.ds(y, 4)] = acc + own_bz[x - D, pl.ds(y - D, 4)]
+        return carry
+
+    lax.fori_loop(0, D - 1, outer_planes, 0)
+    lax.fori_loop(D, D + CX, own_planes, 0)
 
     def second(x, y, n):
         f, acc = fluxes(b, q, cz, x, y, n)
@@ -230,7 +274,6 @@
         f, acc = fluxes(y2, q, cz, x, y, n)
         y1[x, pl.ds(y, n)] = A0 * b[x, pl.ds(y, n)] - f - acc
 
-    sweep(1, 4, first)
     sweep(2, 4, second)
     sweep(3, 4, third)
     sweep(4, 4, fourth)
@@ -269,24 +312,23 @@
         out[i * 72 : (i + 1) * 72, :] = block
 
 
-def scatter(meta, values, rows, cols, per, tiles, lhs, keep, hot=None):
+def scatter(meta, values, rows, per, tiles, lhs, keep, hot):
     for k in range(4):
-        node = meta[k : k + 1, :].astype(jnp.int32)
-        high, low = two_parts(values[k : k + 1, :])
-        hit = lax.broadcasted_iota(jnp.int32, (per, 1024), 0) == rows(node)
+        wanted, numbers = rows16(rows(meta[k : k + 1, :].astype(jnp.int32)))
+        value = jnp.broadcast_to(values[k : k + 1, :], wanted.shape)
+        high, low = two_parts(value)
+        zero = jnp.zeros(wanted.shape, BF16)
         lanes = slice(k * 1024, (k + 1) * 1024)
-        lhs[0:per, lanes] = jnp.where(hit, high.astype(F32), 0.0).astype(BF16)
-        lhs[per : 2 * per, lanes] = jnp.where(hit, low.astype(F32), 0.0).astype(BF16)
+        for r in range(per // 16):
+            hit = numbers + jnp.int16(r * 16) == wanted
+            lhs[r * 16 : (r + 1) * 16, lanes] = jnp.where(hit, high, zero)
+            lhs[per + r * 16 : per + (r + 1) * 16, lanes] = jnp.where(hit, low, zero)
 
     def tile(t, carry):
         total = None
         for k in range(4):
             lanes = slice(k * 1024, (k + 1) * 1024)
-            if hot is None:
-                node = meta[k : k + 1, :].astype(jnp.int32)
-                hits = one_hot(cols(node) - t * 256, 256)
-            else:
-                hits = hot[pl.ds(pl.multiple_of(t * 256, 256), 256), lanes]
+            hits = hot[pl.ds(pl.multiple_of(t * 256, 256), 256), lanes]
             part = dot(lhs[0 : 2 * per, lanes], hits, ((1,), (1,)))
             total = part if total is None else total + part
         keep(t, total[0:per] + total[per : 2 * per])
@@ -316,6 +358,7 @@
     y1,
     y2,
     lhs,
+    near_hot,
     near,
     values,
 ):
@@ -335,84 +378,67 @@
 
     flat = src.reshape(EX * EY * 8, 128)
 
-    def xy(node):
-        return node >> 15, (node >> 10) & (CY - 1)
-
-    def put_planes(x0, planes):
+    def put_planes(x0, planes, tiles):
         def keep(t, sums):
-            for x in range(planes):
-                for half in range(2):
-                    flat[pl.ds(((x + x0) * EY + D) * 8 + t * 2 + half, CY, stride=8), :] = sums[
-                        x * CY : (x + 1) * CY, half * 128 : (half + 1) * 128
-                    ]
+            for zq in range(4 // tiles):
+                for x in range(planes):
+                    first = (zq * planes + x) * CY
+                    for half in range(2):
+                        c = zq * tiles * 2 + t * 2 + half
+                        flat[pl.ds(((x + x0) * EY + D) * 8 + c, CY, stride=8), :] = sums[
+                            first : first + CY, half * 128 : (half + 1) * 128
+                        ]
 
         return keep
 
     def put_strip(x0, planes, y0):
         def keep(t, sums):
             for zq in range(4):
-                for x in range(0, planes):
-                    block = sums[zq * planes * D + x * D : zq * planes * D + (x + 1) * D]
+                for x in range(planes):
+                    first = (zq * planes + x) * D
                     for half in range(2):
                         flat[
                             pl.ds(((x + x0) * EY + y0) * 8 + zq * 2 + half, D, stride=8), :
-                        ] = block[:, half * 128 : (half + 1) * 128]
+                        ] = sums[first : first + D, half * 128 : (half + 1) * 128]
 
         return keep
 
-    def column(node):
-        return node & (CZ - 1)
-
-    def low_column(node):
-        return node & 255
+    def box(first_x, planes, first_y, lines, bits):
+        def rows(node):
+            x, y = (node >> 15) - first_x, ((node >> 10) & (CY - 1)) - first_y
+            good = (x >= 0) & (x < planes) & (y >= 0) & (y < lines)
+            z = (node & (CZ - 1)) >> bits
+            return jnp.where(good, (z * planes + x) * lines + y, -1)
+
+        return rows
 
     returned(meta)
-    scatter(meta, values, lambda n: n >> 10, column, CX * CY, 4, lhs, put_planes(D, CX), hot)
-
-    for ref, x0, first in ((px_low, 0, CX - D), (px_high, D + CX, 0)):
+    scatter(meta, values, lambda n: n >> 10, CX * CY, 4, lhs, put_planes(D, CX, 4), hot)
+
+    def columns(count):
+        for k in range(4):
+            node = near[k : k + 1, :].astype(jnp.int32)
+            put_one_hot(node & (count - 1), count, near_hot, 0, slice(k * 1024, (k + 1) * 1024))
+
+    low_x, high_x = (0, CX - D), (D + CX, 0)
+    low_y, high_y = (0, CY - D), (D + CY, 0)
+    for ref, (x0, first) in ((px_low, low_x), (px_high, high_x)):
         take_meta(ref, PX_META, near)
         returned(near)
-        scatter(
-            near,
-            values,
-            lambda n, first=first: (n >> 10) - first * CY,
-            column,
-            D * CY,
-            4,
-            lhs,
-            put_planes(x0, D),
-        )
-
-    def strip(first_x, planes, first_y):
-        def rows(node):
-            x, y = xy(node)
-            x, y = x - first_x, y - first_y
-            good = (x >= 0) & (x < planes) & (y >= 0) & (y < D)
-            return jnp.where(good, ((node >> 8) & 3) * (planes * D) + x * D + y, -1)
-
-        return rows
-
-    for ref, y0, first in ((py_low, 0, CY - D), (py_high, D + CY, 0)):
-        take_meta(ref, 3 * HALO_Y, near)
+        columns(512)
+        rows = box(first, D, 0, CY, 9)
+        scatter(near, values, rows, 2 * D * CY, 2, lhs, put_planes(x0, D, 2), near_hot)
+    strips = [(ref, 3 * HALO_Y, D, 0, CX) + y for ref, y in ((py_low, low_y), (py_high, high_y))]
+    for ref, (x0, first) in ((c_low, low_x), (c_high, high_x)):
+        for side, y in enumerate((low_y, high_y)):
+            strips.append((ref, side * PART + 3 * HALO_C, x0, first, D) + y)
+    for ref, base, x0, first_x, planes, y0, first_y in strips:
+        take_meta(ref, base, near)
         returned(near)
-        scatter(
-            near, values, strip(0, CX, first), low_column, 4 * CX * D, 1, lhs, put_strip(D, CX, y0)
-        )
-
-    for ref, x0, first_x in ((c_low, 0, CX - D), (c_high, D + CX, 0)):
-        for side, y0, first_y in ((0, 0, CY - D), (1, D + CY, 0)):
-            take_meta(ref, side * PART + 3 * HALO_C, near)
-            returned(near)
-            scatter(
-                near,
-                values,
-                strip(first_x, D, first_y),
-                low_column,
-                4 * D * D,
-                1,
-                lhs,
-                put_strip(x0, D, y0),
-            )
+        columns(256)
+        rows = box(first_x, planes, first_y, D, 8)
+        keep = put_strip(x0, planes, y0)
+        scatter(near, values, rows, 4 * planes * D, 1, lhs, keep, near_hot)
 
     def first(x, y, n):
         f, acc = fluxes(src, q, cz, x, y, n)
@@ -545,7 +571,22 @@
     lax.fori_loop(0, CY, flux, 0)
 
 
-def own_kernel(permit_hbm, back_hbm, perturb_hbm, meta, q, bg, qp, hot, permit, back, perturb, sems):
+def own_kernel(
+    permit_hbm,
+    back_hbm,
+    perturb_hbm,
+    meta,
+    q,
+    bg,
+    qp,
+    cz,
+    bz,
+    hot,
+    permit,
+    back,
+    perturb,
+    sems,
+):
     pairs = ((permit_hbm, permit), (back_hbm, back), (perturb_hbm, perturb))
     copies = [pltpu.make_async_copy(a, b, sems.at[i]) for i, (a, b) in enumerate(pairs)]
     for copy in copies:
@@ -554,7 +595,8 @@
     def entries(i, carry):
         k, lanes = i // 2, pl.ds(pl.multiple_of((i % 2) * 512, 512), 512)
         node = meta[pl.ds(k, 1), lanes].astype(jnp.int32)
-        hot[:, pl.ds(pl.multiple_of(i * 512, 512), 512)] = one_hot(node & (CZ - 1), CZ)
+        at = pl.ds(pl.multiple_of(i * 512, 512), 512)
+        put_one_hot(node & (CZ - 1), CZ, hot, 0, at)
         return carry
 
     lax.fori_loop(0, 8, entries, 0)
@@ -566,12 +608,17 @@
             q[x, y] = row_of(permit, x, y) * (0.5 / HALF)
             bg[x, y] = row_of(back, x, y)
             qp[x, y] = row_of(perturb, x, y) * 0.5
+        for y in range(0, CY, 4):
+            at = pl.ds(y, 4)
+            cz[x, at] = z_face(q[x, at])
+            bz[x, at] = z_fluxes(bg[x, at], z_face(qp[x, at]))
         return carry
 
     lax.fori_loop(0, CX, plane, 0)
 
 
-def corner_kernel(py_low, py_high, low, high):
+def corner_kernel(py_low, py_high, after, low, high):
+    del after
     for side, ref in enumerate((py_low, py_high)):
         for field in range(3):
             for i, (dx, dy) in enumerate(CELLS):
@@ -652,9 +699,9 @@
     py_low, py_high = shift(high_y, "py", 1), shift(low_y, "py", -1)
     compact = jax.ShapeDtypeStruct((CX, CY, 8, 128), F32)
     full = jax.ShapeDtypeStruct((EX, EY, 8, 128), F32)
-    own_q, own_bg, own_qp, hot = call(
+    own_q, own_bg, own_qp, own_cz, own_bz, hot = call(
         own_kernel,
-        [compact] * 3 + [jax.ShapeDtypeStruct((CZ, 4096), BF16)],
+        [compact] * 5 + [jax.ShapeDtypeStruct((CZ, 4096), BF16)],
         *fields,
         meta,
         hbm=3,
@@ -662,7 +709,7 @@
         limit=10,
         bytes_accessed=8 * 2**20,
     )
-    low_c, high_c = call(corner_kernel, rows(size_c, size_c), py_low, py_high, limit=4)
+    low_c, high_c = call(corner_kernel, rows(size_c, size_c), py_low, py_high, own_cz, limit=4)
     c_low, c_high = shift(high_c, "px", 1), shift(low_c, "px", -1)
     sides = (px_low, px_high, py_low, py_high, c_low, c_high)
 
@@ -673,13 +720,15 @@
         own_q,
         own_bg,
         own_qp,
+        own_cz,
+        own_bz,
         *sides,
         meta,
         hot,
         weights,
         scratch=[block] * 4
         + [pltpu.VMEM((2 * CX * CY, CZ), BF16), pltpu.VMEM((8, 1024), F32)],
-        limit=18,
+        limit=20,
     )
     got = lax.all_to_all(
         readings.reshape(devices, 1, 9 * 128),
@@ -701,10 +750,11 @@
         scratch=[block] * 3
         + [
             pltpu.VMEM((2 * CX * CY, 4096), BF16),
+            pltpu.VMEM((512, 4096), BF16),
             pltpu.VMEM((16, 1024), F32),
             pltpu.VMEM((8, 1024), F32),
         ],
-        limit=24,
+        limit=28,
     )
     return from_tiles(result)
 

time: 98.9 us -> 96.7 us (0.978)
  waiting for transfers between devices: 11 us -> 9.56 us
    ppermute x6, waiting for transfers between devices: 11 us -> 9.56 us  [shift(): return lax.ppermute(x, axis, [(i, (i + by) % count) for i in range(count)])]
  transfers between devices with their start and end apart: 6 -> 6, of which waited for: 3 -> 3; matrix products, arithmetic and copies ran while one was open for 0% -> 0% of each run, Pallas kernels for 3% -> 4%
where the time goes in v4:
time: 96.7 us; the launch traced here: 96.5 us
  Pallas kernels  52.2 us (54%)
  blocking collectives  22.5 us (23%)
  starting transfers between devices  12.3 us (13%)
  waiting for transfers between devices  9.56 us (10%)
    pallas_call x5, Pallas kernels, call(): pl.pallas_call(kernel, out_shape=tuple(outs), in_specs=[pl.BlockSpec(memo...  52.2 us
    all_to_all x1, blocking collectives, body(): lax.all_to_all(readings.reshape(devices, 1, 9 * 128), ('px', 'py'), split...  22.5 us
    ppermute x6, starting transfers between devices, shift(): return lax.ppermute(x, axis, [(i, (i + by) % count) for i in range(count)])  12.3 us
    ppermute x6, waiting for transfers between devices, shift(): return lax.ppermute(x, axis, [(i, (i + by) % count) for i in range(count)])  9.56 us
  transfers between devices with their start and end apart: 6, of which 3 were waited for; matrix products, arithmetic and copies ran while one was open for 0% of the time, Pallas kernels for 4%

profile of v4, /device:TPU:1, one launch (start us, length us, event | category | flops | bytes accessed | tf_op | source)
XLA Modules:
  0.0 96.5 jit_solution(15517712382516291485)
XLA Ops:
  0.0 2.8 %shard_map.82 = (f32[2896,128]{1,0:T(8,128)S(1)}, f32[2896,128]{1,0:T(8,128)S(1)}, f32[848,128]{1,0:T(8,128)S(1)}, f32[848,128]{1,0:T(8,128)S(1)}, f32[16,1024]{1,0:T(8,128)S(1)}) custom-call(f32[2048,128]{1,0:T(8,128)} %bitcast.28, f32[2048,128]{1,0:T(8,128)} %bitcast.30, f32[2048,128]{1,0:T(8,128)} %bitcast.32, s32[4,1024]{1,0:T(4,128)} %nodes_hbm.1, ...), custom_call_target="tpu_custom_call" | custom-call | tf_op jit(solution)/shard_map/pallas_call | solution.py:664
  2.8 0.0 copy-start
  2.8 3.0 %collective-permute-start = (f32[2896,128]{1,0:T(8,128)S(1)}, f32[2896,128]{1,0:T(8,128)S(1)}, u32[]{:S(2)}, u32[]{:S(2)}) collective-permute-start(f32[2896,128]{1,0:T(8,128)S(1)} %get-tuple-element.28), channel_id=1, source_target_pairs={{0,16},{16,32},{32,48},{48,64},{64,80},{80,96},{96,112},{112,0},{1... | collective-permute-start | bytes 4448264 | tf_op jit(solution)/shard_map/ppermute | solution.py:641
  5.9 0.0 collective-permute-start.1
  5.9 1.2 %collective-permute-start.2 = (f32[848,128]{1,0:T(8,128)S(1)}, f32[848,128]{1,0:T(8,128)S(1)}, u32[]{:S(2)}, u32[]{:S(2)}) collective-permute-start(f32[848,128]{1,0:T(8,128)S(1)} %get-tuple-element.30), channel_id=1, source_target_pairs={{0,1},{1,2},{2,3},{3,4},{4,5},{5,6},{6,7},{7,8},{8,9},{9,10},{10,1... | collective-permute-start | bytes 1302536 | tf_op jit(solution)/shard_map/ppermute | solution.py:641
  7.1 3.7 %collective-permute-start.3 = (f32[848,128]{1,0:T(8,128)S(1)}, f32[848,128]{1,0:T(8,128)S(1)}, u32[]{:S(2)}, u32[]{:S(2)}) collective-permute-start(f32[848,128]{1,0:T(8,128)S(1)} %get-tuple-element.31), channel_id=1, source_target_pairs={{0,15},{1,0},{2,1},{3,2},{4,3},{5,4},{6,5},{7,6},{8,7},{9,8},{10,9... | collective-permute-start | bytes 1302536 | tf_op jit(solution)/shard_map/ppermute | solution.py:641
  10.8 4.1 %shard_map.83 = (f32[8,32,8,128]{3,2,1,0:T(8,128)S(1)}, f32[8,32,8,128]{3,2,1,0:T(8,128)S(1)}, f32[8,32,8,128]{3,2,1,0:T(8,128)S(1)}, f32[8,32,8,128]{3,2,1,0:T(...) custom-call(f32[2048,128]{1,0:T(8,128)} %bitcast.29, f32[2048,128]{1,0:T(8,128)} %bitcast.31, ...), custom_call_target="tpu_custom_call" | custom-call | bytes 8388608 | tf_op jit(solution)/shard_map/pallas_call | solution.py:664
  14.9 4.1 %collective-permute-done.2.py_low = f32[848,128]{1,0:T(8,128)S(1)} collective-permute-done((f32[848,128]{1,0:T(8,128)S(1)}, f32[848,128]{1,0:T(8,128)S(1)}, u32[]{:S(2)}, u32[]{:S(2)}) %collective-permute-start.2) | collective-permute-done | bytes 434208 | tf_op jit(solution)/shard_map/ppermute | solution.py:641
  19.0 0.0 collective-permute-done.3.py_high
  19.0 4.3 %collective-permute-start.4 = (f32[448,128]{1,0:T(8,128)S(1)}, f32[448,128]{1,0:T(8,128)S(1)}, u32[]{:S(2)}, u32[]{:S(2)}) collective-permute-start(f32[448,128]{1,0:T(8,128)S(1)} %get-tuple-element.32), channel_id=1, source_target_pairs={{0,16},{16,32},{32,48},{48,64},{64,80},{80,96},{96,112},{112,0},{1... | collective-permute-start | bytes 688136 | tf_op jit(solution)/shard_map/ppermute | solution.py:641
  23.3 0.0 collective-permute-start.5
  23.3 0.0 copy-done
  23.3 3.0 %collective-permute-done.4.c_low = f32[448,128]{1,0:T(8,128)S(1)} collective-permute-done((f32[448,128]{1,0:T(8,128)S(1)}, f32[448,128]{1,0:T(8,128)S(1)}, u32[]{:S(2)}, u32[]{:S(2)}) %collective-permute-start.4) | collective-permute-done | bytes 229408 | tf_op jit(solution)/shard_map/ppermute | solution.py:641
  26.3 2.5 %collective-permute-done.5.c_high = f32[448,128]{1,0:T(8,128)S(1)} collective-permute-done((f32[448,128]{1,0:T(8,128)S(1)}, f32[448,128]{1,0:T(8,128)S(1)}, u32[]{:S(2)}, u32[]{:S(2)}) %collective-permute-start.5) | collective-permute-done | bytes 229408 | tf_op jit(solution)/shard_map/ppermute | solution.py:641
  28.8 0.0 collective-permute-done.px_low
  28.8 0.0 collective-permute-done.1.px_high
  28.8 17.7 %shard_map.85 = (f32[1152,128]{1,0:T(8,128)S(1)}, f32[16,40,8,128]{3,2,1,0:T(8,128)S(1)}, f32[16,40,8,128]{3,2,1,0:T(8,128)S(1)}, f32[16,40,8,128]{3,2,1,0:T(8,128)S(1)}) custom-call(f32[8,32,8,128]{3,2,1,0:T(8,128)S(1)} %get-tuple-element.23.permit, f32[8,32,8,128]{3,2,1,0:T(8,128)S(1)} %get-tuple-element.24.back, ...), custom_call_target="tpu_custom_call" | custom-call | tf_op jit(solution)/shard_map/pallas_call | solution.py:664
  46.5 22.5 %all_to_all.5 = f32[128,1,1152]{2,1,0:T(1,128)S(1)} all-to-all(f32[128,1,1152]{2,1,0:T(1,128)S(1)} %bitcast.27), channel_id=1, replica_groups=mesh['px'=8,'py'=16] {'px','py'}, dimensions={0} | all-to-all | bytes 1179648 | tf_op jit(solution)/shard_map/all_to_all | solution.py:733
  69.0 27.6 %shard_map.86 = f32[2048,128]{1,0:T(8,128)} custom-call(f32[1152,128]{1,0:T(8,128)S(1)} %bitcast.26, f32[2896,128]{1,0:T(8,128)S(1)} %collective-permute-done.px_low, f32[2896,128]{1,0:T(8,128)S(1)} %collective-permute-done.1.px_high, f32[848,128]{1,0:T(8,128)S(1)} %collective-permute-done.2.py_low, f32[848,128]{1,0:T(8,128)S(1)} %collective-permute-done.3.py_high, ...), custom_call_target="tpu_custom_call" | custom-call | tf_op jit(solution)/shard_map/pallas_call | solution.py:664
  (2 shorter events, 0.0 us)
Async XLA Ops:
  2.8 20.5 %copy-start = (f32[8]{0:T(128)S(1)}, f32[8]{0:T(128)}, u32[]{:S(2)}) copy-start(f32[8]{0:T(128)} %param.15) | copy-start | bytes 100
  2.8 25.9 %collective-permute-start = (f32[2896,128]{1,0:T(8,128)S(1)}, f32[2896,128]{1,0:T(8,128)S(1)}, u32[]{:S(2)}, u32[]{:S(2)}) collective-permute-start(f32[2896,128]{1,0:T(8,128)S(1)} %get-tuple-element.28), channel_id=1, source_target_pairs={{0,16},{16,32},{32,48},{48,64},{64,80},{80,96},{96,112},{112,0},{1... | collective-permute-start | bytes 4448264 | tf_op jit(solution)/shard_map/ppermute | solution.py:641
  5.9 22.9 %collective-permute-start.1 = (f32[2896,128]{1,0:T(8,128)S(1)}, f32[2896,128]{1,0:T(8,128)S(1)}, u32[]{:S(2)}, u32[]{:S(2)}) collective-permute-start(f32[2896,128]{1,0:T(8,128)S(1)} %get-tuple-element.29), channel_id=1, source_target_pairs={{0,112},{16,0},{32,16},{48,32},{64,48},{80,64},{96,80},{112,96},{1... | collective-permute-start | bytes 4448264 | tf_op jit(solution)/shard_map/ppermute | solution.py:641
  5.9 13.1 %collective-permute-start.2 = (f32[848,128]{1,0:T(8,128)S(1)}, f32[848,128]{1,0:T(8,128)S(1)}, u32[]{:S(2)}, u32[]{:S(2)}) collective-permute-start(f32[848,128]{1,0:T(8,128)S(1)} %get-tuple-element.30), channel_id=1, source_target_pairs={{0,1},{1,2},{2,3},{3,4},{4,5},{5,6},{6,7},{7,8},{8,9},{9,10},{10,1... | collective-permute-start | bytes 1302536 | tf_op jit(solution)/shard_map/ppermute | solution.py:641
  7.1 11.9 %collective-permute-start.3 = (f32[848,128]{1,0:T(8,128)S(1)}, f32[848,128]{1,0:T(8,128)S(1)}, u32[]{:S(2)}, u32[]{:S(2)}) collective-permute-start(f32[848,128]{1,0:T(8,128)S(1)} %get-tuple-element.31), channel_id=1, source_target_pairs={{0,15},{1,0},{2,1},{3,2},{4,3},{5,4},{6,5},{7,6},{8,7},{9,8},{10,9... | collective-permute-start | bytes 1302536 | tf_op jit(solution)/shard_map/ppermute | solution.py:641
  19.0 7.3 %collective-permute-start.4 = (f32[448,128]{1,0:T(8,128)S(1)}, f32[448,128]{1,0:T(8,128)S(1)}, u32[]{:S(2)}, u32[]{:S(2)}) collective-permute-start(f32[448,128]{1,0:T(8,128)S(1)} %get-tuple-element.32), channel_id=1, source_target_pairs={{0,16},{16,32},{32,48},{48,64},{64,80},{80,96},{96,112},{112,0},{1... | collective-permute-start | bytes 688136 | tf_op jit(solution)/shard_map/ppermute | solution.py:641
  23.3 5.4 %collective-permute-start.5 = (f32[448,128]{1,0:T(8,128)S(1)}, f32[448,128]{1,0:T(8,128)S(1)}, u32[]{:S(2)}, u32[]{:S(2)}) collective-permute-start(f32[448,128]{1,0:T(8,128)S(1)} %get-tuple-element.33), channel_id=1, source_target_pairs={{0,112},{16,0},{32,16},{48,32},{64,48},{80,64},{96,80},{112,96},{1... | collective-permute-start | bytes 688136 | tf_op jit(solution)/shard_map/ppermute | solution.py:641

commit v5 on v4

--- a/solution.py
+++ b/solution.py
@@ -20,7 +20,7 @@
 PLANE = CY * 8
 PX_AT = (0, D * PLANE, (2 * D - 1) * PLANE)
 PX_FLUX = (3 * D - 2) * PLANE
-PX_META = (3 * D - 1) * PLANE
+PX_ROWS = (3 * D - 1) * PLANE
 HALO_Y = CX * D * 8
 CELLS = tuple((dx, dy) for dx in range(1, D) for dy in range(1, D) if dx + dy <= D)
 HALO_C = len(CELLS) * 8
@@ -246,9 +246,9 @@
         cz[x, pl.ds(y, n)] = z_face(q[x, pl.ds(y, n)])
 
     def outer_planes(i, carry):
-        for x in (1 + i, D + CX + i):
-            for y in cover(1, EY - 1, 4):
-                outer(x, y, 4)
+        x = jnp.where(i < D - 1, 1 + i, CX + 1 + i)
+        for y in cover(1, EY - 1, 4):
+            outer(x, y, 4)
         return carry
 
     def own_planes(x, carry):
@@ -259,7 +259,7 @@
             b[x, pl.ds(y, 4)] = acc + own_bz[x - D, pl.ds(y - D, 4)]
         return carry
 
-    lax.fori_loop(0, D - 1, outer_planes, 0)
+    lax.fori_loop(0, 2 * (D - 1), outer_planes, 0)
     lax.fori_loop(D, D + CX, own_planes, 0)
 
     def second(x, y, n):
@@ -312,7 +312,7 @@
         out[i * 72 : (i + 1) * 72, :] = block
 
 
-def scatter(meta, values, rows, per, tiles, lhs, keep, hot):
+def scatter(meta, values, rows, per, tiles, width, lhs, keep, hot):
     for k in range(4):
         wanted, numbers = rows16(rows(meta[k : k + 1, :].astype(jnp.int32)))
         value = jnp.broadcast_to(values[k : k + 1, :], wanted.shape)
@@ -328,7 +328,7 @@
         total = None
         for k in range(4):
             lanes = slice(k * 1024, (k + 1) * 1024)
-            hits = hot[pl.ds(pl.multiple_of(t * 256, 256), 256), lanes]
+            hits = hot[pl.ds(pl.multiple_of(t * width, width), width), lanes]
             part = dot(lhs[0 : 2 * per, lanes], hits, ((1,), (1,)))
             total = part if total is None else total + part
         keep(t, total[0:per] + total[per : 2 * per])
@@ -340,105 +340,86 @@
         lax.fori_loop(0, tiles, tile, 0)
 
 
-def adjoint_kernel(
-    got,
-    px_low,
-    px_high,
-    py_low,
-    py_high,
-    c_low,
-    c_high,
-    meta,
-    hot,
-    q,
-    bg,
-    cz,
-    out,
-    src,
-    y1,
-    y2,
-    lhs,
-    near_hot,
-    near,
-    values,
-):
+def returned(weighted, table, values):
+    owner, sensor = table[8:9, :].astype(jnp.int32), table[9:10, :].astype(jnp.int32)
+    parts = jnp.concatenate(three_parts(weighted), axis=0)
+    found = dot(parts, one_hot(owner, 128), ((1,), (0,)))
+    found = found[0:8] + found[8:16] + found[16:24]
+    at = lax.broadcasted_iota(jnp.int32, found.shape, 0)
+    found = jnp.sum(jnp.where(at == sensor, found, 0.0), axis=0, keepdims=True)
+    values[0:4, :] = table[4:8, :] * found
+
+
+def source_kernel(got, meta, hot, weighted, own, low, high, lhs, values):
     count = got.shape[0] // 9
     sums = [jnp.sum(got[pl.ds(i, count, stride=9), :], axis=0, keepdims=True) for i in range(8)]
     readings = jnp.concatenate(sums, axis=0)
     weights = jnp.transpose(got[pl.ds(8, count, stride=9), :])[0:8]
-    weighted = jnp.concatenate(three_parts(readings * weights), axis=0)
-
-    def returned(table):
-        owner, sensor = table[8:9, :].astype(jnp.int32), table[9:10, :].astype(jnp.int32)
-        found = dot(weighted, one_hot(owner, 128), ((1,), (0,)))
-        found = found[0:8] + found[8:16] + found[16:24]
-        at = lax.broadcasted_iota(jnp.int32, found.shape, 0)
-        found = jnp.sum(jnp.where(at == sensor, found, 0.0), axis=0, keepdims=True)
-        values[0:4, :] = table[4:8, :] * found
-
-    flat = src.reshape(EX * EY * 8, 128)
-
-    def put_planes(x0, planes, tiles):
-        def keep(t, sums):
-            for zq in range(4 // tiles):
-                for x in range(planes):
-                    first = (zq * planes + x) * CY
-                    for half in range(2):
-                        c = zq * tiles * 2 + t * 2 + half
-                        flat[pl.ds(((x + x0) * EY + D) * 8 + c, CY, stride=8), :] = sums[
-                            first : first + CY, half * 128 : (half + 1) * 128
-                        ]
-
-        return keep
-
-    def put_strip(x0, planes, y0):
-        def keep(t, sums):
-            for zq in range(4):
-                for x in range(planes):
-                    first = (zq * planes + x) * D
-                    for half in range(2):
-                        flat[
-                            pl.ds(((x + x0) * EY + y0) * 8 + zq * 2 + half, D, stride=8), :
-                        ] = sums[first : first + D, half * 128 : (half + 1) * 128]
-
-        return keep
-
-    def box(first_x, planes, first_y, lines, bits):
+    weighted[...] = readings * weights
+
+    def keep(t, sums):
+        for x in range(CX):
+            for i in range(4):
+                block = sums[x * CY : (x + 1) * CY, i * 128 : (i + 1) * 128]
+                own[pl.ds(x * PLANE + t * 4 + i, CY, stride=8), :] = block
+                side, at = (low, x) if x < D else (high, x - (CX - D))
+                side[pl.ds(at * PLANE + t * 4 + i, CY, stride=8), :] = block
+
+    returned(weighted[...], meta, values)
+    scatter(meta, values, lambda n: n >> 10, CX * CY, 2, 512, lhs, keep, hot)
+
+
+def strips_kernel(
+    weighted, py_low, py_high, c_low, c_high, strips, corners, lhs, near_hot, near, values
+):
+    def box(first_x, planes, first_y):
         def rows(node):
             x, y = (node >> 15) - first_x, ((node >> 10) & (CY - 1)) - first_y
-            good = (x >= 0) & (x < planes) & (y >= 0) & (y < lines)
-            z = (node & (CZ - 1)) >> bits
-            return jnp.where(good, (z * planes + x) * lines + y, -1)
+            good = (x >= 0) & (x < planes) & (y >= 0) & (y < D)
+            return jnp.where(good, (((node >> 8) & 3) * planes + x) * D + y, -1)
 
         return rows
 
-    returned(meta)
-    scatter(meta, values, lambda n: n >> 10, CX * CY, 4, lhs, put_planes(D, CX, 4), hot)
-
-    def columns(count):
+    low_x, high_x, low_y, high_y = CX - D, 0, CY - D, 0
+    tasks = [
+        (py_low, 3 * HALO_Y, 0, CX, low_y, strips, 0),
+        (py_high, 3 * HALO_Y, 0, CX, high_y, strips, HALO_Y),
+    ]
+    for i, (ref, first_x) in enumerate(((c_low, low_x), (c_high, high_x))):
+        for side, first_y in enumerate((low_y, high_y)):
+            base, to = side * PART + 3 * HALO_C, (2 * i + side) * D * D * 8
+            tasks.append((ref, base, first_x, D, first_y, corners, to))
+    for ref, base, first_x, planes, first_y, out, to in tasks:
+        take_meta(ref, base, near)
+        returned(weighted[...], near, values)
         for k in range(4):
             node = near[k : k + 1, :].astype(jnp.int32)
-            put_one_hot(node & (count - 1), count, near_hot, 0, slice(k * 1024, (k + 1) * 1024))
-
-    low_x, high_x = (0, CX - D), (D + CX, 0)
-    low_y, high_y = (0, CY - D), (D + CY, 0)
-    for ref, (x0, first) in ((px_low, low_x), (px_high, high_x)):
-        take_meta(ref, PX_META, near)
-        returned(near)
-        columns(512)
-        rows = box(first, D, 0, CY, 9)
-        scatter(near, values, rows, 2 * D * CY, 2, lhs, put_planes(x0, D, 2), near_hot)
-    strips = [(ref, 3 * HALO_Y, D, 0, CX) + y for ref, y in ((py_low, low_y), (py_high, high_y))]
-    for ref, (x0, first) in ((c_low, low_x), (c_high, high_x)):
-        for side, y in enumerate((low_y, high_y)):
-            strips.append((ref, side * PART + 3 * HALO_C, x0, first, D) + y)
-    for ref, base, x0, first_x, planes, y0, first_y in strips:
-        take_meta(ref, base, near)
-        returned(near)
-        columns(256)
-        rows = box(first_x, planes, first_y, D, 8)
-        keep = put_strip(x0, planes, y0)
-        scatter(near, values, rows, 4 * planes * D, 1, lhs, keep, near_hot)
+            put_one_hot(node & 255, 256, near_hot, 0, slice(k * 1024, (k + 1) * 1024))
+
+        def keep(t, sums, planes=planes, out=out, to=to):
+            lines = planes * D
+            for zq in range(4):
+                for half in range(2):
+                    out[pl.ds(to + zq * 2 + half, lines, stride=8), :] = sums[
+                        zq * lines : (zq + 1) * lines, half * 128 : (half + 1) * 128
+                    ]
+
+        rows = box(first_x, planes, first_y)
+        scatter(near, values, rows, 4 * planes * D, 1, 256, lhs, keep, near_hot)
+
+
+def adjoint_kernel(own, px_low, px_high, strips, corners, q, bg, cz, out, src, y1, y2):
+    middle_x, middle_y = slice(D, D + CX), slice(D, D + CY)
+    src[middle_x, middle_y] = own[...].reshape(CX, CY, 8, 128)
+    for x, ref in ((0, px_low), (D + CX, px_high)):
+        src[x : x + D, middle_y] = ref[...].reshape(D, CY, 8, 128)
+    for side, y in enumerate((0, D + CY)):
+        v = strips[side * HALO_Y : (side + 1) * HALO_Y, :]
+        src[middle_x, y : y + D] = v.reshape(CX, D, 8, 128)
+        for i, x in enumerate((0, D + CX)):
+            at = (2 * i + side) * D * D * 8
+            v = corners[at : at + D * D * 8, :]
+            src[x : x + D, y : y + D] = v.reshape(D, D, 8, 128)
 
     def first(x, y, n):
         f, acc = fluxes(src, q, cz, x, y, n)
@@ -536,7 +517,7 @@
     meta[8:9, :] = owner[...].astype(F32)
     meta[9:10, :] = sensor[...].astype(F32)
     meta[10:16, :] = jnp.zeros((6, 1024), F32)
-    for out, at in ((low_x, PX_META), (high_x, PX_META), (low_y, 3 * HALO_Y), (high_y, 3 * HALO_Y)):
+    for out, at in ((low_y, 3 * HALO_Y), (high_y, 3 * HALO_Y)):
         for c in range(8):
             lanes = slice(c * 128, (c + 1) * 128)
             out[at + c * 8 : at + c * 8 + 8, :] = meta[0:8, lanes]
@@ -673,7 +654,7 @@
             ),
         )(*args)
 
-    size_x, size_y, size_c = PX_META + META, 3 * HALO_Y + META, 2 * PART
+    size_x, size_y, size_c = PX_ROWS, 3 * HALO_Y + META, 2 * PART
     raw = [pltpu.VMEM((ROWS, 128), F32)] * 3
     table = jax.ShapeDtypeStruct((16, 1024), F32)
     low_x, high_x, low_y, high_y, meta = call(
@@ -737,24 +718,43 @@
         concat_axis=0,
         tiled=True,
     ).reshape(devices * 9, 128)
+    weighted, own_source, low_s, high_s = call(
+        source_kernel,
+        rows(8, ROWS, D * PLANE, D * PLANE),
+        got,
+        meta,
+        hot,
+        scratch=[pltpu.VMEM((2 * CX * CY, 4096), BF16), pltpu.VMEM((8, 1024), F32)],
+        limit=18,
+    )
+    source_low, source_high = shift(high_s, "px", 1), shift(low_s, "px", -1)
+    strips, corners = call(
+        strips_kernel,
+        rows(2 * HALO_Y, 4 * D * D * 8),
+        weighted,
+        *sides[2:],
+        scratch=[
+            pltpu.VMEM((2 * 4 * CX * D, 4096), BF16),
+            pltpu.VMEM((256, 4096), BF16),
+            pltpu.VMEM((16, 1024), F32),
+            pltpu.VMEM((8, 1024), F32),
+        ],
+        limit=16,
+        bytes_accessed=16 * 2**20,
+    )
     (result,) = call(
         adjoint_kernel,
         rows(ROWS),
-        got,
-        *sides,
-        meta,
-        hot,
+        own_source,
+        source_low,
+        source_high,
+        strips,
+        corners,
         q,
         bg,
         cz,
-        scratch=[block] * 3
-        + [
-            pltpu.VMEM((2 * CX * CY, 4096), BF16),
-            pltpu.VMEM((512, 4096), BF16),
-            pltpu.VMEM((16, 1024), F32),
-            pltpu.VMEM((8, 1024), F32),
-        ],
-        limit=28,
+        scratch=[block] * 3,
+        limit=16,
     )
     return from_tiles(result)
 

time: 96.7 us -> 93.9 us (0.971)
  Pallas kernels: 52.2 us -> 43.8 us
  waiting for transfers between devices: 9.56 us -> 14 us
  starting transfers between devices: 12.3 us -> 13.5 us
    pallas_call x5 -> x7, Pallas kernels: 52.2 us -> 43.8 us  [call(): pl.pallas_call(kernel, out_shape=tuple(outs), in_specs=[pl.BlockSpec(memo...]
    ppermute x6 -> x8, waiting for transfers between devices: 9.56 us -> 14 us  [shift(): return lax.ppermute(x, axis, [(i, (i + by) % count) for i in range(count)])]
    ppermute x6 -> x8, starting transfers between devices: 12.3 us -> 13.5 us  [shift(): return lax.ppermute(x, axis, [(i, (i + by) % count) for i in range(count)])]
  transfers between devices with their start and end apart: 6 -> 8, of which waited for: 3 -> 5; matrix products, arithmetic and copies ran while one was open for 0% -> 0% of each run, Pallas kernels for 4% -> 9%
where the time goes in v5:
time: 93.9 us; the launch traced here: 93.8 us
  Pallas kernels  43.8 us (47%)
  blocking collectives  22.4 us (24%)
  waiting for transfers between devices  14 us (15%)
  starting transfers between devices  13.5 us (14%)
    pallas_call x7, Pallas kernels, call(): pl.pallas_call(kernel, out_shape=tuple(outs), in_specs=[pl.BlockSpec(memo...  43.8 us
    all_to_all x1, blocking collectives, body(): lax.all_to_all(readings.reshape(devices, 1, 9 * 128), ('px', 'py'), split...  22.4 us
    ppermute x8, waiting for transfers between devices, shift(): return lax.ppermute(x, axis, [(i, (i + by) % count) for i in range(count)])  14 us
    ppermute x8, starting transfers between devices, shift(): return lax.ppermute(x, axis, [(i, (i + by) % count) for i in range(count)])  13.5 us
  transfers between devices with their start and end apart: 8, of which 5 were waited for; matrix products, arithmetic and copies ran while one was open for 0% of the time, Pallas kernels for 9%

profile of v5, /device:TPU:1, one launch (start us, length us, event | category | flops | bytes accessed | tf_op | source)
XLA Modules:
  0.0 93.8 jit_solution(13330645259570550598)
XLA Ops:
  0.0 2.8 %shard_map.82 = (f32[2816,128]{1,0:T(8,128)S(1)}, f32[2816,128]{1,0:T(8,128)S(1)}, f32[848,128]{1,0:T(8,128)S(1)}, f32[848,128]{1,0:T(8,128)S(1)}, f32[16,1024]{1,0:T(8,128)S(1)}) custom-call(f32[2048,128]{1,0:T(8,128)} %bitcast.28, f32[2048,128]{1,0:T(8,128)} %bitcast.30, f32[2048,128]{1,0:T(8,128)} %bitcast.32, s32[4,1024]{1,0:T(4,128)} %nodes_hbm.1, ...), custom_call_target="tpu_custom_call" | custom-call | tf_op jit(solution)/shard_map/pallas_call | solution.py:645
  2.8 0.0 copy-start
  2.8 3.0 %collective-permute-start = (f32[2816,128]{1,0:T(8,128)S(1)}, f32[2816,128]{1,0:T(8,128)S(1)}, u32[]{:S(2)}, u32[]{:S(2)}) collective-permute-start(f32[2816,128]{1,0:T(8,128)S(1)} %get-tuple-element.34), channel_id=1, source_target_pairs={{0,16},{16,32},{32,48},{48,64},{64,80},{80,96},{96,112},{112,0},{1... | collective-permute-start | bytes 4325384 | tf_op jit(solution)/shard_map/ppermute | solution.py:622
  5.9 0.0 collective-permute-start.1
  5.9 1.2 %collective-permute-start.2 = (f32[848,128]{1,0:T(8,128)S(1)}, f32[848,128]{1,0:T(8,128)S(1)}, u32[]{:S(2)}, u32[]{:S(2)}) collective-permute-start(f32[848,128]{1,0:T(8,128)S(1)} %get-tuple-element.36), channel_id=1, source_target_pairs={{0,1},{1,2},{2,3},{3,4},{4,5},{5,6},{6,7},{7,8},{8,9},{9,10},{10,1... | collective-permute-start | bytes 1302536 | tf_op jit(solution)/shard_map/ppermute | solution.py:622
  7.1 3.7 %collective-permute-start.3 = (f32[848,128]{1,0:T(8,128)S(1)}, f32[848,128]{1,0:T(8,128)S(1)}, u32[]{:S(2)}, u32[]{:S(2)}) collective-permute-start(f32[848,128]{1,0:T(8,128)S(1)} %get-tuple-element.37), channel_id=1, source_target_pairs={{0,15},{1,0},{2,1},{3,2},{4,3},{5,4},{6,5},{7,6},{8,7},{9,8},{10,9... | collective-permute-start | bytes 1302536 | tf_op jit(solution)/shard_map/ppermute | solution.py:622
  10.8 4.0 %shard_map.83 = (f32[8,32,8,128]{3,2,1,0:T(8,128)S(1)}, f32[8,32,8,128]{3,2,1,0:T(8,128)S(1)}, f32[8,32,8,128]{3,2,1,0:T(8,128)S(1)}, f32[8,32,8,128]{3,2,1,0:T(...) custom-call(f32[2048,128]{1,0:T(8,128)} %bitcast.29, f32[2048,128]{1,0:T(8,128)} %bitcast.31, ...), custom_call_target="tpu_custom_call" | custom-call | bytes 8388608 | tf_op jit(solution)/shard_map/pallas_call | solution.py:645
  14.9 4.1 %collective-permute-done.2.py_low = f32[848,128]{1,0:T(8,128)S(1)} collective-permute-done((f32[848,128]{1,0:T(8,128)S(1)}, f32[848,128]{1,0:T(8,128)S(1)}, u32[]{:S(2)}, u32[]{:S(2)}) %collective-permute-start.2) | collective-permute-done | bytes 434208 | tf_op jit(solution)/shard_map/ppermute | solution.py:622
  19.0 0.0 collective-permute-done.3.py_high
  19.0 4.3 %collective-permute-start.4 = (f32[448,128]{1,0:T(8,128)S(1)}, f32[448,128]{1,0:T(8,128)S(1)}, u32[]{:S(2)}, u32[]{:S(2)}) collective-permute-start(f32[448,128]{1,0:T(8,128)S(1)} %get-tuple-element.38), channel_id=1, source_target_pairs={{0,16},{16,32},{32,48},{48,64},{64,80},{80,96},{96,112},{112,0},{1... | collective-permute-start | bytes 688136 | tf_op jit(solution)/shard_map/ppermute | solution.py:622
  23.3 0.0 collective-permute-start.5
  23.3 0.0 copy-done
  23.3 3.0 %collective-permute-done.4.c_low = f32[448,128]{1,0:T(8,128)S(1)} collective-permute-done((f32[448,128]{1,0:T(8,128)S(1)}, f32[448,128]{1,0:T(8,128)S(1)}, u32[]{:S(2)}, u32[]{:S(2)}) %collective-permute-start.4) | collective-permute-done | bytes 229408 | tf_op jit(solution)/shard_map/ppermute | solution.py:622
  26.3 2.5 %collective-permute-done.5.c_high = f32[448,128]{1,0:T(8,128)S(1)} collective-permute-done((f32[448,128]{1,0:T(8,128)S(1)}, f32[448,128]{1,0:T(8,128)S(1)}, u32[]{:S(2)}, u32[]{:S(2)}) %collective-permute-start.5) | collective-permute-done | bytes 229408 | tf_op jit(solution)/shard_map/ppermute | solution.py:622
  28.8 0.0 collective-permute-done.px_low
  28.8 0.0 collective-permute-done.1.px_high
  28.8 16.5 %shard_map.85 = (f32[1152,128]{1,0:T(8,128)S(1)}, f32[16,40,8,128]{3,2,1,0:T(8,128)S(1)}, f32[16,40,8,128]{3,2,1,0:T(8,128)S(1)}, f32[16,40,8,128]{3,2,1,0:T(8,128)S(1)}) custom-call(f32[8,32,8,128]{3,2,1,0:T(8,128)S(1)} %get-tuple-element.29.permit, f32[8,32,8,128]{3,2,1,0:T(8,128)S(1)} %get-tuple-element.30.back, ...), custom_call_target="tpu_custom_call" | custom-call | tf_op jit(solution)/shard_map/pallas_call | solution.py:645
  45.3 22.4 %all_to_all.5 = f32[128,1,1152]{2,1,0:T(1,128)S(1)} all-to-all(f32[128,1,1152]{2,1,0:T(1,128)S(1)} %bitcast.27), channel_id=1, replica_groups=mesh['px'=8,'py'=16] {'px','py'}, dimensions={0} | all-to-all | bytes 1179648 | tf_op jit(solution)/shard_map/all_to_all | solution.py:714
  67.7 5.5 %shard_map.86 = (f32[8,128]{1,0:T(8,128)S(1)}, f32[2048,128]{1,0:T(8,128)S(1)}, f32[1024,128]{1,0:T(8,128)S(1)}, f32[1024,128]{1,0:T(8,128)S(1)}) custom-call(f32[1152,128]{1,0:T(8,128)S(1)} %bitcast.26, f32[16,1024]{1,0:T(8,128)S(1)} %get-tuple-element.28.meta, bf16[1024,4096]{1,0:T(8,128)(2,1)S(1)} %get-tuple-element.40.hot), custom_call_target="tpu_custom_call" | custom-call | tf_op jit(solution)/shard_map/pallas_call | solution.py:645
  73.2 1.2 %collective-permute-start.6 = (f32[1024,128]{1,0:T(8,128)S(1)}, f32[1024,128]{1,0:T(8,128)S(1)}, u32[]{:S(2)}, u32[]{:S(2)}) collective-permute-start(f32[1024,128]{1,0:T(8,128)S(1)} %get-tuple-element.43), channel_id=1, source_target_pairs={{0,16},{16,32},{32,48},{48,64},{64,80},{80,96},{96,112},{112,0},{1... | collective-permute-start | bytes 1572872 | tf_op jit(solution)/shard_map/ppermute | solution.py:622
  74.4 0.0 collective-permute-start.7
  74.5 4.5 %shard_map.87 = (f32[512,128]{1,0:T(8,128)S(1)}, f32[512,128]{1,0:T(8,128)S(1)}) custom-call(f32[8,128]{1,0:T(8,128)S(1)} %get-tuple-element.45.weighted, f32[848,128]{1,0:T(8,128)S(1)} %collective-permute-done.2.py_low, f32[848,128]{1,0:T(8,128)S(1)} %collective-permute-done.3.py_high, f32[448,128]{1,0:T(8,128)S(1)} %collective-permute-done.4.c_low, ...), custom_call_target="tpu_custom_call" | custom-call | bytes 16777216 | tf_op jit(solution)/shard_map/pallas_call | solution.py:645
  79.0 1.6 %collective-permute-done.6.px_low = f32[1024,128]{1,0:T(8,128)S(1)} collective-permute-done((f32[1024,128]{1,0:T(8,128)S(1)}, f32[1024,128]{1,0:T(8,128)S(1)}, u32[]{:S(2)}, u32[]{:S(2)}) %collective-permute-start.6) | collective-permute-done | bytes 524320 | tf_op jit(solution)/shard_map/ppermute | solution.py:622
  80.6 2.8 %collective-permute-done.7.px_high = f32[1024,128]{1,0:T(8,128)S(1)} collective-permute-done((f32[1024,128]{1,0:T(8,128)S(1)}, f32[1024,128]{1,0:T(8,128)S(1)}, u32[]{:S(2)}, u32[]{:S(2)}) %collective-permute-start.7) | collective-permute-done | bytes 524320 | tf_op jit(solution)/shard_map/ppermute | solution.py:622
  83.3 10.4 %shard_map.88 = f32[2048,128]{1,0:T(8,128)} custom-call(f32[2048,128]{1,0:T(8,128)S(1)} %get-tuple-element.42.own, f32[1024,128]{1,0:T(8,128)S(1)} %collective-permute-done.6.px_low, f32[1024,128]{1,0:T(8,128)S(1)} %collective-permute-done.7.px_high, f32[512,128]{1,0:T(8,128)S(1)} %get-tuple-element.46.strips, f32[512,128]{1,0:T(8,128)S(1)} %get-tuple-element.47.corners, ...), custom_call_target="tpu_custom_call" | custom-call | tf_op jit(solution)/shard_map/pallas_call | solution.py:645
  (2 shorter events, 0.0 us)
Async XLA Ops:
  2.8 20.5 %copy-start = (f32[8]{0:T(128)S(1)}, f32[8]{0:T(128)}, u32[]{:S(2)}) copy-start(f32[8]{0:T(128)} %param.15) | copy-start | bytes 100
  2.8 25.9 %collective-permute-start = (f32[2816,128]{1,0:T(8,128)S(1)}, f32[2816,128]{1,0:T(8,128)S(1)}, u32[]{:S(2)}, u32[]{:S(2)}) collective-permute-start(f32[2816,128]{1,0:T(8,128)S(1)} %get-tuple-element.34), channel_id=1, source_target_pairs={{0,16},{16,32},{32,48},{48,64},{64,80},{80,96},{96,112},{112,0},{1... | collective-permute-start | bytes 4325384 | tf_op jit(solution)/shard_map/ppermute | solution.py:622
  5.9 22.9 %collective-permute-start.1 = (f32[2816,128]{1,0:T(8,128)S(1)}, f32[2816,128]{1,0:T(8,128)S(1)}, u32[]{:S(2)}, u32[]{:S(2)}) collective-permute-start(f32[2816,128]{1,0:T(8,128)S(1)} %get-tuple-element.35), channel_id=1, source_target_pairs={{0,112},{16,0},{32,16},{48,32},{64,48},{80,64},{96,80},{112,96},{1... | collective-permute-start | bytes 4325384 | tf_op jit(solution)/shard_map/ppermute | solution.py:622
  5.9 13.1 %collective-permute-start.2 = (f32[848,128]{1,0:T(8,128)S(1)}, f32[848,128]{1,0:T(8,128)S(1)}, u32[]{:S(2)}, u32[]{:S(2)}) collective-permute-start(f32[848,128]{1,0:T(8,128)S(1)} %get-tuple-element.36), channel_id=1, source_target_pairs={{0,1},{1,2},{2,3},{3,4},{4,5},{5,6},{6,7},{7,8},{8,9},{9,10},{10,1... | collective-permute-start | bytes 1302536 | tf_op jit(solution)/shard_map/ppermute | solution.py:622
  7.1 11.9 %collective-permute-start.3 = (f32[848,128]{1,0:T(8,128)S(1)}, f32[848,128]{1,0:T(8,128)S(1)}, u32[]{:S(2)}, u32[]{:S(2)}) collective-permute-start(f32[848,128]{1,0:T(8,128)S(1)} %get-tuple-element.37), channel_id=1, source_target_pairs={{0,15},{1,0},{2,1},{3,2},{4,3},{5,4},{6,5},{7,6},{8,7},{9,8},{10,9... | collective-permute-start | bytes 1302536 | tf_op jit(solution)/shard_map/ppermute | solution.py:622
  19.0 7.3 %collective-permute-start.4 = (f32[448,128]{1,0:T(8,128)S(1)}, f32[448,128]{1,0:T(8,128)S(1)}, u32[]{:S(2)}, u32[]{:S(2)}) collective-permute-start(f32[448,128]{1,0:T(8,128)S(1)} %get-tuple-element.38), channel_id=1, source_target_pairs={{0,16},{16,32},{32,48},{48,64},{64,80},{80,96},{96,112},{112,0},{1... | collective-permute-start | bytes 688136 | tf_op jit(solution)/shard_map/ppermute | solution.py:622
  23.3 5.4 %collective-permute-start.5 = (f32[448,128]{1,0:T(8,128)S(1)}, f32[448,128]{1,0:T(8,128)S(1)}, u32[]{:S(2)}, u32[]{:S(2)}) collective-permute-start(f32[448,128]{1,0:T(8,128)S(1)} %get-tuple-element.39), channel_id=1, source_target_pairs={{0,112},{16,0},{32,16},{48,32},{64,48},{80,64},{96,80},{112,96},{1... | collective-permute-start | bytes 688136 | tf_op jit(solution)/shard_map/ppermute | solution.py:622
  73.2 7.3 %collective-permute-start.6 = (f32[1024,128]{1,0:T(8,128)S(1)}, f32[1024,128]{1,0:T(8,128)S(1)}, u32[]{:S(2)}, u32[]{:S(2)}) collective-permute-start(f32[1024,128]{1,0:T(8,128)S(1)} %get-tuple-element.43), channel_id=1, source_target_pairs={{0,16},{16,32},{32,48},{48,64},{64,80},{80,96},{96,112},{112,0},{1... | collective-permute-start | bytes 1572872 | tf_op jit(solution)/shard_map/ppermute | solution.py:622
  74.4 8.9 %collective-permute-start.7 = (f32[1024,128]{1,0:T(8,128)S(1)}, f32[1024,128]{1,0:T(8,128)S(1)}, u32[]{:S(2)}, u32[]{:S(2)}) collective-permute-start(f32[1024,128]{1,0:T(8,128)S(1)} %get-tuple-element.44), channel_id=1, source_target_pairs={{0,112},{16,0},{32,16},{48,32},{64,48},{80,64},{96,80},{112,96},{1... | collective-permute-start | bytes 1572872 | tf_op jit(solution)/shard_map/ppermute | solution.py:622

commit v6 on v5

--- a/solution.py
+++ b/solution.py
@@ -99,26 +99,43 @@
     return starts
 
 
-def sweep(margin, n, step):
-    def plane(x, carry):
+def early(margin, plane):
+    def step(x, carry):
+        plane(x)
+        return carry
+
+    lax.fori_loop(margin + D, EX - D - margin, step, 0)
+
+
+def late(margin, plane):
+    def step(i, carry):
+        plane(jnp.where(i < D, margin + i, EX - 2 * D - margin + i))
+        return carry
+
+    lax.fori_loop(0, 2 * D, step, 0)
+
+
+def lines(margin, n, step):
+    def plane(x):
         for y in cover(margin, EY - margin, n):
             step(x, y, n)
-        return carry
-
-    lax.fori_loop(margin, EX - margin, plane, 0)
-
-
-def extend(field, own, sides, out, scale):
-    px_low, px_high, py_low, py_high, c_low, c_high = sides
-    middle_x, middle_y = slice(D, D + CX), slice(D, D + CY)
-    out[middle_x, middle_y] = own[...]
+
+    return plane
+
+
+def put_py(field, py_low, py_high, out, scale):
+    for ref, at in ((py_low, 0), (py_high, D + CY)):
+        v = ref[field * HALO_Y : (field + 1) * HALO_Y, :]
+        out[D : D + CX, at : at + D] = v.reshape(CX, D, 8, 128) * scale
+
+
+def put_px(field, sides, out, scale):
+    px_low, px_high, c_low, c_high = sides
+    middle_y = slice(D, D + CY)
     planes = D if field == 0 else D - 1
     for ref, at in ((px_low, D - planes), (px_high, D + CX)):
         v = ref[PX_AT[field] : PX_AT[field] + planes * PLANE, :]
         out[at : at + planes, middle_y] = v.reshape(planes, CY, 8, 128) * scale
-    for ref, at in ((py_low, 0), (py_high, D + CY)):
-        v = ref[field * HALO_Y : (field + 1) * HALO_Y, :]
-        out[middle_x, at : at + D] = v.reshape(CX, D, 8, 128) * scale
     blank = jnp.zeros((D, D, 8, 128), F32)
     for x, ref in ((0, c_low), (D + CX, c_high)):
         for side, y in enumerate((0, D + CY)):
@@ -138,9 +155,58 @@
         qp[at, middle_y] = 1.0 - qp[beside, middle_y]
 
 
+def close_py(out, sign, planes):
+    py, last_y = lax.axis_index("py"), lax.axis_size("py") - 1
+
+    @pl.when(py == 0)
+    def _():
+        out[planes, D - 1] = out[planes, D] * sign
+
+    @pl.when(py == last_y)
+    def _():
+        out[planes, D + CY] = out[planes, D + CY - 1] * sign
+
+
+def first_solve(q, bg, qp, cz, bz, b, y1, y2):
+    def whole(x, y, n):
+        f, acc = side_fluxes(bg, qp, x, y, n)
+        b[x, pl.ds(y, n)] = acc + z_fluxes(f, z_face(qp[x, pl.ds(y, n)]))
+        cz[x, pl.ds(y, n)] = z_face(q[x, pl.ds(y, n)])
+
+    def right_own(x):
+        whole(x, 1, D - 1)
+        whole(x, D + CY, D - 1)
+        for y in cover(D, D + CY, 4):
+            _, acc = side_fluxes(bg, qp, x, y, 4)
+            b[x, pl.ds(y, 4)] = acc + bz[x - D, pl.ds(y - D, 4)]
+
+    def second(x, y, n):
+        f, acc = fluxes(b, q, cz, x, y, n)
+        y1[x, pl.ds(y, n)] = (A2 - A3) * f - A3 * acc
+
+    def third(x, y, n):
+        f, acc = fluxes(y1, q, cz, x, y, n)
+        y2[x, pl.ds(y, n)] = A1 * b[x, pl.ds(y, n)] - f - acc
+
+    return lines(1, 4, whole), right_own, lines(2, 4, second), lines(3, 4, third)
+
+
+def middle_kernel(
+    py_low, py_high, after, bz, q_in, bg_in, qp_in, cz_in, q, bg, qp, cz, b, y1, y2
+):
+    del after, q_in, bg_in, qp_in, cz_in
+    own = slice(D, D + CX)
+    for field, out, scale, sign in ((0, q, 0.5 / HALF, -1.0), (1, bg, 1.0, 1.0), (2, qp, 0.5, -1.0)):
+        put_py(field, py_low, py_high, out, scale)
+        close_py(out, sign, own)
+    _, right_own, second, third = first_solve(q, bg, qp, cz, bz, b, y1, y2)
+    early(1, right_own)
+    early(2, second)
+    early(3, third)
+
+
 def close_edges(out, sign):
-    px, py = lax.axis_index("px"), lax.axis_index("py")
-    last_x, last_y = lax.axis_size("px") - 1, lax.axis_size("py") - 1
+    px, last_x = lax.axis_index("px"), lax.axis_size("px") - 1
 
     @pl.when(px == 0)
     def _():
@@ -150,13 +216,7 @@
     def _():
         out[D + CX] = out[D + CX - 1] * sign
 
-    @pl.when(py == 0)
-    def _():
-        out[:, D - 1] = out[:, D] * sign
-
-    @pl.when(py == last_y)
-    def _():
-        out[:, D + CY] = out[:, D + CY - 1] * sign
+    close_py(out, sign, slice(0, EX))
 
 
 def take_meta(ref, base, out):
@@ -204,81 +264,64 @@
 
 
 def tangent_kernel(
-    permit,
-    back,
-    perturb,
-    own_cz,
-    own_bz,
     px_low,
     px_high,
-    py_low,
-    py_high,
     c_low,
     c_high,
+    bz,
     meta,
     hot,
     weights,
+    q_in,
+    bg_in,
+    qp_in,
+    cz_in,
+    b_in,
+    y1_in,
+    y2_in,
     out,
     q,
     bg,
+    qp,
     cz,
-    qp,
     b,
     y1,
     y2,
+    y3,
     table,
     vals,
 ):
-    sides = (px_low, px_high, py_low, py_high, c_low, c_high)
-    extend(0, permit, sides, q, 0.5 / HALF)
-    extend(1, back, sides, bg, 1.0)
-    extend(2, perturb, sides, qp, 0.5)
+    del q_in, bg_in, qp_in, cz_in, b_in, y1_in, y2_in
+    sides = (px_low, px_high, c_low, c_high)
+    put_px(0, sides, q, 0.5 / HALF)
+    put_px(1, sides, bg, 1.0)
+    put_px(2, sides, qp, 0.5)
     far_planes(sides, bg, qp)
     close_edges(q, -1.0)
     close_edges(qp, -1.0)
     close_edges(bg, 1.0)
-
-    cz[D : D + CX, D : D + CY] = own_cz[...]
-
-    def outer(x, y, n):
-        f, acc = side_fluxes(bg, qp, x, y, n)
-        b[x, pl.ds(y, n)] = acc + z_fluxes(f, z_face(qp[x, pl.ds(y, n)]))
-        cz[x, pl.ds(y, n)] = z_face(q[x, pl.ds(y, n)])
+    right, right_own, second, third = first_solve(q, bg, qp, cz, bz, b, y1, y2)
 
     def outer_planes(i, carry):
-        x = jnp.where(i < D - 1, 1 + i, CX + 1 + i)
-        for y in cover(1, EY - 1, 4):
-            outer(x, y, 4)
+        right(jnp.where(i < D - 1, 1 + i, CX + 1 + i))
         return carry
 
-    def own_planes(x, carry):
-        outer(x, 1, D - 1)
-        outer(x, D + CY, D - 1)
-        for y in cover(D, D + CY, 4):
-            _, acc = side_fluxes(bg, qp, x, y, 4)
-            b[x, pl.ds(y, 4)] = acc + own_bz[x - D, pl.ds(y - D, 4)]
+    def edge_planes(i, carry):
+        right_own(D + i * (CX - 1))
         return carry
 
     lax.fori_loop(0, 2 * (D - 1), outer_planes, 0)
-    lax.fori_loop(D, D + CX, own_planes, 0)
-
-    def second(x, y, n):
-        f, acc = fluxes(b, q, cz, x, y, n)
-        y1[x, pl.ds(y, n)] = (A2 - A3) * f - A3 * acc
-
-    def third(x, y, n):
-        f, acc = fluxes(y1, q, cz, x, y, n)
-        y2[x, pl.ds(y, n)] = A1 * b[x, pl.ds(y, n)] - f - acc
+    lax.fori_loop(0, 2, edge_planes, 0)
+    late(2, second)
+    late(3, third)
 
     def fourth(x, y, n):
         f, acc = fluxes(y2, q, cz, x, y, n)
-        y1[x, pl.ds(y, n)] = A0 * b[x, pl.ds(y, n)] - f - acc
-
-    sweep(2, 4, second)
-    sweep(3, 4, third)
-    sweep(4, 4, fourth)
-
-    flat = y1.reshape(EX * EY * 8, 128)
+        y3[x, pl.ds(y, n)] = A0 * b[x, pl.ds(y, n)] - f - acc
+
+    late(4, lines(4, 4, fourth))
+
+    flat = y3.reshape(EX * EY * 8, 128)
     for x in range(CX):
         for c in range(8):
             v = flat[pl.ds(((x + D) * EY + D) * 8 + c, CY, stride=8), :]
@@ -369,9 +412,43 @@
     scatter(meta, values, lambda n: n >> 10, CX * CY, 2, 512, lhs, keep, hot)
 
 
+def second_solve(src, q, cz, y1, y2, y3):
+    def first(x, y, n):
+        f, acc = fluxes(src, q, cz, x, y, n)
+        y1[x, pl.ds(y, n)] = (A2 - A3) * f - A3 * acc
+
+    def second(x, y, n):
+        f, acc = fluxes(y1, q, cz, x, y, n)
+        y2[x, pl.ds(y, n)] = A1 * src[x, pl.ds(y, n)] - f - acc
+
+    def third(x, y, n):
+        f, acc = fluxes(y2, q, cz, x, y, n)
+        y3[x, pl.ds(y, n)] = A0 * src[x, pl.ds(y, n)] - f - acc
+
+    return lines(1, 4, first), lines(2, 4, second), lines(3, 4, third)
+
+
 def strips_kernel(
-    weighted, py_low, py_high, c_low, c_high, strips, corners, lhs, near_hot, near, values
+    weighted,
+    py_low,
+    py_high,
+    c_low,
+    c_high,
+    own,
+    q,
+    cz,
+    src,
+    y1,
+    y2,
+    y3,
+    lhs,
+    near_hot,
+    near,
+    values,
 ):
+    src[D : D + CX, D : D + CY] = own[...].reshape(CX, CY, 8, 128)
+    flat = src.reshape(EX * EY * 8, 128)
+
     def box(first_x, planes, first_y):
         def rows(node):
             x, y = (node >> 15) - first_x, ((node >> 10) & (CY - 1)) - first_y
@@ -382,68 +459,55 @@
 
     low_x, high_x, low_y, high_y = CX - D, 0, CY - D, 0
     tasks = [
-        (py_low, 3 * HALO_Y, 0, CX, low_y, strips, 0),
-        (py_high, 3 * HALO_Y, 0, CX, high_y, strips, HALO_Y),
+        (py_low, 3 * HALO_Y, D, 0, CX, low_y, 0),
+        (py_high, 3 * HALO_Y, D, 0, CX, high_y, D + CY),
     ]
-    for i, (ref, first_x) in enumerate(((c_low, low_x), (c_high, high_x))):
-        for side, first_y in enumerate((low_y, high_y)):
-            base, to = side * PART + 3 * HALO_C, (2 * i + side) * D * D * 8
-            tasks.append((ref, base, first_x, D, first_y, corners, to))
-    for ref, base, first_x, planes, first_y, out, to in tasks:
+    for ref, x0, first_x in ((c_low, 0, low_x), (c_high, D + CX, high_x)):
+        for side, (y0, first_y) in enumerate(((0, low_y), (D + CY, high_y))):
+            tasks.append((ref, side * PART + 3 * HALO_C, x0, first_x, D, first_y, y0))
+    for ref, base, x0, first_x, planes, first_y, y0 in tasks:
         take_meta(ref, base, near)
         returned(weighted[...], near, values)
         for k in range(4):
             node = near[k : k + 1, :].astype(jnp.int32)
             put_one_hot(node & 255, 256, near_hot, 0, slice(k * 1024, (k + 1) * 1024))
 
-        def keep(t, sums, planes=planes, out=out, to=to):
-            lines = planes * D
+        def keep(t, sums, planes=planes, x0=x0, y0=y0):
             for zq in range(4):
-                for half in range(2):
-                    out[pl.ds(to + zq * 2 + half, lines, stride=8), :] = sums[
-                        zq * lines : (zq + 1) * lines, half * 128 : (half + 1) * 128
-                    ]
+                for x in range(planes):
+                    first = (zq * planes + x) * D
+                    for half in range(2):
+                        flat[
+                            pl.ds(((x + x0) * EY + y0) * 8 + zq * 2 + half, D, stride=8), :
+                        ] = sums[first : first + D, half * 128 : (half + 1) * 128]
 
         rows = box(first_x, planes, first_y)
         scatter(near, values, rows, 4 * planes * D, 1, 256, lhs, keep, near_hot)
 
-
-def adjoint_kernel(own, px_low, px_high, strips, corners, q, bg, cz, out, src, y1, y2):
-    middle_x, middle_y = slice(D, D + CX), slice(D, D + CY)
-    src[middle_x, middle_y] = own[...].reshape(CX, CY, 8, 128)
+    first, second, third = second_solve(src, q, cz, y1, y2, y3)
+    early(1, first)
+    early(2, second)
+    early(3, third)
+
+
+def adjoint_kernel(
+    px_low, px_high, q, bg, cz, src_in, y1_in, y2_in, y3_in, out, src, y1, y2, y3
+):
+    del src_in, y1_in, y2_in, y3_in
     for x, ref in ((0, px_low), (D + CX, px_high)):
-        src[x : x + D, middle_y] = ref[...].reshape(D, CY, 8, 128)
-    for side, y in enumerate((0, D + CY)):
-        v = strips[side * HALO_Y : (side + 1) * HALO_Y, :]
-        src[middle_x, y : y + D] = v.reshape(CX, D, 8, 128)
-        for i, x in enumerate((0, D + CX)):
-            at = (2 * i + side) * D * D * 8
-            v = corners[at : at + D * D * 8, :]
-            src[x : x + D, y : y + D] = v.reshape(D, D, 8, 128)
-
-    def first(x, y, n):
-        f, acc = fluxes(src, q, cz, x, y, n)
-        y1[x, pl.ds(y, n)] = (A2 - A3) * f - A3 * acc
-
-    def second(x, y, n):
-        f, acc = fluxes(y1, q, cz, x, y, n)
-        y2[x, pl.ds(y, n)] = A1 * src[x, pl.ds(y, n)] - f - acc
-
-    def third(x, y, n):
-        f, acc = fluxes(y2, q, cz, x, y, n)
-        y1[x, pl.ds(y, n)] = A0 * src[x, pl.ds(y, n)] - f - acc
-
-    sweep(1, 4, first)
-    sweep(2, 4, second)
-    sweep(3, 4, third)
+        src[x : x + D, D : D + CY] = ref[...].reshape(D, CY, 8, 128)
+    first, second, third = second_solve(src, q, cz, y1, y2, y3)
+    late(1, first)
+    late(2, second)
+    late(3, third)
 
     def last(x, y, n):
-        ae, be = y1[x, pl.ds(y - 1, n + 2)], bg[x, pl.ds(y - 1, n + 2)]
+        ae, be = y3[x, pl.ds(y - 1, n + 2)], bg[x, pl.ds(y - 1, n + 2)]
         a, k = ae[1:-1], be[1:-1]
         sy = (ae[1:] - ae[:-1]) * (be[1:] - be[:-1])
         total = sy[1:] + sy[:-1]
-        total += (y1[x + 1, pl.ds(y, n)] - a) * (bg[x + 1, pl.ds(y, n)] - k)
-        total += (y1[x - 1, pl.ds(y, n)] - a) * (bg[x - 1, pl.ds(y, n)] - k)
+        total += (y3[x + 1, pl.ds(y, n)] - a) * (bg[x + 1, pl.ds(y, n)] - k)
+        total += (y3[x - 1, pl.ds(y, n)] - a) * (bg[x - 1, pl.ds(y, n)] - k)
         sub = lax.broadcasted_iota(jnp.int32, (n, 8, 128), 1)
         end = (sub == 7) & (lane_of(n) == 127)
         sz = jnp.where(end, 0.0, (z_up(a) - a) * (z_up(k) - k))
@@ -453,7 +517,7 @@
             row = (x - D) * (CY // 8) + (yy + i) // 8
             out[pl.ds(row * 64 + (yy + i) % 8, 8, stride=8), :] = total[i]
 
-    sweep(4, 4, last)
+    late(4, lines(4, 4, last))
 
 
 def by_tiles(block):
@@ -586,13 +650,13 @@
 
     def plane(x, carry):
         for y in range(CY):
-            q[x, y] = row_of(permit, x, y) * (0.5 / HALF)
-            bg[x, y] = row_of(back, x, y)
-            qp[x, y] = row_of(perturb, x, y) * 0.5
+            q[x + D, y + D] = row_of(permit, x, y) * (0.5 / HALF)
+            bg[x + D, y + D] = row_of(back, x, y)
+            qp[x + D, y + D] = row_of(perturb, x, y) * 0.5
         for y in range(0, CY, 4):
-            at = pl.ds(y, 4)
-            cz[x, at] = z_face(q[x, at])
-            bz[x, at] = z_fluxes(bg[x, at], z_face(qp[x, at]))
+            at = pl.ds(y + D, 4)
+            cz[x + D, at] = z_face(q[x + D, at])
+            bz[x, pl.ds(y, 4)] = z_fluxes(bg[x + D, at], z_face(qp[x + D, at]))
         return carry
 
     lax.fori_loop(0, CX, plane, 0)
@@ -639,7 +703,7 @@
     def rows(*counts):
         return [jax.ShapeDtypeStruct((n, 128), F32) for n in counts]
 
-    def call(kernel, outs, *args, hbm=0, scratch=(), limit, bytes_accessed=0):
+    def call(kernel, outs, *args, hbm=0, passed=0, at=1, scratch=(), limit, bytes_accessed=0):
         held = [pltpu.with_memory_space_constraint(a, pltpu.HBM) for a in args[:hbm]]
         args = held + list(args[hbm:])
         return pl.pallas_call(
@@ -648,6 +712,7 @@
             in_specs=[pl.BlockSpec(memory_space=pltpu.HBM)] * hbm + vmem(len(args) - hbm),
             out_specs=tuple(vmem(len(outs))),
             scratch_shapes=scratch,
+            input_output_aliases={len(args) - passed + i: at + i for i in range(passed)},
             compiler_params=pltpu.CompilerParams(vmem_limit_bytes=limit * 2**20),
             cost_estimate=pl.CostEstimate(
                 flops=0, bytes_accessed=bytes_accessed, transcendentals=0
@@ -680,9 +745,9 @@
     py_low, py_high = shift(high_y, "py", 1), shift(low_y, "py", -1)
     compact = jax.ShapeDtypeStruct((CX, CY, 8, 128), F32)
     full = jax.ShapeDtypeStruct((EX, EY, 8, 128), F32)
-    own_q, own_bg, own_qp, own_cz, own_bz, hot = call(
+    q, bg, qp, cz, bz, hot = call(
         own_kernel,
-        [compact] * 5 + [jax.ShapeDtypeStruct((CZ, 4096), BF16)],
+        [full] * 4 + [compact, jax.ShapeDtypeStruct((CZ, 4096), BF16)],
         *fields,
         meta,
         hbm=3,
@@ -690,26 +755,46 @@
         limit=10,
         bytes_accessed=8 * 2**20,
     )
-    low_c, high_c = call(corner_kernel, rows(size_c, size_c), py_low, py_high, own_cz, limit=4)
+    low_c, high_c = call(corner_kernel, rows(size_c, size_c), py_low, py_high, bz, limit=4)
     c_low, c_high = shift(high_c, "px", 1), shift(low_c, "px", -1)
-    sides = (px_low, px_high, py_low, py_high, c_low, c_high)
-
+    q, bg, qp, cz, b, y1, y2 = call(
+        middle_kernel,
+        [full] * 7,
+        py_low,
+        py_high,
+        low_c,
+        bz,
+        q,
+        bg,
+        qp,
+        cz,
+        passed=4,
+        at=0,
+        limit=6,
+        bytes_accessed=8 * 2**20,
+    )
     block = pltpu.VMEM((EX, EY, 8, 128), F32)
-    readings, q, bg, cz = call(
+    readings, q, bg, qp, cz, b, y1, y2 = call(
         tangent_kernel,
-        rows(devices * 9) + [full] * 3,
-        own_q,
-        own_bg,
-        own_qp,
-        own_cz,
-        own_bz,
-        *sides,
+        rows(devices * 9) + [full] * 7,
+        px_low,
+        px_high,
+        c_low,
+        c_high,
+        bz,
         meta,
         hot,
         weights,
-        scratch=[block] * 4
-        + [pltpu.VMEM((2 * CX * CY, CZ), BF16), pltpu.VMEM((8, 1024), F32)],
-        limit=20,
+        q,
+        bg,
+        qp,
+        cz,
+        b,
+        y1,
+        y2,
+        passed=7,
+        scratch=[block, pltpu.VMEM((2 * CX * CY, CZ), BF16), pltpu.VMEM((8, 1024), F32)],
+        limit=14,
     )
     got = lax.all_to_all(
         readings.reshape(devices, 1, 9 * 128),
@@ -728,11 +813,17 @@
         limit=18,
     )
     source_low, source_high = shift(high_s, "px", 1), shift(low_s, "px", -1)
-    strips, corners = call(
+    src, y1, y2, y3 = call(
         strips_kernel,
-        rows(2 * HALO_Y, 4 * D * D * 8),
+        [full] * 4,
         weighted,
-        *sides[2:],
+        py_low,
+        py_high,
+        c_low,
+        c_high,
+        own_source,
+        q,
+        cz,
         scratch=[
             pltpu.VMEM((2 * 4 * CX * D, 4096), BF16),
             pltpu.VMEM((256, 4096), BF16),
@@ -740,22 +831,23 @@
             pltpu.VMEM((8, 1024), F32),
         ],
         limit=16,
-        bytes_accessed=16 * 2**20,
+        bytes_accessed=24 * 2**20,
     )
-    (result,) = call(
+    result = call(
         adjoint_kernel,
-        rows(ROWS),
-        own_source,
+        rows(ROWS) + [full] * 4,
         source_low,
         source_high,
-        strips,
-        corners,
         q,
         bg,
         cz,
-        scratch=[block] * 3,
-        limit=16,
-    )
+        src,
+        y1,
+        y2,
+        y3,
+        passed=4,
+        limit=8,
+    )[0]
     return from_tiles(result)
 
 

time: 93.9 us -> 88.6 us (0.944)
  waiting for transfers between devices: 14 us -> 9.15 us
    ppermute x8, waiting for transfers between devices: 14 us -> 9.15 us  [shift(): return lax.ppermute(x, axis, [(i, (i + by) % count) for i in range(count)])]
    pallas_call x7 -> x8, Pallas kernels: 43.8 us -> 43.3 us  [call(): pl.pallas_call(kernel, out_shape=tuple(outs), in_specs=[pl.BlockSpec(memo...]
  transfers between devices with their start and end apart: 8 -> 8, of which waited for: 5 -> 4; matrix products, arithmetic and copies ran while one was open for 0% -> 0% of each run, Pallas kernels for 9% -> 15%
where the time goes in v6:
time: 88.6 us; the launch traced here: 88.4 us
  Pallas kernels  43.3 us (49%)
  blocking collectives  22.4 us (25%)
  starting transfers between devices  13.5 us (15%)
  waiting for transfers between devices  9.15 us (10%)
    pallas_call x8, Pallas kernels, call(): pl.pallas_call(kernel, out_shape=tuple(outs), in_specs=[pl.BlockSpec(memo...  43.3 us
    all_to_all x1, blocking collectives, body(): lax.all_to_all(readings.reshape(devices, 1, 9 * 128), ('px', 'py'), split...  22.4 us
    ppermute x8, starting transfers between devices, shift(): return lax.ppermute(x, axis, [(i, (i + by) % count) for i in range(count)])  13.5 us
    ppermute x8, waiting for transfers between devices, shift(): return lax.ppermute(x, axis, [(i, (i + by) % count) for i in range(count)])  9.15 us
  transfers between devices with their start and end apart: 8, of which 4 were waited for; matrix products, arithmetic and copies ran while one was open for 0% of the time, Pallas kernels for 15%

profile of v6, /device:TPU:1, one launch (start us, length us, event | category | flops | bytes accessed | tf_op | source)
XLA Modules:
  0.0 88.4 jit_solution(12547962218551405132)
XLA Ops:
  0.0 2.8 %shard_map.82 = (f32[2816,128]{1,0:T(8,128)S(1)}, f32[2816,128]{1,0:T(8,128)S(1)}, f32[848,128]{1,0:T(8,128)S(1)}, f32[848,128]{1,0:T(8,128)S(1)}, f32[16,1024]{1,0:T(8,128)S(1)}) custom-call(f32[2048,128]{1,0:T(8,128)} %bitcast.28, f32[2048,128]{1,0:T(8,128)} %bitcast.30, f32[2048,128]{1,0:T(8,128)} %bitcast.32, s32[4,1024]{1,0:T(4,128)} %nodes_hbm.1, ...), custom_call_target="tpu_custom_call" | custom-call | tf_op jit(solution)/shard_map/pallas_call | solution.py:709
  2.8 0.0 copy-start
  2.8 3.0 %collective-permute-start = (f32[2816,128]{1,0:T(8,128)S(1)}, f32[2816,128]{1,0:T(8,128)S(1)}, u32[]{:S(2)}, u32[]{:S(2)}) collective-permute-start(f32[2816,128]{1,0:T(8,128)S(1)} %get-tuple-element.38), channel_id=1, source_target_pairs={{0,16},{16,32},{32,48},{48,64},{64,80},{80,96},{96,112},{112,0},{1... | collective-permute-start | bytes 4325384 | tf_op jit(solution)/shard_map/ppermute | solution.py:686
  5.9 0.0 collective-permute-start.1
  5.9 1.2 %collective-permute-start.2 = (f32[848,128]{1,0:T(8,128)S(1)}, f32[848,128]{1,0:T(8,128)S(1)}, u32[]{:S(2)}, u32[]{:S(2)}) collective-permute-start(f32[848,128]{1,0:T(8,128)S(1)} %get-tuple-element.40), channel_id=1, source_target_pairs={{0,1},{1,2},{2,3},{3,4},{4,5},{5,6},{6,7},{7,8},{8,9},{9,10},{10,1... | collective-permute-start | bytes 1302536 | tf_op jit(solution)/shard_map/ppermute | solution.py:686
  7.1 3.7 %collective-permute-start.3 = (f32[848,128]{1,0:T(8,128)S(1)}, f32[848,128]{1,0:T(8,128)S(1)}, u32[]{:S(2)}, u32[]{:S(2)}) collective-permute-start(f32[848,128]{1,0:T(8,128)S(1)} %get-tuple-element.41), channel_id=1, source_target_pairs={{0,15},{1,0},{2,1},{3,2},{4,3},{5,4},{6,5},{7,6},{8,7},{9,8},{10,9... | collective-permute-start | bytes 1302536 | tf_op jit(solution)/shard_map/ppermute | solution.py:686
  10.8 4.1 %shard_map.83 = (f32[16,40,8,128]{3,2,1,0:T(8,128)S(1)}, f32[16,40,8,128]{3,2,1,0:T(8,128)S(1)}, f32[16,40,8,128]{3,2,1,0:T(8,128)S(1)}, f32[16,40,8,128]{3,2,1,...) custom-call(f32[2048,128]{1,0:T(8,128)} %bitcast.29, f32[2048,128]{1,0:T(8,128)} %bitcast.31, ...), custom_call_target="tpu_custom_call" | custom-call | bytes 8388608 | tf_op jit(solution)/shard_map/pallas_call | solution.py:709
  14.9 4.1 %collective-permute-done.2.py_low = f32[848,128]{1,0:T(8,128)S(1)} collective-permute-done((f32[848,128]{1,0:T(8,128)S(1)}, f32[848,128]{1,0:T(8,128)S(1)}, u32[]{:S(2)}, u32[]{:S(2)}) %collective-permute-start.2) | collective-permute-done | bytes 434208 | tf_op jit(solution)/shard_map/ppermute | solution.py:686
  19.0 0.0 collective-permute-done.3.py_high
  19.0 4.3 %collective-permute-start.4 = (f32[448,128]{1,0:T(8,128)S(1)}, f32[448,128]{1,0:T(8,128)S(1)}, u32[]{:S(2)}, u32[]{:S(2)}) collective-permute-start(f32[448,128]{1,0:T(8,128)S(1)} %get-tuple-element.44), channel_id=1, source_target_pairs={{0,16},{16,32},{32,48},{48,64},{64,80},{80,96},{96,112},{112,0},{1... | collective-permute-start | bytes 688136 | tf_op jit(solution)/shard_map/ppermute | solution.py:686
  23.3 0.0 collective-permute-start.5
  23.3 0.0 copy-done
  23.3 2.3 %shard_map.85 = (f32[16,40,8,128]{3,2,1,0:T(8,128)S(1)}, f32[16,40,8,128]{3,2,1,0:T(8,128)S(1)}, f32[16,40,8,128]{3,2,1,0:T(8,128)S(1)}, f32[16,40,8,128]{3,2,1,...) custom-call(f32[848,128]{1,0:T(8,128)S(1)} %collective-permute-done., ...), custom_call_target="tpu_custom_call", output_to_operand_aliasing={{0}: (4, {}), {1}: (5, {}), {2}: (6, {}), {3}: (7, {})} | custom-call | bytes 8388608 | tf_op jit(solution)/shard_map/pallas_call | solution.py:709
  25.6 0.7 collective-permute-done.4.c_low
  26.3 2.5 %collective-permute-done.5.c_high = f32[448,128]{1,0:T(8,128)S(1)} collective-permute-done((f32[448,128]{1,0:T(8,128)S(1)}, f32[448,128]{1,0:T(8,128)S(1)}, u32[]{:S(2)}, u32[]{:S(2)}) %collective-permute-start.5) | collective-permute-done | bytes 229408 | tf_op jit(solution)/shard_map/ppermute | solution.py:686
  28.8 0.0 collective-permute-done.px_low
  28.8 0.0 collective-permute-done.1.px_high
  28.8 13.9 %shard_map.86 = (f32[1152,128]{1,0:T(8,128)S(1)}, f32[16,40,8,128]{3,2,1,0:T(8,128)S(1)}, f32[16,40,8,128]{3,2,1,0:T(8,128)S(1)}, f32[16,40,8,128]{3,2,1,0:T(8,1...) custom-call(f32[2816,128]{1,0:T(8,128)S(1)} %collective-permute-done, ...), custom_call_target="tpu_custom_call", output_to_operand_aliasing={{1}: (8, {}), {2}: (9, {}), {3}: (10, {}), {4}: (11, {}), {... | custom-call | tf_op jit(solution)/shard_map/pallas_call | solution.py:709
  42.7 22.4 %all_to_all.5 = f32[128,1,1152]{2,1,0:T(1,128)S(1)} all-to-all(f32[128,1,1152]{2,1,0:T(1,128)S(1)} %bitcast.27), channel_id=1, replica_groups=mesh['px'=8,'py'=16] {'px','py'}, dimensions={0} | all-to-all | bytes 1179648 | tf_op jit(solution)/shard_map/all_to_all | solution.py:799
  65.1 5.5 %shard_map.87 = (f32[8,128]{1,0:T(8,128)S(1)}, f32[2048,128]{1,0:T(8,128)S(1)}, f32[1024,128]{1,0:T(8,128)S(1)}, f32[1024,128]{1,0:T(8,128)S(1)}) custom-call(f32[1152,128]{1,0:T(8,128)S(1)} %bitcast.26, f32[16,1024]{1,0:T(8,128)S(1)} %get-tuple-element.42.meta, bf16[1024,4096]{1,0:T(8,128)(2,1)S(1)} %get-tuple-element.46.hot), custom_call_target="tpu_custom_call" | custom-call | tf_op jit(solution)/shard_map/pallas_call | solution.py:709
  70.6 1.2 %collective-permute-start.6 = (f32[1024,128]{1,0:T(8,128)S(1)}, f32[1024,128]{1,0:T(8,128)S(1)}, u32[]{:S(2)}, u32[]{:S(2)}) collective-permute-start(f32[1024,128]{1,0:T(8,128)S(1)} %get-tuple-element.59), channel_id=1, source_target_pairs={{0,16},{16,32},{32,48},{48,64},{64,80},{80,96},{96,112},{112,0},{1... | collective-permute-start | bytes 1572872 | tf_op jit(solution)/shard_map/ppermute | solution.py:686
  71.8 0.0 collective-permute-start.7
  71.8 7.0 %shard_map.88 = (f32[16,40,8,128]{3,2,1,0:T(8,128)S(1)}, f32[16,40,8,128]{3,2,1,0:T(8,128)S(1)}, f32[16,40,8,128]{3,2,1,0:T(8,128)S(1)}, f32[16,40,8,128]{3,2,1,0:T(8,128)S(1)}) custom-call(f32[8,128]{1,0:T(8,128)S(1)} %get-tuple-element.64.weighted, f32[848,128]{1,0:T(8,128)S(1)} %collective-permute-done.2.py_low, ...), custom_call_target="tpu_custom_call" | custom-call | bytes 25165824 | tf_op jit(solution)/shard_map/pallas_call | solution.py:709
  78.9 0.0 collective-permute-done.6.px_low
  78.9 1.8 %collective-permute-done.7.px_high = f32[1024,128]{1,0:T(8,128)S(1)} collective-permute-done((f32[1024,128]{1,0:T(8,128)S(1)}, f32[1024,128]{1,0:T(8,128)S(1)}, u32[]{:S(2)}, u32[]{:S(2)}) %collective-permute-start.7) | collective-permute-done | bytes 524320 | tf_op jit(solution)/shard_map/ppermute | solution.py:686
  80.7 7.7 %shard_map.89 = (f32[2048,128]{1,0:T(8,128)}, f32[16,40,8,128]{3,2,1,0:T(8,128)S(1)}, f32[16,40,8,128]{3,2,1,0:T(8,128)S(1)}, f32[16,40,8,128]{3,2,1,0:T(8,128)S(1)}, f32[16,40,8,128]{3,2,1,0:T(8,128)S(1)}) custom-call(f32[1024,128]{1,0:T(8,128)S(1)} %collective-permute-done.6.px_low, ...), custom_call_target="tpu_custom_call", output_to_operand_aliasing={{1}: (5, {}), {2}: (6, {}), {3}: (7, {}), {4}: (8, {})} | custom-call | tf_op jit(solution)/shard_map/pallas_call | solution.py:709
  (2 shorter events, 0.0 us)
Async XLA Ops:
  2.8 20.5 %copy-start = (f32[8]{0:T(128)S(1)}, f32[8]{0:T(128)}, u32[]{:S(2)}) copy-start(f32[8]{0:T(128)} %param.15) | copy-start | bytes 100
  2.8 25.9 %collective-permute-start = (f32[2816,128]{1,0:T(8,128)S(1)}, f32[2816,128]{1,0:T(8,128)S(1)}, u32[]{:S(2)}, u32[]{:S(2)}) collective-permute-start(f32[2816,128]{1,0:T(8,128)S(1)} %get-tuple-element.38), channel_id=1, source_target_pairs={{0,16},{16,32},{32,48},{48,64},{64,80},{80,96},{96,112},{112,0},{1... | collective-permute-start | bytes 4325384 | tf_op jit(solution)/shard_map/ppermute | solution.py:686
  5.9 22.9 %collective-permute-start.1 = (f32[2816,128]{1,0:T(8,128)S(1)}, f32[2816,128]{1,0:T(8,128)S(1)}, u32[]{:S(2)}, u32[]{:S(2)}) collective-permute-start(f32[2816,128]{1,0:T(8,128)S(1)} %get-tuple-element.39), channel_id=1, source_target_pairs={{0,112},{16,0},{32,16},{48,32},{64,48},{80,64},{96,80},{112,96},{1... | collective-permute-start | bytes 4325384 | tf_op jit(solution)/shard_map/ppermute | solution.py:686
  5.9 13.1 %collective-permute-start.2 = (f32[848,128]{1,0:T(8,128)S(1)}, f32[848,128]{1,0:T(8,128)S(1)}, u32[]{:S(2)}, u32[]{:S(2)}) collective-permute-start(f32[848,128]{1,0:T(8,128)S(1)} %get-tuple-element.40), channel_id=1, source_target_pairs={{0,1},{1,2},{2,3},{3,4},{4,5},{5,6},{6,7},{7,8},{8,9},{9,10},{10,1... | collective-permute-start | bytes 1302536 | tf_op jit(solution)/shard_map/ppermute | solution.py:686
  7.1 11.9 %collective-permute-start.3 = (f32[848,128]{1,0:T(8,128)S(1)}, f32[848,128]{1,0:T(8,128)S(1)}, u32[]{:S(2)}, u32[]{:S(2)}) collective-permute-start(f32[848,128]{1,0:T(8,128)S(1)} %get-tuple-element.41), channel_id=1, source_target_pairs={{0,15},{1,0},{2,1},{3,2},{4,3},{5,4},{6,5},{7,6},{8,7},{9,8},{10,9... | collective-permute-start | bytes 1302536 | tf_op jit(solution)/shard_map/ppermute | solution.py:686
  19.0 7.3 %collective-permute-start.4 = (f32[448,128]{1,0:T(8,128)S(1)}, f32[448,128]{1,0:T(8,128)S(1)}, u32[]{:S(2)}, u32[]{:S(2)}) collective-permute-start(f32[448,128]{1,0:T(8,128)S(1)} %get-tuple-element.44), channel_id=1, source_target_pairs={{0,16},{16,32},{32,48},{48,64},{64,80},{80,96},{96,112},{112,0},{1... | collective-permute-start | bytes 688136 | tf_op jit(solution)/shard_map/ppermute | solution.py:686
  23.3 5.4 %collective-permute-start.5 = (f32[448,128]{1,0:T(8,128)S(1)}, f32[448,128]{1,0:T(8,128)S(1)}, u32[]{:S(2)}, u32[]{:S(2)}) collective-permute-start(f32[448,128]{1,0:T(8,128)S(1)} %get-tuple-element.45.after), channel_id=1, source_target_pairs={{0,112},{16,0},{32,16},{48,32},{64,48},{80,64},{96,80},{112,96},{1... | collective-permute-start | bytes 688136 | tf_op jit(solution)/shard_map/ppermute | solution.py:686
  70.6 8.3 %collective-permute-start.6 = (f32[1024,128]{1,0:T(8,128)S(1)}, f32[1024,128]{1,0:T(8,128)S(1)}, u32[]{:S(2)}, u32[]{:S(2)}) collective-permute-start(f32[1024,128]{1,0:T(8,128)S(1)} %get-tuple-element.59), channel_id=1, source_target_pairs={{0,16},{16,32},{32,48},{48,64},{64,80},{80,96},{96,112},{112,0},{1... | collective-permute-start | bytes 1572872 | tf_op jit(solution)/shard_map/ppermute | solution.py:686
  71.8 8.9 %collective-permute-start.7 = (f32[1024,128]{1,0:T(8,128)S(1)}, f32[1024,128]{1,0:T(8,128)S(1)}, u32[]{:S(2)}, u32[]{:S(2)}) collective-permute-start(f32[1024,128]{1,0:T(8,128)S(1)} %get-tuple-element.60), channel_id=1, source_target_pairs={{0,112},{16,0},{32,16},{48,32},{64,48},{80,64},{96,80},{112,96},{1... | collective-permute-start | bytes 1572872 | tf_op jit(solution)/shard_map/ppermute | solution.py:686

commit v7 on v6

--- a/solution.py
+++ b/solution.py
@@ -26,6 +26,8 @@
 HALO_C = len(CELLS) * 8
 META = 80
 PART = 3 * HALO_C + META
+AHEAD_META = 6 * HALO_C
+AHEAD = AHEAD_META + META
 F32 = jnp.float32
 BF16 = jnp.bfloat16
 
@@ -430,8 +432,8 @@
 
 def strips_kernel(
     weighted,
-    py_low,
-    py_high,
+    a_low,
+    a_high,
     c_low,
     c_high,
     own,
@@ -459,8 +461,8 @@
 
     low_x, high_x, low_y, high_y = CX - D, 0, CY - D, 0
     tasks = [
-        (py_low, 3 * HALO_Y, D, 0, CX, low_y, 0),
-        (py_high, 3 * HALO_Y, D, 0, CX, high_y, D + CY),
+        (a_low, AHEAD_META, D, 0, CX, low_y, 0),
+        (a_high, AHEAD_META, D, 0, CX, high_y, D + CY),
     ]
     for ref, x0, first_x in ((c_low, 0, low_x), (c_high, D + CX, high_x)):
         for side, (y0, first_y) in enumerate(((0, low_y), (D + CY, high_y))):
@@ -550,6 +552,8 @@
     sensor_hbm,
     low_x,
     high_x,
+    low_a,
+    high_a,
     low_y,
     high_y,
     meta,
@@ -581,7 +585,8 @@
     meta[8:9, :] = owner[...].astype(F32)
     meta[9:10, :] = sensor[...].astype(F32)
     meta[10:16, :] = jnp.zeros((6, 1024), F32)
-    for out, at in ((low_y, 3 * HALO_Y), (high_y, 3 * HALO_Y)):
+    at = AHEAD_META
+    for out in (low_a, high_a):
         for c in range(8):
             lanes = slice(c * 128, (c + 1) * 128)
             out[at + c * 8 : at + c * 8 + 8, :] = meta[0:8, lanes]
@@ -605,6 +610,11 @@
                 at = pl.ds(field * HALO_Y + (x * D + y) * 8, 8)
                 low_y[at, :] = row_of(ref, x, y)
                 high_y[at, :] = row_of(ref, x, y + CY - D)
+        for i, (dx, dy) in enumerate(CELLS):
+            for part, x in enumerate((dx - 1, CX - dx)):
+                at = (3 * part + field) * HALO_C + i * 8
+                low_a[at : at + 8, :] = row_of(ref, x, dy - 1)
+                high_a[at : at + 8, :] = row_of(ref, x, CY - dy)
 
     def flux(y, carry):
         for out, near, far in ((low_x, D - 2, D - 1), (high_x, CX - D + 1, CX - D)):
@@ -621,17 +631,22 @@
     back_hbm,
     perturb_hbm,
     meta,
+    low_in,
+    high_in,
     q,
     bg,
     qp,
     cz,
     bz,
     hot,
+    low_y,
+    high_y,
     permit,
     back,
     perturb,
     sems,
 ):
+    del low_in, high_in, low_y, high_y
     pairs = ((permit_hbm, permit), (back_hbm, back), (perturb_hbm, perturb))
     copies = [pltpu.make_async_copy(a, b, sems.at[i]) for i, (a, b) in enumerate(pairs)]
     for copy in copies:
@@ -662,19 +677,13 @@
     lax.fori_loop(0, CX, plane, 0)
 
 
-def corner_kernel(py_low, py_high, after, low, high):
+def corner_kernel(from_low, from_high, after, low, high):
     del after
-    for side, ref in enumerate((py_low, py_high)):
-        for field in range(3):
-            for i, (dx, dy) in enumerate(CELLS):
-                y = D - dy if side == 0 else dy - 1
-                at = side * PART + field * HALO_C + i * 8
-                for out, x in ((low, dx - 1), (high, CX - dx)):
-                    first = field * HALO_Y + (x * D + y) * 8
-                    out[at : at + 8, :] = ref[first : first + 8, :]
-        at = side * PART + 3 * HALO_C
-        low[at : at + META, :] = ref[3 * HALO_Y :, :]
-        high[at : at + META, :] = ref[3 * HALO_Y :, :]
+    for side, ref in enumerate((from_low, from_high)):
+        for part, out in enumerate((low, high)):
+            at, first = side * PART, part * 3 * HALO_C
+            out[at : at + 3 * HALO_C, :] = ref[first : first + 3 * HALO_C, :]
+            out[at + 3 * HALO_C : at + PART, :] = ref[AHEAD_META:, :]
 
 
 def vmem(count):
@@ -719,12 +728,12 @@
             ),
         )(*args)
 
-    size_x, size_y, size_c = PX_ROWS, 3 * HALO_Y + META, 2 * PART
+    size_x, size_y, size_c = PX_ROWS, 3 * HALO_Y, 2 * PART
     raw = [pltpu.VMEM((ROWS, 128), F32)] * 3
     table = jax.ShapeDtypeStruct((16, 1024), F32)
-    low_x, high_x, low_y, high_y, meta = call(
+    low_x, high_x, low_a, high_a, low_y, high_y, meta = call(
         pack_kernel,
-        rows(size_x, size_x, size_y, size_y) + [table],
+        rows(size_x, size_x, AHEAD, AHEAD, size_y, size_y) + [table],
         *fields,
         probe_nodes,
         probe_weights,
@@ -742,20 +751,25 @@
         limit=6,
     )
     px_low, px_high = shift(high_x, "px", 1), shift(low_x, "px", -1)
-    py_low, py_high = shift(high_y, "py", 1), shift(low_y, "py", -1)
+    a_low, a_high = shift(high_a, "py", 1), shift(low_a, "py", -1)
     compact = jax.ShapeDtypeStruct((CX, CY, 8, 128), F32)
     full = jax.ShapeDtypeStruct((EX, EY, 8, 128), F32)
-    q, bg, qp, cz, bz, hot = call(
+    q, bg, qp, cz, bz, hot, low_y, high_y = call(
         own_kernel,
-        [full] * 4 + [compact, jax.ShapeDtypeStruct((CZ, 4096), BF16)],
+        [full] * 4 + [compact, jax.ShapeDtypeStruct((CZ, 4096), BF16)] + rows(size_y, size_y),
         *fields,
         meta,
+        low_y,
+        high_y,
         hbm=3,
+        passed=2,
+        at=6,
         scratch=raw + [pltpu.SemaphoreType.DMA((3,))],
         limit=10,
         bytes_accessed=8 * 2**20,
     )
-    low_c, high_c = call(corner_kernel, rows(size_c, size_c), py_low, py_high, bz, limit=4)
+    py_low, py_high = shift(high_y, "py", 1), shift(low_y, "py", -1)
+    low_c, high_c = call(corner_kernel, rows(size_c, size_c), a_low, a_high, bz, limit=4)
     c_low, c_high = shift(high_c, "px", 1), shift(low_c, "px", -1)
     q, bg, qp, cz, b, y1, y2 = call(
         middle_kernel,
@@ -817,8 +831,8 @@
         strips_kernel,
         [full] * 4,
         weighted,
-        py_low,
-        py_high,
+        a_low,
+        a_high,
         c_low,
         c_high,
         own_source,

time: 88.6 us -> 102 us (1.15)
  waiting for transfers between devices: 9.15 us -> 15.3 us
  blocking collectives: 22.4 us -> 27 us
  starting transfers between devices: 13.5 us -> 16.4 us
    ppermute x8 -> x10, waiting for transfers between devices: 9.15 us -> 15.3 us  [shift(): return lax.ppermute(x, axis, [(i, (i + by) % count) for i in range(count)])]
    all_to_all x1, blocking collectives: 22.4 us -> 27 us  [body(): lax.all_to_all(readings.reshape(devices, 1, 9 * 128), ('px', 'py'), split...]
    ppermute x8 -> x10, starting transfers between devices: 13.5 us -> 16.4 us  [shift(): return lax.ppermute(x, axis, [(i, (i + by) % count) for i in range(count)])]
  transfers between devices with their start and end apart: 8 -> 10, of which waited for: 4 -> 4; matrix products, arithmetic and copies ran while one was open for 0% -> 0% of each run, Pallas kernels for 15% -> 13%
where the time goes in v7:
time: 102 us
  Pallas kernels  43.3 us (42%)
  blocking collectives  27 us (26%)
  starting transfers between devices  16.4 us (16%)
  waiting for transfers between devices  15.3 us (15%)
    pallas_call x8, Pallas kernels, call(): pl.pallas_call(kernel, out_shape=tuple(outs), in_specs=[pl.BlockSpec(memo...  43.3 us
    all_to_all x1, blocking collectives, body(): lax.all_to_all(readings.reshape(devices, 1, 9 * 128), ('px', 'py'), split...  27 us
    ppermute x10, starting transfers between devices, shift(): return lax.ppermute(x, axis, [(i, (i + by) % count) for i in range(count)])  16.4 us
    ppermute x10, waiting for transfers between devices, shift(): return lax.ppermute(x, axis, [(i, (i + by) % count) for i in range(count)])  15.3 us
  transfers between devices with their start and end apart: 10, of which 4 were waited for; matrix products, arithmetic and copies ran while one was open for 0% of the time, Pallas kernels for 13%

profile of v7, /device:TPU:1, one launch (start us, length us, event | category | flops | bytes accessed | tf_op | source)
XLA Modules:
  0.0 102.1 jit_solution(16751743396343340828)
XLA Ops:
  0.0 2.8 %shard_map.82 = (f32[2816,128]{1,0:T(8,128)S(1)}, f32[2816,128]{1,0:T(8,128)S(1)}, f32[368,128]{1,0:T(8,128)S(1)}, f32[368,128]{1,0:T(8,128)S(1)}, f32[768,128]{...) custom-call(f32[2048,128]{1,0:T(8,128)} %bitcast.28, f32[2048,128]{1,0:T(8,128)} %bitcast.30, ...), custom_call_target="tpu_custom_call" | custom-call | tf_op jit(solution)/shard_map/pallas_call | solution.py:718
  2.8 3.0 %collective-permute-start = (f32[2816,128]{1,0:T(8,128)S(1)}, f32[2816,128]{1,0:T(8,128)S(1)}, u32[]{:S(2)}, u32[]{:S(2)}) collective-permute-start(f32[2816,128]{1,0:T(8,128)S(1)} %get-tuple-element.42), channel_id=1, source_target_pairs={{0,16},{16,32},{32,48},{48,64},{64,80},{80,96},{96,112},{112,0},{1... | collective-permute-start | bytes 4325384 | tf_op jit(solution)/shard_map/ppermute | solution.py:695
  5.9 0.0 collective-permute-start.1
  5.9 0.0 copy-start
  5.9 4.1 %shard_map.83 = (f32[16,40,8,128]{3,2,1,0:T(8,128)S(1)}, f32[16,40,8,128]{3,2,1,0:T(8,128)S(1)}, f32[16,40,8,128]{3,2,1,0:T(8,128)S(1)}, f32[16,40,8,128]{3,2,1,...) custom-call(f32[2048,128]{1,0:T(8,128)} %bitcast.29, ...), custom_call_target="tpu_custom_call", output_to_operand_aliasing={{6}: (4, {}), {7}: (5, {})} | custom-call | bytes 8388608 | tf_op jit(solution)/shard_map/pallas_call | solution.py:718
  10.0 1.3 %collective-permute-start.6 = (f32[768,128]{1,0:T(8,128)S(1)}, f32[768,128]{1,0:T(8,128)S(1)}, u32[]{:S(2)}, u32[]{:S(2)}) collective-permute-start(f32[768,128]{1,0:T(8,128)S(1)} %get-tuple-element.53), channel_id=1, source_target_pairs={{0,1},{1,2},{2,3},{3,4},{4,5},{5,6},{6,7},{7,8},{8,9},{9,10},{10,1... | collective-permute-start | bytes 1179656 | tf_op jit(solution)/shard_map/ppermute | solution.py:695
  11.2 1.2 %collective-permute-start.2 = (f32[368,128]{1,0:T(8,128)S(1)}, f32[368,128]{1,0:T(8,128)S(1)}, u32[]{:S(2)}, u32[]{:S(2)}) collective-permute-start(f32[368,128]{1,0:T(8,128)S(1)} %get-tuple-element.44), channel_id=1, source_target_pairs={{0,1},{1,2},{2,3},{3,4},{4,5},{5,6},{6,7},{7,8},{8,9},{9,10},{10,1... | collective-permute-start | bytes 565256 | tf_op jit(solution)/shard_map/ppermute | solution.py:695
  12.4 3.6 %collective-permute-start.3 = (f32[368,128]{1,0:T(8,128)S(1)}, f32[368,128]{1,0:T(8,128)S(1)}, u32[]{:S(2)}, u32[]{:S(2)}) collective-permute-start(f32[368,128]{1,0:T(8,128)S(1)} %get-tuple-element.45), channel_id=1, source_target_pairs={{0,15},{1,0},{2,1},{3,2},{4,3},{5,4},{6,5},{7,6},{8,7},{9,8},{10,9... | collective-permute-start | bytes 565256 | tf_op jit(solution)/shard_map/ppermute | solution.py:695
  16.0 10.3 %collective-permute-done.2.from_low.a_low = f32[368,128]{1,0:T(8,128)S(1)} collective-permute-done((f32[368,128]{1,0:T(8,128)S(1)}, f32[368,128]{1,0:T(8,128)S(1)}, u32[]{:S(2)}, u32[]{:S(2)}) %collective-permute-start.2) | collective-permute-done | bytes 188448 | tf_op jit(solution)/shard_map/ppermute | solution.py:695
  26.3 1.3 %collective-permute-start.7 = (f32[768,128]{1,0:T(8,128)S(1)}, f32[768,128]{1,0:T(8,128)S(1)}, u32[]{:S(2)}, u32[]{:S(2)}) collective-permute-start(f32[768,128]{1,0:T(8,128)S(1)} %get-tuple-element.54), channel_id=1, source_target_pairs={{0,15},{1,0},{2,1},{3,2},{4,3},{5,4},{6,5},{7,6},{8,7},{9,8},{10,9... | collective-permute-start | bytes 1179656 | tf_op jit(solution)/shard_map/ppermute | solution.py:695
  27.6 0.0 collective-permute-done.3.from_high.a_high
  27.7 4.7 %collective-permute-start.4 = (f32[448,128]{1,0:T(8,128)S(1)}, f32[448,128]{1,0:T(8,128)S(1)}, u32[]{:S(2)}, u32[]{:S(2)}) collective-permute-start(f32[448,128]{1,0:T(8,128)S(1)} %get-tuple-element.50), channel_id=1, source_target_pairs={{0,16},{16,32},{32,48},{48,64},{64,80},{80,96},{96,112},{112,0},{1... | collective-permute-start | bytes 688136 | tf_op jit(solution)/shard_map/ppermute | solution.py:695
  32.4 0.0 collective-permute-done.6.py_low
  32.4 0.0 collective-permute-start.5
  32.4 0.0 copy-done
  32.4 1.8 %collective-permute-done.7.py_high = f32[768,128]{1,0:T(8,128)S(1)} collective-permute-done((f32[768,128]{1,0:T(8,128)S(1)}, f32[768,128]{1,0:T(8,128)S(1)}, u32[]{:S(2)}, u32[]{:S(2)}) %collective-permute-start.7) | collective-permute-done | bytes 393248 | tf_op jit(solution)/shard_map/ppermute | solution.py:695
  34.2 2.2 %shard_map.85 = (f32[16,40,8,128]{3,2,1,0:T(8,128)S(1)}, f32[16,40,8,128]{3,2,1,0:T(8,128)S(1)}, f32[16,40,8,128]{3,2,1,0:T(8,128)S(1)}, f32[16,40,8,128]{3,2,1,...) custom-call(f32[768,128]{1,0:T(8,128)S(1)} %collective-permute-done., ...), custom_call_target="tpu_custom_call", output_to_operand_aliasing={{0}: (4, {}), {1}: (5, {}), {2}: (6, {}), {3}: (7, {})} | custom-call | bytes 8388608 | tf_op jit(solution)/shard_map/pallas_call | solution.py:718
  36.4 0.0 collective-permute-done.4.c_low
  36.4 1.4 %collective-permute-done.5.c_high = f32[448,128]{1,0:T(8,128)S(1)} collective-permute-done((f32[448,128]{1,0:T(8,128)S(1)}, f32[448,128]{1,0:T(8,128)S(1)}, u32[]{:S(2)}, u32[]{:S(2)}) %collective-permute-start.5) | collective-permute-done | bytes 229408 | tf_op jit(solution)/shard_map/ppermute | solution.py:695
  37.8 0.0 collective-permute-done.px_low
  37.8 0.0 collective-permute-done.1.px_high
  37.8 13.9 %shard_map.86 = (f32[1152,128]{1,0:T(8,128)S(1)}, f32[16,40,8,128]{3,2,1,0:T(8,128)S(1)}, f32[16,40,8,128]{3,2,1,0:T(8,128)S(1)}, f32[16,40,8,128]{3,2,1,0:T(8,1...) custom-call(f32[2816,128]{1,0:T(8,128)S(1)} %collective-permute-done, ...), custom_call_target="tpu_custom_call", output_to_operand_aliasing={{1}: (8, {}), {2}: (9, {}), {3}: (10, {}), {4}: (11, {}), {... | custom-call | tf_op jit(solution)/shard_map/pallas_call | solution.py:718
  51.7 27.0 %all_to_all.5 = f32[128,1,1152]{2,1,0:T(1,128)S(1)} all-to-all(f32[128,1,1152]{2,1,0:T(1,128)S(1)} %bitcast.27), channel_id=1, replica_groups=mesh['px'=8,'py'=16] {'px','py'}, dimensions={0} | all-to-all | bytes 1179648 | tf_op jit(solution)/shard_map/all_to_all | solution.py:813
  78.8 5.5 %shard_map.87 = (f32[8,128]{1,0:T(8,128)S(1)}, f32[2048,128]{1,0:T(8,128)S(1)}, f32[1024,128]{1,0:T(8,128)S(1)}, f32[1024,128]{1,0:T(8,128)S(1)}) custom-call(f32[1152,128]{1,0:T(8,128)S(1)} %bitcast.26, f32[16,1024]{1,0:T(8,128)S(1)} %get-tuple-element.46.meta, bf16[1024,4096]{1,0:T(8,128)(2,1)S(1)} %get-tuple-element.52.hot), custom_call_target="tpu_custom_call" | custom-call | tf_op jit(solution)/shard_map/pallas_call | solution.py:718
  84.3 1.2 %collective-permute-start.8 = (f32[1024,128]{1,0:T(8,128)S(1)}, f32[1024,128]{1,0:T(8,128)S(1)}, u32[]{:S(2)}, u32[]{:S(2)}) collective-permute-start(f32[1024,128]{1,0:T(8,128)S(1)} %get-tuple-element.67), channel_id=1, source_target_pairs={{0,16},{16,32},{32,48},{48,64},{64,80},{80,96},{96,112},{112,0},{1... | collective-permute-start | bytes 1572872 | tf_op jit(solution)/shard_map/ppermute | solution.py:695
  85.5 0.0 collective-permute-start.9
  85.5 7.0 %shard_map.88 = (f32[16,40,8,128]{3,2,1,0:T(8,128)S(1)}, f32[16,40,8,128]{3,2,1,0:T(8,128)S(1)}, f32[16,40,8,128]{3,2,1,0:T(8,128)S(1)}, f32[16,40,8,128]{3,2,1,0:T(8,128)S(1)}) custom-call(f32[8,128]{1,0:T(8,128)S(1)} %get-tuple-element.72.weighted, f32[368,128]{1,0:T(8,128)S(1)} %collective-permute-done.2.from_low.a_low, ...), custom_call_target="tpu_custom_call" | custom-call | bytes 25165824 | tf_op jit(solution)/shard_map/pallas_call | solution.py:718
  92.5 0.0 collective-permute-done.8.px_low
  92.5 1.8 %collective-permute-done.9.px_high = f32[1024,128]{1,0:T(8,128)S(1)} collective-permute-done((f32[1024,128]{1,0:T(8,128)S(1)}, f32[1024,128]{1,0:T(8,128)S(1)}, u32[]{:S(2)}, u32[]{:S(2)}) %collective-permute-start.9) | collective-permute-done | bytes 524320 | tf_op jit(solution)/shard_map/ppermute | solution.py:695
  94.4 7.7 %shard_map.89 = (f32[2048,128]{1,0:T(8,128)}, f32[16,40,8,128]{3,2,1,0:T(8,128)S(1)}, f32[16,40,8,128]{3,2,1,0:T(8,128)S(1)}, f32[16,40,8,128]{3,2,1,0:T(8,128)S(1)}, f32[16,40,8,128]{3,2,1,0:T(8,128)S(1)}) custom-call(f32[1024,128]{1,0:T(8,128)S(1)} %collective-permute-done.8.px_low, ...), custom_call_target="tpu_custom_call", output_to_operand_aliasing={{1}: (5, {}), {2}: (6, {}), {3}: (7, {}), {4}: (8, {})} | custom-call | tf_op jit(solution)/shard_map/pallas_call | solution.py:718
  (2 shorter events, 0.0 us)
Async XLA Ops:
  2.8 35.0 %collective-permute-start = (f32[2816,128]{1,0:T(8,128)S(1)}, f32[2816,128]{1,0:T(8,128)S(1)}, u32[]{:S(2)}, u32[]{:S(2)}) collective-permute-start(f32[2816,128]{1,0:T(8,128)S(1)} %get-tuple-element.42), channel_id=1, source_target_pairs={{0,16},{16,32},{32,48},{48,64},{64,80},{80,96},{96,112},{112,0},{1... | collective-permute-start | bytes 4325384 | tf_op jit(solution)/shard_map/ppermute | solution.py:695
  5.9 32.0 %collective-permute-start.1 = (f32[2816,128]{1,0:T(8,128)S(1)}, f32[2816,128]{1,0:T(8,128)S(1)}, u32[]{:S(2)}, u32[]{:S(2)}) collective-permute-start(f32[2816,128]{1,0:T(8,128)S(1)} %get-tuple-element.43), channel_id=1, source_target_pairs={{0,112},{16,0},{32,16},{48,32},{64,48},{80,64},{96,80},{112,96},{1... | collective-permute-start | bytes 4325384 | tf_op jit(solution)/shard_map/ppermute | solution.py:695
  5.9 26.5 %copy-start = (f32[8]{0:T(128)S(1)}, f32[8]{0:T(128)}, u32[]{:S(2)}) copy-start(f32[8]{0:T(128)} %param.15) | copy-start | bytes 100
  10.0 22.4 %collective-permute-start.6 = (f32[768,128]{1,0:T(8,128)S(1)}, f32[768,128]{1,0:T(8,128)S(1)}, u32[]{:S(2)}, u32[]{:S(2)}) collective-permute-start(f32[768,128]{1,0:T(8,128)S(1)} %get-tuple-element.53), channel_id=1, source_target_pairs={{0,1},{1,2},{2,3},{3,4},{4,5},{5,6},{6,7},{7,8},{8,9},{9,10},{10,1... | collective-permute-start | bytes 1179656 | tf_op jit(solution)/shard_map/ppermute | solution.py:695
  11.2 15.1 %collective-permute-start.2 = (f32[368,128]{1,0:T(8,128)S(1)}, f32[368,128]{1,0:T(8,128)S(1)}, u32[]{:S(2)}, u32[]{:S(2)}) collective-permute-start(f32[368,128]{1,0:T(8,128)S(1)} %get-tuple-element.44), channel_id=1, source_target_pairs={{0,1},{1,2},{2,3},{3,4},{4,5},{5,6},{6,7},{7,8},{8,9},{9,10},{10,1... | collective-permute-start | bytes 565256 | tf_op jit(solution)/shard_map/ppermute | solution.py:695
  12.4 15.2 %collective-permute-start.3 = (f32[368,128]{1,0:T(8,128)S(1)}, f32[368,128]{1,0:T(8,128)S(1)}, u32[]{:S(2)}, u32[]{:S(2)}) collective-permute-start(f32[368,128]{1,0:T(8,128)S(1)} %get-tuple-element.45), channel_id=1, source_target_pairs={{0,15},{1,0},{2,1},{3,2},{4,3},{5,4},{6,5},{7,6},{8,7},{9,8},{10,9... | collective-permute-start | bytes 565256 | tf_op jit(solution)/shard_map/ppermute | solution.py:695
  26.3 7.9 %collective-permute-start.7 = (f32[768,128]{1,0:T(8,128)S(1)}, f32[768,128]{1,0:T(8,128)S(1)}, u32[]{:S(2)}, u32[]{:S(2)}) collective-permute-start(f32[768,128]{1,0:T(8,128)S(1)} %get-tuple-element.54), channel_id=1, source_target_pairs={{0,15},{1,0},{2,1},{3,2},{4,3},{5,4},{6,5},{7,6},{8,7},{9,8},{10,9... | collective-permute-start | bytes 1179656 | tf_op jit(solution)/shard_map/ppermute | solution.py:695
  27.7 8.8 %collective-permute-start.4 = (f32[448,128]{1,0:T(8,128)S(1)}, f32[448,128]{1,0:T(8,128)S(1)}, u32[]{:S(2)}, u32[]{:S(2)}) collective-permute-start(f32[448,128]{1,0:T(8,128)S(1)} %get-tuple-element.50), channel_id=1, source_target_pairs={{0,16},{16,32},{32,48},{48,64},{64,80},{80,96},{96,112},{112,0},{1... | collective-permute-start | bytes 688136 | tf_op jit(solution)/shard_map/ppermute | solution.py:695
  32.4 5.4 %collective-permute-start.5 = (f32[448,128]{1,0:T(8,128)S(1)}, f32[448,128]{1,0:T(8,128)S(1)}, u32[]{:S(2)}, u32[]{:S(2)}) collective-permute-start(f32[448,128]{1,0:T(8,128)S(1)} %get-tuple-element.51.after), channel_id=1, source_target_pairs={{0,112},{16,0},{32,16},{48,32},{64,48},{80,64},{96,80},{112,96},{1... | collective-permute-start | bytes 688136 | tf_op jit(solution)/shard_map/ppermute | solution.py:695
  84.3 8.3 %collective-permute-start.8 = (f32[1024,128]{1,0:T(8,128)S(1)}, f32[1024,128]{1,0:T(8,128)S(1)}, u32[]{:S(2)}, u32[]{:S(2)}) collective-permute-start(f32[1024,128]{1,0:T(8,128)S(1)} %get-tuple-element.67), channel_id=1, source_target_pairs={{0,16},{16,32},{32,48},{48,64},{64,80},{80,96},{96,112},{112,0},{1... | collective-permute-start | bytes 1572872 | tf_op jit(solution)/shard_map/ppermute | solution.py:695
  85.5 8.9 %collective-permute-start.9 = (f32[1024,128]{1,0:T(8,128)S(1)}, f32[1024,128]{1,0:T(8,128)S(1)}, u32[]{:S(2)}, u32[]{:S(2)}) collective-permute-start(f32[1024,128]{1,0:T(8,128)S(1)} %get-tuple-element.68), channel_id=1, source_target_pairs={{0,112},{16,0},{32,16},{48,32},{64,48},{80,64},{96,80},{112,96},{1... | collective-permute-start | bytes 1572872 | tf_op jit(solution)/shard_map/ppermute | solution.py:695

commit v8 on v6

--- a/solution.py
+++ b/solution.py
@@ -449,40 +449,58 @@
     src[D : D + CX, D : D + CY] = own[...].reshape(CX, CY, 8, 128)
     flat = src.reshape(EX * EY * 8, 128)
 
-    def box(first_x, planes, first_y):
-        def rows(node):
-            x, y = (node >> 15) - first_x, ((node >> 10) & (CY - 1)) - first_y
-            good = (x >= 0) & (x < planes) & (y >= 0) & (y < D)
-            return jnp.where(good, (((node >> 8) & 3) * planes + x) * D + y, -1)
-
-        return rows
-
-    low_x, high_x, low_y, high_y = CX - D, 0, CY - D, 0
-    tasks = [
-        (py_low, 3 * HALO_Y, D, 0, CX, low_y, 0),
-        (py_high, 3 * HALO_Y, D, 0, CX, high_y, D + CY),
-    ]
-    for ref, x0, first_x in ((c_low, 0, low_x), (c_high, D + CX, high_x)):
-        for side, (y0, first_y) in enumerate(((0, low_y), (D + CY, high_y))):
-            tasks.append((ref, side * PART + 3 * HALO_C, x0, first_x, D, first_y, y0))
-    for ref, base, x0, first_x, planes, first_y, y0 in tasks:
-        take_meta(ref, base, near)
-        returned(weighted[...], near, values)
+    def columns(count):
         for k in range(4):
             node = near[k : k + 1, :].astype(jnp.int32)
-            put_one_hot(node & 255, 256, near_hot, 0, slice(k * 1024, (k + 1) * 1024))
-
-        def keep(t, sums, planes=planes, x0=x0, y0=y0):
+            put_one_hot(node & (count - 1), count, near_hot, 0, slice(k * 1024, (k + 1) * 1024))
+
+    for ref, y0, first_y in ((py_low, 0, CY - D), (py_high, D + CY, 0)):
+        take_meta(ref, 3 * HALO_Y, near)
+        returned(weighted[...], near, values)
+        columns(256)
+
+        def rows(node, first_y=first_y):
+            x, y = node >> 15, ((node >> 10) & (CY - 1)) - first_y
+            good = (y >= 0) & (y < D)
+            return jnp.where(good, (((node >> 8) & 3) * CX + x) * D + y, -1)
+
+        def keep(t, sums, y0=y0):
             for zq in range(4):
-                for x in range(planes):
-                    first = (zq * planes + x) * D
+                for x in range(CX):
+                    first = (zq * CX + x) * D
                     for half in range(2):
                         flat[
-                            pl.ds(((x + x0) * EY + y0) * 8 + zq * 2 + half, D, stride=8), :
+                            pl.ds(((x + D) * EY + y0) * 8 + zq * 2 + half, D, stride=8), :
                         ] = sums[first : first + D, half * 128 : (half + 1) * 128]
 
-        rows = box(first_x, planes, first_y)
-        scatter(near, values, rows, 4 * planes * D, 1, 256, lhs, keep, near_hot)
+        scatter(near, values, rows, 4 * CX * D, 1, 256, lhs, keep, near_hot)
+
+    for ref, x_low in ((c_low, True), (c_high, False)):
+        for side, y_low in enumerate((True, False)):
+            take_meta(ref, side * PART + 3 * HALO_C, near)
+            returned(weighted[...], near, values)
+            columns(128)
+
+            def rows(node, x_low=x_low, y_low=y_low):
+                x, y = node >> 15, (node >> 10) & (CY - 1)
+                dx = CX - x if x_low else x + 1
+                dy = CY - y if y_low else y + 1
+                cell = jnp.where(dx == 1, dy - 1, jnp.where(dx == 2, dy + 2, 5))
+                return jnp.where(dx + dy <= D, ((node >> 7) & 7) * len(CELLS) + cell, -1)
+
+            def keep(t, sums, x_low=x_low, y_low=y_low):
+                x0, y0 = 0 if x_low else D + CX, 0 if y_low else D + CY
+                src[x0 : x0 + D, y0 : y0 + D] = jnp.zeros((D, D, 8, 128), F32)
+                for i, (dx, dy) in enumerate(CELLS):
+                    x = D - dx if x_low else D + CX + dx - 1
+                    y = D - dy if y_low else D + CY + dy - 1
+                    for c in range(8):
+                        row = c * len(CELLS) + i
+                        flat[(x * EY + y) * 8 + c : (x * EY + y) * 8 + c + 1, :] = sums[
+                            row : row + 1, :
+                        ]
+
+            scatter(near, values, rows, 8 * len(CELLS), 1, 128, lhs, keep, near_hot)
 
     first, second, third = second_solve(src, q, cz, y1, y2, y3)
     early(1, first)
@@ -491,7 +509,7 @@
 
 
 def adjoint_kernel(
-    px_low, px_high, q, bg, cz, src_in, y1_in, y2_in, y3_in, out, src, y1, y2, y3
+    px_low, px_high, q, bg, cz, src_in, y1_in, y2_in, y3_in, out_hbm, src, y1, y2, y3, out, sems
 ):
     del src_in, y1_in, y2_in, y3_in
     for x, ref in ((0, px_low), (D + CX, px_high)):
@@ -517,7 +535,20 @@
             row = (x - D) * (CY // 8) + (yy + i) // 8
             out[pl.ds(row * 64 + (yy + i) % 8, 8, stride=8), :] = total[i]
 
-    late(4, lines(4, 4, last))
+    def leave(x):
+        i = x - D
+        at = pl.ds(pl.multiple_of(i * PLANE, PLANE), PLANE)
+        return pltpu.make_async_copy(out.at[at], out_hbm.at[at], sems.at[i])
+
+    compute = lines(4, 4, last)
+
+    def plane(x):
+        compute(x)
+        leave(x).start()
+
+    late(4, plane)
+    for x in range(D, D + CX):
+        leave(x).wait()
 
 
 def by_tiles(block):
@@ -703,14 +734,16 @@
     def rows(*counts):
         return [jax.ShapeDtypeStruct((n, 128), F32) for n in counts]
 
-    def call(kernel, outs, *args, hbm=0, passed=0, at=1, scratch=(), limit, bytes_accessed=0):
+    def call(kernel, outs, *args, hbm=0, away=0, passed=0, at=1, scratch=(), limit, bytes_accessed=0):
         held = [pltpu.with_memory_space_constraint(a, pltpu.HBM) for a in args[:hbm]]
         args = held + list(args[hbm:])
         return pl.pallas_call(
             kernel,
             out_shape=tuple(outs),
             in_specs=[pl.BlockSpec(memory_space=pltpu.HBM)] * hbm + vmem(len(args) - hbm),
-            out_specs=tuple(vmem(len(outs))),
+            out_specs=tuple(
+                [pl.BlockSpec(memory_space=pl.ANY)] * away + vmem(len(outs) - away)
+            ),
             scratch_shapes=scratch,
             input_output_aliases={len(args) - passed + i: at + i for i in range(passed)},
             compiler_params=pltpu.CompilerParams(vmem_limit_bytes=limit * 2**20),
@@ -846,6 +879,8 @@
         y2,
         y3,
         passed=4,
+        away=1,
+        scratch=[pltpu.VMEM((ROWS, 128), F32), pltpu.SemaphoreType.DMA((CX,))],
         limit=8,
     )[0]
     return from_tiles(result)

time: 88.6 us -> 88.4 us (level)
  Pallas kernels: 43.3 us -> 42.3 us
    pallas_call x8, Pallas kernels: 43.3 us -> 42.3 us  [call(): pl.pallas_call(kernel, out_shape=tuple(outs), in_specs=[pl.BlockSpec(memo...]
  transfers between devices with their start and end apart: 8 -> 8, of which waited for: 4 -> 4; matrix products, arithmetic and copies ran while one was open for 0% -> 0% of each run, Pallas kernels for 15% -> 14%
where the time goes in v8:
time: 88.4 us; the launch traced here: 88.2 us
  Pallas kernels  42.3 us (48%)
  blocking collectives  22.4 us (25%)
  starting transfers between devices  13.5 us (15%)
  waiting for transfers between devices  9.92 us (11%)
    pallas_call x8, Pallas kernels, call(): pl.pallas_call(kernel, out_shape=tuple(outs), in_specs=[pl.BlockSpec(memo...  42.3 us
    all_to_all x1, blocking collectives, body(): lax.all_to_all(readings.reshape(devices, 1, 9 * 128), ('px', 'py'), split...  22.4 us
    ppermute x8, starting transfers between devices, shift(): return lax.ppermute(x, axis, [(i, (i + by) % count) for i in range(count)])  13.5 us
    ppermute x8, waiting for transfers between devices, shift(): return lax.ppermute(x, axis, [(i, (i + by) % count) for i in range(count)])  9.92 us
  transfers between devices with their start and end apart: 8, of which 4 were waited for; matrix products, arithmetic and copies ran while one was open for 0% of the time, Pallas kernels for 14%

profile of v8, /device:TPU:1, one launch (start us, length us, event | category | flops | bytes accessed | tf_op | source)
XLA Modules:
  0.0 88.2 jit_solution(16550092772305665571)
XLA Ops:
  0.0 2.8 %shard_map.82 = (f32[2816,128]{1,0:T(8,128)S(1)}, f32[2816,128]{1,0:T(8,128)S(1)}, f32[848,128]{1,0:T(8,128)S(1)}, f32[848,128]{1,0:T(8,128)S(1)}, f32[16,1024]{1,0:T(8,128)S(1)}) custom-call(f32[2048,128]{1,0:T(8,128)} %bitcast.28, f32[2048,128]{1,0:T(8,128)} %bitcast.30, f32[2048,128]{1,0:T(8,128)} %bitcast.32, s32[4,1024]{1,0:T(4,128)} %nodes_hbm.1, ...), custom_call_target="tpu_custom_call" | custom-call | tf_op jit(solution)/shard_map/pallas_call | solution.py:740
  2.8 0.0 copy-start
  2.8 3.0 %collective-permute-start = (f32[2816,128]{1,0:T(8,128)S(1)}, f32[2816,128]{1,0:T(8,128)S(1)}, u32[]{:S(2)}, u32[]{:S(2)}) collective-permute-start(f32[2816,128]{1,0:T(8,128)S(1)} %get-tuple-element.38), channel_id=1, source_target_pairs={{0,16},{16,32},{32,48},{48,64},{64,80},{80,96},{96,112},{112,0},{1... | collective-permute-start | bytes 4325384 | tf_op jit(solution)/shard_map/ppermute | solution.py:717
  5.9 0.0 collective-permute-start.1
  5.9 1.2 %collective-permute-start.2 = (f32[848,128]{1,0:T(8,128)S(1)}, f32[848,128]{1,0:T(8,128)S(1)}, u32[]{:S(2)}, u32[]{:S(2)}) collective-permute-start(f32[848,128]{1,0:T(8,128)S(1)} %get-tuple-element.40), channel_id=1, source_target_pairs={{0,1},{1,2},{2,3},{3,4},{4,5},{5,6},{6,7},{7,8},{8,9},{9,10},{10,1... | collective-permute-start | bytes 1302536 | tf_op jit(solution)/shard_map/ppermute | solution.py:717
  7.1 3.7 %collective-permute-start.3 = (f32[848,128]{1,0:T(8,128)S(1)}, f32[848,128]{1,0:T(8,128)S(1)}, u32[]{:S(2)}, u32[]{:S(2)}) collective-permute-start(f32[848,128]{1,0:T(8,128)S(1)} %get-tuple-element.41), channel_id=1, source_target_pairs={{0,15},{1,0},{2,1},{3,2},{4,3},{5,4},{6,5},{7,6},{8,7},{9,8},{10,9... | collective-permute-start | bytes 1302536 | tf_op jit(solution)/shard_map/ppermute | solution.py:717
  10.8 4.1 %shard_map.83 = (f32[16,40,8,128]{3,2,1,0:T(8,128)S(1)}, f32[16,40,8,128]{3,2,1,0:T(8,128)S(1)}, f32[16,40,8,128]{3,2,1,0:T(8,128)S(1)}, f32[16,40,8,128]{3,2,1,...) custom-call(f32[2048,128]{1,0:T(8,128)} %bitcast.29, f32[2048,128]{1,0:T(8,128)} %bitcast.31, ...), custom_call_target="tpu_custom_call" | custom-call | bytes 8388608 | tf_op jit(solution)/shard_map/pallas_call | solution.py:740
  14.9 4.1 %collective-permute-done.2.py_low = f32[848,128]{1,0:T(8,128)S(1)} collective-permute-done((f32[848,128]{1,0:T(8,128)S(1)}, f32[848,128]{1,0:T(8,128)S(1)}, u32[]{:S(2)}, u32[]{:S(2)}) %collective-permute-start.2) | collective-permute-done | bytes 434208 | tf_op jit(solution)/shard_map/ppermute | solution.py:717
  19.0 0.0 collective-permute-done.3.py_high
  19.0 4.3 %collective-permute-start.4 = (f32[448,128]{1,0:T(8,128)S(1)}, f32[448,128]{1,0:T(8,128)S(1)}, u32[]{:S(2)}, u32[]{:S(2)}) collective-permute-start(f32[448,128]{1,0:T(8,128)S(1)} %get-tuple-element.44), channel_id=1, source_target_pairs={{0,16},{16,32},{32,48},{48,64},{64,80},{80,96},{96,112},{112,0},{1... | collective-permute-start | bytes 688136 | tf_op jit(solution)/shard_map/ppermute | solution.py:717
  23.3 0.0 collective-permute-start.5
  23.3 0.0 copy-done
  23.3 2.3 %shard_map.85 = (f32[16,40,8,128]{3,2,1,0:T(8,128)S(1)}, f32[16,40,8,128]{3,2,1,0:T(8,128)S(1)}, f32[16,40,8,128]{3,2,1,0:T(8,128)S(1)}, f32[16,40,8,128]{3,2,1,...) custom-call(f32[848,128]{1,0:T(8,128)S(1)} %collective-permute-done., ...), custom_call_target="tpu_custom_call", output_to_operand_aliasing={{0}: (4, {}), {1}: (5, {}), {2}: (6, {}), {3}: (7, {})} | custom-call | bytes 8388608 | tf_op jit(solution)/shard_map/pallas_call | solution.py:740
  25.6 0.7 collective-permute-done.4.c_low
  26.3 2.5 %collective-permute-done.5.c_high = f32[448,128]{1,0:T(8,128)S(1)} collective-permute-done((f32[448,128]{1,0:T(8,128)S(1)}, f32[448,128]{1,0:T(8,128)S(1)}, u32[]{:S(2)}, u32[]{:S(2)}) %collective-permute-start.5) | collective-permute-done | bytes 229408 | tf_op jit(solution)/shard_map/ppermute | solution.py:717
  28.8 0.0 collective-permute-done.px_low
  28.8 0.0 collective-permute-done.1.px_high
  28.8 13.9 %shard_map.86 = (f32[1152,128]{1,0:T(8,128)S(1)}, f32[16,40,8,128]{3,2,1,0:T(8,128)S(1)}, f32[16,40,8,128]{3,2,1,0:T(8,128)S(1)}, f32[16,40,8,128]{3,2,1,0:T(8,1...) custom-call(f32[2816,128]{1,0:T(8,128)S(1)} %collective-permute-done, ...), custom_call_target="tpu_custom_call", output_to_operand_aliasing={{1}: (8, {}), {2}: (9, {}), {3}: (10, {}), {4}: (11, {}), {... | custom-call | tf_op jit(solution)/shard_map/pallas_call | solution.py:740
  42.7 22.4 %all_to_all.5 = f32[128,1,1152]{2,1,0:T(1,128)S(1)} all-to-all(f32[128,1,1152]{2,1,0:T(1,128)S(1)} %bitcast.27), channel_id=1, replica_groups=mesh['px'=8,'py'=16] {'px','py'}, dimensions={0} | all-to-all | bytes 1179648 | tf_op jit(solution)/shard_map/all_to_all | solution.py:832
  65.1 5.5 %shard_map.87 = (f32[8,128]{1,0:T(8,128)S(1)}, f32[2048,128]{1,0:T(8,128)S(1)}, f32[1024,128]{1,0:T(8,128)S(1)}, f32[1024,128]{1,0:T(8,128)S(1)}) custom-call(f32[1152,128]{1,0:T(8,128)S(1)} %bitcast.26, f32[16,1024]{1,0:T(8,128)S(1)} %get-tuple-element.42.meta, bf16[1024,4096]{1,0:T(8,128)(2,1)S(1)} %get-tuple-element.46.hot), custom_call_target="tpu_custom_call" | custom-call | tf_op jit(solution)/shard_map/pallas_call | solution.py:740
  70.6 1.2 %collective-permute-start.6 = (f32[1024,128]{1,0:T(8,128)S(1)}, f32[1024,128]{1,0:T(8,128)S(1)}, u32[]{:S(2)}, u32[]{:S(2)}) collective-permute-start(f32[1024,128]{1,0:T(8,128)S(1)} %get-tuple-element.59), channel_id=1, source_target_pairs={{0,16},{16,32},{32,48},{48,64},{64,80},{80,96},{96,112},{112,0},{1... | collective-permute-start | bytes 1572872 | tf_op jit(solution)/shard_map/ppermute | solution.py:717
  71.8 0.0 collective-permute-start.7
  71.8 6.3 %shard_map.88 = (f32[16,40,8,128]{3,2,1,0:T(8,128)S(1)}, f32[16,40,8,128]{3,2,1,0:T(8,128)S(1)}, f32[16,40,8,128]{3,2,1,0:T(8,128)S(1)}, f32[16,40,8,128]{3,2,1,0:T(8,128)S(1)}) custom-call(f32[8,128]{1,0:T(8,128)S(1)} %get-tuple-element.64.weighted, f32[848,128]{1,0:T(8,128)S(1)} %collective-permute-done.2.py_low, ...), custom_call_target="tpu_custom_call" | custom-call | bytes 25165824 | tf_op jit(solution)/shard_map/pallas_call | solution.py:740
  78.1 0.0 collective-permute-done.6.px_low
  78.1 2.6 %collective-permute-done.7.px_high = f32[1024,128]{1,0:T(8,128)S(1)} collective-permute-done((f32[1024,128]{1,0:T(8,128)S(1)}, f32[1024,128]{1,0:T(8,128)S(1)}, u32[]{:S(2)}, u32[]{:S(2)}) %collective-permute-start.7) | collective-permute-done | bytes 524320 | tf_op jit(solution)/shard_map/ppermute | solution.py:717
  80.7 7.4 %shard_map.89 = (f32[2048,128]{1,0:T(8,128)}, f32[16,40,8,128]{3,2,1,0:T(8,128)S(1)}, f32[16,40,8,128]{3,2,1,0:T(8,128)S(1)}, f32[16,40,8,128]{3,2,1,0:T(8,128)S(1)}, f32[16,40,8,128]{3,2,1,0:T(8,128)S(1)}) custom-call(f32[1024,128]{1,0:T(8,128)S(1)} %collective-permute-done.6.px_low, ...), custom_call_target="tpu_custom_call", output_to_operand_aliasing={{1}: (5, {}), {2}: (6, {}), {3}: (7, {}), {4}: (8, {})} | custom-call | tf_op jit(solution)/shard_map/pallas_call | solution.py:740
  (2 shorter events, 0.0 us)
Async XLA Ops:
  2.8 20.5 %copy-start = (f32[8]{0:T(128)S(1)}, f32[8]{0:T(128)}, u32[]{:S(2)}) copy-start(f32[8]{0:T(128)} %param.15) | copy-start | bytes 100
  2.8 25.9 %collective-permute-start = (f32[2816,128]{1,0:T(8,128)S(1)}, f32[2816,128]{1,0:T(8,128)S(1)}, u32[]{:S(2)}, u32[]{:S(2)}) collective-permute-start(f32[2816,128]{1,0:T(8,128)S(1)} %get-tuple-element.38), channel_id=1, source_target_pairs={{0,16},{16,32},{32,48},{48,64},{64,80},{80,96},{96,112},{112,0},{1... | collective-permute-start | bytes 4325384 | tf_op jit(solution)/shard_map/ppermute | solution.py:717
  5.9 22.9 %collective-permute-start.1 = (f32[2816,128]{1,0:T(8,128)S(1)}, f32[2816,128]{1,0:T(8,128)S(1)}, u32[]{:S(2)}, u32[]{:S(2)}) collective-permute-start(f32[2816,128]{1,0:T(8,128)S(1)} %get-tuple-element.39), channel_id=1, source_target_pairs={{0,112},{16,0},{32,16},{48,32},{64,48},{80,64},{96,80},{112,96},{1... | collective-permute-start | bytes 4325384 | tf_op jit(solution)/shard_map/ppermute | solution.py:717
  5.9 13.1 %collective-permute-start.2 = (f32[848,128]{1,0:T(8,128)S(1)}, f32[848,128]{1,0:T(8,128)S(1)}, u32[]{:S(2)}, u32[]{:S(2)}) collective-permute-start(f32[848,128]{1,0:T(8,128)S(1)} %get-tuple-element.40), channel_id=1, source_target_pairs={{0,1},{1,2},{2,3},{3,4},{4,5},{5,6},{6,7},{7,8},{8,9},{9,10},{10,1... | collective-permute-start | bytes 1302536 | tf_op jit(solution)/shard_map/ppermute | solution.py:717
  7.1 11.9 %collective-permute-start.3 = (f32[848,128]{1,0:T(8,128)S(1)}, f32[848,128]{1,0:T(8,128)S(1)}, u32[]{:S(2)}, u32[]{:S(2)}) collective-permute-start(f32[848,128]{1,0:T(8,128)S(1)} %get-tuple-element.41), channel_id=1, source_target_pairs={{0,15},{1,0},{2,1},{3,2},{4,3},{5,4},{6,5},{7,6},{8,7},{9,8},{10,9... | collective-permute-start | bytes 1302536 | tf_op jit(solution)/shard_map/ppermute | solution.py:717
  19.0 7.3 %collective-permute-start.4 = (f32[448,128]{1,0:T(8,128)S(1)}, f32[448,128]{1,0:T(8,128)S(1)}, u32[]{:S(2)}, u32[]{:S(2)}) collective-permute-start(f32[448,128]{1,0:T(8,128)S(1)} %get-tuple-element.44), channel_id=1, source_target_pairs={{0,16},{16,32},{32,48},{48,64},{64,80},{80,96},{96,112},{112,0},{1... | collective-permute-start | bytes 688136 | tf_op jit(solution)/shard_map/ppermute | solution.py:717
  23.3 5.4 %collective-permute-start.5 = (f32[448,128]{1,0:T(8,128)S(1)}, f32[448,128]{1,0:T(8,128)S(1)}, u32[]{:S(2)}, u32[]{:S(2)}) collective-permute-start(f32[448,128]{1,0:T(8,128)S(1)} %get-tuple-element.45.after), channel_id=1, source_target_pairs={{0,112},{16,0},{32,16},{48,32},{64,48},{80,64},{96,80},{112,96},{1... | collective-permute-start | bytes 688136 | tf_op jit(solution)/shard_map/ppermute | solution.py:717
  70.6 7.5 %collective-permute-start.6 = (f32[1024,128]{1,0:T(8,128)S(1)}, f32[1024,128]{1,0:T(8,128)S(1)}, u32[]{:S(2)}, u32[]{:S(2)}) collective-permute-start(f32[1024,128]{1,0:T(8,128)S(1)} %get-tuple-element.59), channel_id=1, source_target_pairs={{0,16},{16,32},{32,48},{48,64},{64,80},{80,96},{96,112},{112,0},{1... | collective-permute-start | bytes 1572872 | tf_op jit(solution)/shard_map/ppermute | solution.py:717
  71.8 8.9 %collective-permute-start.7 = (f32[1024,128]{1,0:T(8,128)S(1)}, f32[1024,128]{1,0:T(8,128)S(1)}, u32[]{:S(2)}, u32[]{:S(2)}) collective-permute-start(f32[1024,128]{1,0:T(8,128)S(1)} %get-tuple-element.60), channel_id=1, source_target_pairs={{0,112},{16,0},{32,16},{48,32},{64,48},{80,64},{96,80},{112,96},{1... | collective-permute-start | bytes 1572872 | tf_op jit(solution)/shard_map/ppermute | solution.py:717

commit v9 on v8

--- a/solution.py
+++ b/solution.py
@@ -65,11 +65,12 @@
     return jnp.where(lane_of(f.shape[0]) == 0, pltpu.roll(r, 1, 1), r)
 
 
+def z_end(n):
+    return (lax.broadcasted_iota(jnp.int32, (n, 8, 128), 1) == 7) & (lane_of(n) == 127)
+
+
 def z_face(q):
-    n = q.shape[0]
-    sub = lax.broadcasted_iota(jnp.int32, (n, 8, 128), 1)
-    last = (sub == 7) & (lane_of(n) == 127)
-    return jnp.where(last, 0.0, q + z_up(q))
+    return jnp.where(z_end(q.shape[0]), 0.0, q + z_up(q))
 
 
 def side_fluxes(src, q, x, y, n):
@@ -330,19 +331,18 @@
             table[CX * CY + x * CY : CX * CY + (x + 1) * CY, c * 128 : (c + 1) * 128] = low
 
     vals[...] = jnp.zeros_like(vals)
-    wide = 512
-
-    def gather(i, carry):
-        k, lanes = i // 2, pl.ds(pl.multiple_of((i % 2) * wide, wide), wide)
-        node = meta[pl.ds(k, 1), lanes].astype(jnp.int32)
-        found = dot(table[...], hot[:, pl.ds(pl.multiple_of(i * wide, wide), wide)], ((1,), (0,)))
+
+    def gather(k, carry):
+        node = meta[pl.ds(k, 1), :].astype(jnp.int32)
+        lanes = pl.ds(pl.multiple_of(k * 1024, 1024), 1024)
+        found = dot(table[...], hot[:, lanes], ((1,), (0,)))
         found = found[: CX * CY] + found[CX * CY :]
         at = lax.broadcasted_iota(jnp.int32, found.shape, 0)
         found = jnp.sum(jnp.where(at == node >> 10, found, 0.0), axis=0, keepdims=True)
-        vals[0:1, lanes] += meta[pl.ds(k + 4, 1), lanes] * found
+        vals[0:1, :] += meta[pl.ds(k + 4, 1), :] * found
         return carry
 
-    lax.fori_loop(0, 8, gather, 0)
+    lax.fori_loop(0, 4, gather, 0)
 
     owner, sensor = meta[8:9, :].astype(jnp.int32), meta[9:10, :].astype(jnp.int32)
     at = lax.broadcasted_iota(jnp.int32, (8, 1024), 0)
@@ -509,7 +509,7 @@
 
 
 def adjoint_kernel(
-    px_low, px_high, q, bg, cz, src_in, y1_in, y2_in, y3_in, out_hbm, src, y1, y2, y3, out, sems
+    px_low, px_high, q, bg, cz, dz, src_in, y1_in, y2_in, y3_in, out_hbm, src, y1, y2, y3, out, sems
 ):
     del src_in, y1_in, y2_in, y3_in
     for x, ref in ((0, px_low), (D + CX, px_high)):
@@ -526,9 +526,7 @@
         total = sy[1:] + sy[:-1]
         total += (y3[x + 1, pl.ds(y, n)] - a) * (bg[x + 1, pl.ds(y, n)] - k)
         total += (y3[x - 1, pl.ds(y, n)] - a) * (bg[x - 1, pl.ds(y, n)] - k)
-        sub = lax.broadcasted_iota(jnp.int32, (n, 8, 128), 1)
-        end = (sub == 7) & (lane_of(n) == 127)
-        sz = jnp.where(end, 0.0, (z_up(a) - a) * (z_up(k) - k))
+        sz = (z_up(a) - a) * dz[x - D, pl.ds(y - D, n)]
         total = -0.5 * (total + (sz + z_down(sz)))
         yy = y - D
         for i in range(n):
@@ -657,6 +655,7 @@
     qp,
     cz,
     bz,
+    dz,
     hot,
     permit,
     back,
@@ -687,7 +686,11 @@
         for y in range(0, CY, 4):
             at = pl.ds(y + D, 4)
             cz[x + D, at] = z_face(q[x + D, at])
-            bz[x, pl.ds(y, 4)] = z_fluxes(bg[x + D, at], z_face(qp[x + D, at]))
+            field = bg[x + D, at]
+            step = jnp.where(z_end(4), 0.0, z_up(field) - field)
+            dz[x, pl.ds(y, 4)] = step
+            fz = step * z_face(qp[x + D, at])
+            bz[x, pl.ds(y, 4)] = fz - z_down(fz)
         return carry
 
     lax.fori_loop(0, CX, plane, 0)
@@ -778,9 +781,9 @@
     py_low, py_high = shift(high_y, "py", 1), shift(low_y, "py", -1)
     compact = jax.ShapeDtypeStruct((CX, CY, 8, 128), F32)
     full = jax.ShapeDtypeStruct((EX, EY, 8, 128), F32)
-    q, bg, qp, cz, bz, hot = call(
+    q, bg, qp, cz, bz, dz, hot = call(
         own_kernel,
-        [full] * 4 + [compact, jax.ShapeDtypeStruct((CZ, 4096), BF16)],
+        [full] * 4 + [compact] * 2 + [jax.ShapeDtypeStruct((CZ, 4096), BF16)],
         *fields,
         meta,
         hbm=3,
@@ -827,7 +830,7 @@
         y2,
         passed=7,
         scratch=[block, pltpu.VMEM((2 * CX * CY, CZ), BF16), pltpu.VMEM((8, 1024), F32)],
-        limit=14,
+        limit=20,
     )
     got = lax.all_to_all(
         readings.reshape(devices, 1, 9 * 128),
@@ -874,6 +877,7 @@
         q,
         bg,
         cz,
+        dz,
         src,
         y1,
         y2,

time: 88.4 us -> 87.3 us (0.988)
  Pallas kernels: 42.3 us -> 41.2 us
    pallas_call x8, Pallas kernels: 42.3 us -> 41.2 us  [call(): pl.pallas_call(kernel, out_shape=tuple(outs), in_specs=[pl.BlockSpec(memo...]
where the time goes in v9:
time: 87.3 us; the launch traced here: 87.1 us
  Pallas kernels  41.2 us (47%)
  blocking collectives  22.4 us (26%)
  starting transfers between devices  13.5 us (15%)
  waiting for transfers between devices  9.93 us (11%)
    pallas_call x8, Pallas kernels, call(): pl.pallas_call(kernel, out_shape=tuple(outs), in_specs=[pl.BlockSpec(memo...  41.2 us
    all_to_all x1, blocking collectives, body(): lax.all_to_all(readings.reshape(devices, 1, 9 * 128), ('px', 'py'), split...  22.4 us
    ppermute x8, starting transfers between devices, shift(): return lax.ppermute(x, axis, [(i, (i + by) % count) for i in range(count)])  13.5 us
    ppermute x8, waiting for transfers between devices, shift(): return lax.ppermute(x, axis, [(i, (i + by) % count) for i in range(count)])  9.93 us
  transfers between devices with their start and end apart: 8, of which 4 were waited for; matrix products, arithmetic and copies ran while one was open for 0% of the time, Pallas kernels for 14%

profile of v9, /device:TPU:1, one launch (start us, length us, event | category | flops | bytes accessed | tf_op | source)
XLA Modules:
  0.0 87.1 jit_solution(2536605691697628336)
XLA Ops:
  0.0 2.8 %shard_map.82 = (f32[2816,128]{1,0:T(8,128)S(1)}, f32[2816,128]{1,0:T(8,128)S(1)}, f32[848,128]{1,0:T(8,128)S(1)}, f32[848,128]{1,0:T(8,128)S(1)}, f32[16,1024]{1,0:T(8,128)S(1)}) custom-call(f32[2048,128]{1,0:T(8,128)} %bitcast.28, f32[2048,128]{1,0:T(8,128)} %bitcast.30, f32[2048,128]{1,0:T(8,128)} %bitcast.32, s32[4,1024]{1,0:T(4,128)} %nodes_hbm.1, ...), custom_call_target="tpu_custom_call" | custom-call | tf_op jit(solution)/shard_map/pallas_call | solution.py:743
  2.8 0.0 copy-start
  2.8 3.0 %collective-permute-start = (f32[2816,128]{1,0:T(8,128)S(1)}, f32[2816,128]{1,0:T(8,128)S(1)}, u32[]{:S(2)}, u32[]{:S(2)}) collective-permute-start(f32[2816,128]{1,0:T(8,128)S(1)} %get-tuple-element.39), channel_id=1, source_target_pairs={{0,16},{16,32},{32,48},{48,64},{64,80},{80,96},{96,112},{112,0},{1... | collective-permute-start | bytes 4325384 | tf_op jit(solution)/shard_map/ppermute | solution.py:720
  5.9 0.0 collective-permute-start.1
  5.9 1.2 %collective-permute-start.2 = (f32[848,128]{1,0:T(8,128)S(1)}, f32[848,128]{1,0:T(8,128)S(1)}, u32[]{:S(2)}, u32[]{:S(2)}) collective-permute-start(f32[848,128]{1,0:T(8,128)S(1)} %get-tuple-element.41), channel_id=1, source_target_pairs={{0,1},{1,2},{2,3},{3,4},{4,5},{5,6},{6,7},{7,8},{8,9},{9,10},{10,1... | collective-permute-start | bytes 1302536 | tf_op jit(solution)/shard_map/ppermute | solution.py:720
  7.1 3.7 %collective-permute-start.3 = (f32[848,128]{1,0:T(8,128)S(1)}, f32[848,128]{1,0:T(8,128)S(1)}, u32[]{:S(2)}, u32[]{:S(2)}) collective-permute-start(f32[848,128]{1,0:T(8,128)S(1)} %get-tuple-element.42), channel_id=1, source_target_pairs={{0,15},{1,0},{2,1},{3,2},{4,3},{5,4},{6,5},{7,6},{8,7},{9,8},{10,9... | collective-permute-start | bytes 1302536 | tf_op jit(solution)/shard_map/ppermute | solution.py:720
  10.8 4.0 %shard_map.83 = (f32[16,40,8,128]{3,2,1,0:T(8,128)S(1)}, f32[16,40,8,128]{3,2,1,0:T(8,128)S(1)}, f32[16,40,8,128]{3,2,1,0:T(8,128)S(1)}, f32[16,40,8,128]{3,2,1,...) custom-call(f32[2048,128]{1,0:T(8,128)} %bitcast.29, ...), custom_call_target="tpu_custom_call" | custom-call | bytes 8388608 | tf_op jit(solution)/shard_map/pallas_call | solution.py:743
  14.9 4.1 %collective-permute-done.2.py_low = f32[848,128]{1,0:T(8,128)S(1)} collective-permute-done((f32[848,128]{1,0:T(8,128)S(1)}, f32[848,128]{1,0:T(8,128)S(1)}, u32[]{:S(2)}, u32[]{:S(2)}) %collective-permute-start.2) | collective-permute-done | bytes 434208 | tf_op jit(solution)/shard_map/ppermute | solution.py:720
  19.0 0.0 collective-permute-done.3.py_high
  19.0 4.3 %collective-permute-start.4 = (f32[448,128]{1,0:T(8,128)S(1)}, f32[448,128]{1,0:T(8,128)S(1)}, u32[]{:S(2)}, u32[]{:S(2)}) collective-permute-start(f32[448,128]{1,0:T(8,128)S(1)} %get-tuple-element.45), channel_id=1, source_target_pairs={{0,16},{16,32},{32,48},{48,64},{64,80},{80,96},{96,112},{112,0},{1... | collective-permute-start | bytes 688136 | tf_op jit(solution)/shard_map/ppermute | solution.py:720
  23.3 0.0 collective-permute-start.5
  23.3 0.0 copy-done
  23.3 2.3 %shard_map.85 = (f32[16,40,8,128]{3,2,1,0:T(8,128)S(1)}, f32[16,40,8,128]{3,2,1,0:T(8,128)S(1)}, f32[16,40,8,128]{3,2,1,0:T(8,128)S(1)}, f32[16,40,8,128]{3,2,1,...) custom-call(f32[848,128]{1,0:T(8,128)S(1)} %collective-permute-done., ...), custom_call_target="tpu_custom_call", output_to_operand_aliasing={{0}: (4, {}), {1}: (5, {}), {2}: (6, {}), {3}: (7, {})} | custom-call | bytes 8388608 | tf_op jit(solution)/shard_map/pallas_call | solution.py:743
  25.6 0.7 collective-permute-done.4.c_low
  26.3 2.5 %collective-permute-done.5.c_high = f32[448,128]{1,0:T(8,128)S(1)} collective-permute-done((f32[448,128]{1,0:T(8,128)S(1)}, f32[448,128]{1,0:T(8,128)S(1)}, u32[]{:S(2)}, u32[]{:S(2)}) %collective-permute-start.5) | collective-permute-done | bytes 229408 | tf_op jit(solution)/shard_map/ppermute | solution.py:720
  28.8 0.0 collective-permute-done.px_low
  28.8 0.0 collective-permute-done.1.px_high
  28.8 13.1 %shard_map.86 = (f32[1152,128]{1,0:T(8,128)S(1)}, f32[16,40,8,128]{3,2,1,0:T(8,128)S(1)}, f32[16,40,8,128]{3,2,1,0:T(8,128)S(1)}, f32[16,40,8,128]{3,2,1,0:T(8,1...) custom-call(f32[2816,128]{1,0:T(8,128)S(1)} %collective-permute-done, ...), custom_call_target="tpu_custom_call", output_to_operand_aliasing={{1}: (8, {}), {2}: (9, {}), {3}: (10, {}), {4}: (11, {}), {... | custom-call | tf_op jit(solution)/shard_map/pallas_call | solution.py:743
  41.9 22.4 %all_to_all.5 = f32[128,1,1152]{2,1,0:T(1,128)S(1)} all-to-all(f32[128,1,1152]{2,1,0:T(1,128)S(1)} %bitcast.27), channel_id=1, replica_groups=mesh['px'=8,'py'=16] {'px','py'}, dimensions={0} | all-to-all | bytes 1179648 | tf_op jit(solution)/shard_map/all_to_all | solution.py:835
  64.3 5.5 %shard_map.87 = (f32[8,128]{1,0:T(8,128)S(1)}, f32[2048,128]{1,0:T(8,128)S(1)}, f32[1024,128]{1,0:T(8,128)S(1)}, f32[1024,128]{1,0:T(8,128)S(1)}) custom-call(f32[1152,128]{1,0:T(8,128)S(1)} %bitcast.26, f32[16,1024]{1,0:T(8,128)S(1)} %get-tuple-element.43.meta, bf16[1024,4096]{1,0:T(8,128)(2,1)S(1)} %get-tuple-element.47.hot), custom_call_target="tpu_custom_call" | custom-call | tf_op jit(solution)/shard_map/pallas_call | solution.py:743
  69.8 1.2 %collective-permute-start.6 = (f32[1024,128]{1,0:T(8,128)S(1)}, f32[1024,128]{1,0:T(8,128)S(1)}, u32[]{:S(2)}, u32[]{:S(2)}) collective-permute-start(f32[1024,128]{1,0:T(8,128)S(1)} %get-tuple-element.60), channel_id=1, source_target_pairs={{0,16},{16,32},{32,48},{48,64},{64,80},{80,96},{96,112},{112,0},{1... | collective-permute-start | bytes 1572872 | tf_op jit(solution)/shard_map/ppermute | solution.py:720
  71.0 0.0 collective-permute-start.7
  71.0 6.3 %shard_map.88 = (f32[16,40,8,128]{3,2,1,0:T(8,128)S(1)}, f32[16,40,8,128]{3,2,1,0:T(8,128)S(1)}, f32[16,40,8,128]{3,2,1,0:T(8,128)S(1)}, f32[16,40,8,128]{3,2,1,0:T(8,128)S(1)}) custom-call(f32[8,128]{1,0:T(8,128)S(1)} %get-tuple-element.66.weighted, f32[848,128]{1,0:T(8,128)S(1)} %collective-permute-done.2.py_low, ...), custom_call_target="tpu_custom_call" | custom-call | bytes 25165824 | tf_op jit(solution)/shard_map/pallas_call | solution.py:743
  77.3 0.0 collective-permute-done.6.px_low
  77.3 2.6 %collective-permute-done.7.px_high = f32[1024,128]{1,0:T(8,128)S(1)} collective-permute-done((f32[1024,128]{1,0:T(8,128)S(1)}, f32[1024,128]{1,0:T(8,128)S(1)}, u32[]{:S(2)}, u32[]{:S(2)}) %collective-permute-start.7) | collective-permute-done | bytes 524320 | tf_op jit(solution)/shard_map/ppermute | solution.py:720
  79.9 7.2 %shard_map.89 = (f32[2048,128]{1,0:T(8,128)}, f32[16,40,8,128]{3,2,1,0:T(8,128)S(1)}, f32[16,40,8,128]{3,2,1,0:T(8,128)S(1)}, f32[16,40,8,128]{3,2,1,0:T(8,128)S(1)}, f32[16,40,8,128]{3,2,1,0:T(8,128)S(1)}) custom-call(f32[1024,128]{1,0:T(8,128)S(1)} %collective-permute-done.6.px_low, ...), custom_call_target="tpu_custom_call", output_to_operand_aliasing={{1}: (6, {}), {2}: (7, {}), {3}: (8, {}), {4}: (9, {})} | custom-call | tf_op jit(solution)/shard_map/pallas_call | solution.py:743
  (2 shorter events, 0.0 us)
Async XLA Ops:
  2.8 20.5 %copy-start = (f32[8]{0:T(128)S(1)}, f32[8]{0:T(128)}, u32[]{:S(2)}) copy-start(f32[8]{0:T(128)} %param.15) | copy-start | bytes 100
  2.8 25.9 %collective-permute-start = (f32[2816,128]{1,0:T(8,128)S(1)}, f32[2816,128]{1,0:T(8,128)S(1)}, u32[]{:S(2)}, u32[]{:S(2)}) collective-permute-start(f32[2816,128]{1,0:T(8,128)S(1)} %get-tuple-element.39), channel_id=1, source_target_pairs={{0,16},{16,32},{32,48},{48,64},{64,80},{80,96},{96,112},{112,0},{1... | collective-permute-start | bytes 4325384 | tf_op jit(solution)/shard_map/ppermute | solution.py:720
  5.9 22.9 %collective-permute-start.1 = (f32[2816,128]{1,0:T(8,128)S(1)}, f32[2816,128]{1,0:T(8,128)S(1)}, u32[]{:S(2)}, u32[]{:S(2)}) collective-permute-start(f32[2816,128]{1,0:T(8,128)S(1)} %get-tuple-element.40), channel_id=1, source_target_pairs={{0,112},{16,0},{32,16},{48,32},{64,48},{80,64},{96,80},{112,96},{1... | collective-permute-start | bytes 4325384 | tf_op jit(solution)/shard_map/ppermute | solution.py:720
  5.9 13.1 %collective-permute-start.2 = (f32[848,128]{1,0:T(8,128)S(1)}, f32[848,128]{1,0:T(8,128)S(1)}, u32[]{:S(2)}, u32[]{:S(2)}) collective-permute-start(f32[848,128]{1,0:T(8,128)S(1)} %get-tuple-element.41), channel_id=1, source_target_pairs={{0,1},{1,2},{2,3},{3,4},{4,5},{5,6},{6,7},{7,8},{8,9},{9,10},{10,1... | collective-permute-start | bytes 1302536 | tf_op jit(solution)/shard_map/ppermute | solution.py:720
  7.1 11.9 %collective-permute-start.3 = (f32[848,128]{1,0:T(8,128)S(1)}, f32[848,128]{1,0:T(8,128)S(1)}, u32[]{:S(2)}, u32[]{:S(2)}) collective-permute-start(f32[848,128]{1,0:T(8,128)S(1)} %get-tuple-element.42), channel_id=1, source_target_pairs={{0,15},{1,0},{2,1},{3,2},{4,3},{5,4},{6,5},{7,6},{8,7},{9,8},{10,9... | collective-permute-start | bytes 1302536 | tf_op jit(solution)/shard_map/ppermute | solution.py:720
  19.0 7.3 %collective-permute-start.4 = (f32[448,128]{1,0:T(8,128)S(1)}, f32[448,128]{1,0:T(8,128)S(1)}, u32[]{:S(2)}, u32[]{:S(2)}) collective-permute-start(f32[448,128]{1,0:T(8,128)S(1)} %get-tuple-element.45), channel_id=1, source_target_pairs={{0,16},{16,32},{32,48},{48,64},{64,80},{80,96},{96,112},{112,0},{1... | collective-permute-start | bytes 688136 | tf_op jit(solution)/shard_map/ppermute | solution.py:720
  23.3 5.4 %collective-permute-start.5 = (f32[448,128]{1,0:T(8,128)S(1)}, f32[448,128]{1,0:T(8,128)S(1)}, u32[]{:S(2)}, u32[]{:S(2)}) collective-permute-start(f32[448,128]{1,0:T(8,128)S(1)} %get-tuple-element.46.after), channel_id=1, source_target_pairs={{0,112},{16,0},{32,16},{48,32},{64,48},{80,64},{96,80},{112,96},{1... | collective-permute-start | bytes 688136 | tf_op jit(solution)/shard_map/ppermute | solution.py:720
  69.8 7.5 %collective-permute-start.6 = (f32[1024,128]{1,0:T(8,128)S(1)}, f32[1024,128]{1,0:T(8,128)S(1)}, u32[]{:S(2)}, u32[]{:S(2)}) collective-permute-start(f32[1024,128]{1,0:T(8,128)S(1)} %get-tuple-element.60), channel_id=1, source_target_pairs={{0,16},{16,32},{32,48},{48,64},{64,80},{80,96},{96,112},{112,0},{1... | collective-permute-start | bytes 1572872 | tf_op jit(solution)/shard_map/ppermute | solution.py:720
  71.0 8.9 %collective-permute-start.7 = (f32[1024,128]{1,0:T(8,128)S(1)}, f32[1024,128]{1,0:T(8,128)S(1)}, u32[]{:S(2)}, u32[]{:S(2)}) collective-permute-start(f32[1024,128]{1,0:T(8,128)S(1)} %get-tuple-element.61), channel_id=1, source_target_pairs={{0,112},{16,0},{32,16},{48,32},{64,48},{80,64},{96,80},{112,96},{1... | collective-permute-start | bytes 1572872 | tf_op jit(solution)/shard_map/ppermute | solution.py:720

commit v10 on v9

--- a/solution.py
+++ b/solution.py
@@ -355,7 +355,7 @@
         out[i * 72 : (i + 1) * 72, :] = block
 
 
-def scatter(meta, values, rows, per, tiles, width, lhs, keep, hot):
+def put_values(meta, values, rows, per, lhs):
     for k in range(4):
         wanted, numbers = rows16(rows(meta[k : k + 1, :].astype(jnp.int32)))
         value = jnp.broadcast_to(values[k : k + 1, :], wanted.shape)
@@ -367,20 +367,14 @@
             lhs[r * 16 : (r + 1) * 16, lanes] = jnp.where(hit, high, zero)
             lhs[per + r * 16 : per + (r + 1) * 16, lanes] = jnp.where(hit, low, zero)
 
-    def tile(t, carry):
-        total = None
-        for k in range(4):
-            lanes = slice(k * 1024, (k + 1) * 1024)
-            hits = hot[pl.ds(pl.multiple_of(t * width, width), width), lanes]
-            part = dot(lhs[0 : 2 * per, lanes], hits, ((1,), (1,)))
-            total = part if total is None else total + part
-        keep(t, total[0:per] + total[per : 2 * per])
-        return carry
-
-    if tiles == 1:
-        tile(0, 0)
-    else:
-        lax.fori_loop(0, tiles, tile, 0)
+
+def add_up(per, first, width, lhs, hot):
+    total = None
+    for k in range(4):
+        lanes = slice(k * 1024, (k + 1) * 1024)
+        part = dot(lhs[0 : 2 * per, lanes], hot[first : first + width, lanes], ((1,), (1,)))
+        total = part if total is None else total + part
+    return total[0:per] + total[per : 2 * per]
 
 
 def returned(weighted, table, values):
@@ -393,23 +387,30 @@
     values[0:4, :] = table[4:8, :] * found
 
 
-def source_kernel(got, meta, hot, weighted, own, low, high, lhs, values):
+def source_kernel(got, meta, hot, weighted, lhs, own, low, high, values):
     count = got.shape[0] // 9
     sums = [jnp.sum(got[pl.ds(i, count, stride=9), :], axis=0, keepdims=True) for i in range(8)]
     readings = jnp.concatenate(sums, axis=0)
     weights = jnp.transpose(got[pl.ds(8, count, stride=9), :])[0:8]
     weighted[...] = readings * weights
 
-    def keep(t, sums):
-        for x in range(CX):
-            for i in range(4):
-                block = sums[x * CY : (x + 1) * CY, i * 128 : (i + 1) * 128]
-                own[pl.ds(x * PLANE + t * 4 + i, CY, stride=8), :] = block
-                side, at = (low, x) if x < D else (high, x - (CX - D))
-                side[pl.ds(at * PLANE + t * 4 + i, CY, stride=8), :] = block
-
     returned(weighted[...], meta, values)
-    scatter(meta, values, lambda n: n >> 10, CX * CY, 2, 512, lhs, keep, hot)
+    put_values(meta, values, lambda n: n >> 10, CX * CY, lhs)
+    put_half(0, add_up(CX * CY, 0, CZ // 2, lhs, hot), own, low, high)
+
+
+def put_half(half, sums, own, low, high):
+    for x in range(CX):
+        side, at = (low, x) if x < D else (high, x - (CX - D))
+        for i in range(4):
+            block = sums[x * CY : (x + 1) * CY, i * 128 : (i + 1) * 128]
+            own[pl.ds(x * PLANE + half * 4 + i, CY, stride=8), :] = block
+            side[pl.ds(at * CY * 4 + i, CY, stride=4), :] = block
+
+
+def other_half_kernel(lhs, hot, own_in, own, low, high):
+    del own_in
+    put_half(1, add_up(CX * CY, CZ // 2, CZ // 2, lhs, hot), own, low, high)
 
 
 def second_solve(src, q, cz, y1, y2, y3):
@@ -464,7 +465,7 @@
             good = (y >= 0) & (y < D)
             return jnp.where(good, (((node >> 8) & 3) * CX + x) * D + y, -1)
 
-        def keep(t, sums, y0=y0):
+        def keep(sums, y0=y0):
             for zq in range(4):
                 for x in range(CX):
                     first = (zq * CX + x) * D
@@ -473,7 +474,8 @@
                             pl.ds(((x + D) * EY + y0) * 8 + zq * 2 + half, D, stride=8), :
                         ] = sums[first : first + D, half * 128 : (half + 1) * 128]
 
-        scatter(near, values, rows, 4 * CX * D, 1, 256, lhs, keep, near_hot)
+        put_values(near, values, rows, 4 * CX * D, lhs)
+        keep(add_up(4 * CX * D, 0, 256, lhs, near_hot))
 
     for ref, x_low in ((c_low, True), (c_high, False)):
         for side, y_low in enumerate((True, False)):
@@ -488,7 +490,7 @@
                 cell = jnp.where(dx == 1, dy - 1, jnp.where(dx == 2, dy + 2, 5))
                 return jnp.where(dx + dy <= D, ((node >> 7) & 7) * len(CELLS) + cell, -1)
 
-            def keep(t, sums, x_low=x_low, y_low=y_low):
+            def keep(sums, x_low=x_low, y_low=y_low):
                 x0, y0 = 0 if x_low else D + CX, 0 if y_low else D + CY
                 src[x0 : x0 + D, y0 : y0 + D] = jnp.zeros((D, D, 8, 128), F32)
                 for i, (dx, dy) in enumerate(CELLS):
@@ -500,7 +502,8 @@
                             row : row + 1, :
                         ]
 
-            scatter(near, values, rows, 8 * len(CELLS), 1, 128, lhs, keep, near_hot)
+            put_values(near, values, rows, 8 * len(CELLS), lhs)
+            keep(add_up(8 * len(CELLS), 0, 128, lhs, near_hot))
 
     first, second, third = second_solve(src, q, cz, y1, y2, y3)
     early(1, first)
@@ -509,11 +512,13 @@
 
 
 def adjoint_kernel(
-    px_low, px_high, q, bg, cz, dz, src_in, y1_in, y2_in, y3_in, out_hbm, src, y1, y2, y3, out, sems
+    low_0, high_0, low_1, high_1, q, bg, cz, dz, src_in, y1_in, y2_in, y3_in, out_hbm, src, y1, y2, y3, out, sems
 ):
     del src_in, y1_in, y2_in, y3_in
-    for x, ref in ((0, px_low), (D + CX, px_high)):
-        src[x : x + D, D : D + CY] = ref[...].reshape(D, CY, 8, 128)
+    for half, x, ref in ((0, 0, low_0), (0, D + CX, high_0), (1, 0, low_1), (1, D + CX, high_1)):
+        for i in range(D):
+            v = ref[i * CY * 4 : (i + 1) * CY * 4, :].reshape(CY, 4, 128)
+            src[x + i, D : D + CY, half * 4 : half * 4 + 4] = v
     first, second, third = second_solve(src, q, cz, y1, y2, y3)
     late(1, first)
     late(2, second)
@@ -839,16 +844,29 @@
         concat_axis=0,
         tiled=True,
     ).reshape(devices * 9, 128)
-    weighted, own_source, low_s, high_s = call(
+    half = D * PLANE // 2
+    weighted, lhs, own_source, low_s, high_s = call(
         source_kernel,
-        rows(8, ROWS, D * PLANE, D * PLANE),
+        rows(8) + [jax.ShapeDtypeStruct((2 * CX * CY, 4096), BF16)] + rows(ROWS, half, half),
         got,
         meta,
         hot,
-        scratch=[pltpu.VMEM((2 * CX * CY, 4096), BF16), pltpu.VMEM((8, 1024), F32)],
-        limit=18,
+        scratch=[pltpu.VMEM((8, 1024), F32)],
+        limit=12,
     )
-    source_low, source_high = shift(high_s, "px", 1), shift(low_s, "px", -1)
+    low_0, high_0 = shift(high_s, "px", 1), shift(low_s, "px", -1)
+    own_source, low_s, high_s = call(
+        other_half_kernel,
+        rows(ROWS, half, half),
+        lhs,
+        hot,
+        own_source,
+        passed=1,
+        at=0,
+        limit=12,
+        bytes_accessed=8 * 2**20,
+    )
+    low_1, high_1 = shift(high_s, "px", 1), shift(low_s, "px", -1)
     src, y1, y2, y3 = call(
         strips_kernel,
         [full] * 4,
@@ -872,8 +890,10 @@
     result = call(
         adjoint_kernel,
         rows(ROWS) + [full] * 4,
-        source_low,
-        source_high,
+        low_0,
+        high_0,
+        low_1,
+        high_1,
         q,
         bg,
         cz,

time: 87.3 us -> 88.8 us (1.017); the launches traced: 87.1 us -> 87.1 us
  waiting for transfers between devices: 9.93 us -> 7.32 us
  starting transfers between devices: 13.5 us -> 16 us
    ppermute x8 -> x10, waiting for transfers between devices: 9.93 us -> 7.32 us  [shift(): return lax.ppermute(x, axis, [(i, (i + by) % count) for i in range(count)])]
    ppermute x8 -> x10, starting transfers between devices: 13.5 us -> 16 us  [shift(): return lax.ppermute(x, axis, [(i, (i + by) % count) for i in range(count)])]
    pallas_call x8 -> x9, Pallas kernels: 41.2 us -> 41 us  [call(): pl.pallas_call(kernel, out_shape=tuple(outs), in_specs=[pl.BlockSpec(memo...]
  transfers between devices with their start and end apart: 8 -> 10, of which waited for: 4 -> 3; matrix products, arithmetic and copies ran while one was open for 0% -> 0% of each run, Pallas kernels for 14% -> 17%
where the time goes in v10:
time: 88.8 us; the launch traced here: 87.1 us
  Pallas kernels  41 us (46%)
  blocking collectives  22.4 us (25%)
  starting transfers between devices  16 us (18%)
  waiting for transfers between devices  7.32 us (8%)
    pallas_call x9, Pallas kernels, call(): pl.pallas_call(kernel, out_shape=tuple(outs), in_specs=[pl.BlockSpec(memo...  41 us
    all_to_all x1, blocking collectives, body(): lax.all_to_all(readings.reshape(devices, 1, 9 * 128), ('px', 'py'), split...  22.4 us
    ppermute x10, starting transfers between devices, shift(): return lax.ppermute(x, axis, [(i, (i + by) % count) for i in range(count)])  16 us
    ppermute x10, waiting for transfers between devices, shift(): return lax.ppermute(x, axis, [(i, (i + by) % count) for i in range(count)])  7.32 us
  transfers between devices with their start and end apart: 10, of which 3 were waited for; matrix products, arithmetic and copies ran while one was open for 0% of the time, Pallas kernels for 17%

profile of v10, /device:TPU:1, one launch (start us, length us, event | category | flops | bytes accessed | tf_op | source)
XLA Modules:
  0.0 87.1 jit_solution(12408872351345108944)
XLA Ops:
  0.0 2.8 %shard_map.82 = (f32[2816,128]{1,0:T(8,128)S(1)}, f32[2816,128]{1,0:T(8,128)S(1)}, f32[848,128]{1,0:T(8,128)S(1)}, f32[848,128]{1,0:T(8,128)S(1)}, f32[16,1024]{1,0:T(8,128)S(1)}) custom-call(f32[2048,128]{1,0:T(8,128)} %bitcast.28, f32[2048,128]{1,0:T(8,128)} %bitcast.30, f32[2048,128]{1,0:T(8,128)} %bitcast.32, s32[4,1024]{1,0:T(4,128)} %nodes_hbm.1, ...), custom_call_target="tpu_custom_call" | custom-call | tf_op jit(solution)/shard_map/pallas_call | solution.py:748
  2.8 0.0 copy-start
  2.8 3.0 %collective-permute-start = (f32[2816,128]{1,0:T(8,128)S(1)}, f32[2816,128]{1,0:T(8,128)S(1)}, u32[]{:S(2)}, u32[]{:S(2)}) collective-permute-start(f32[2816,128]{1,0:T(8,128)S(1)} %get-tuple-element.43), channel_id=1, source_target_pairs={{0,16},{16,32},{32,48},{48,64},{64,80},{80,96},{96,112},{112,0},{1... | collective-permute-start | bytes 4325384 | tf_op jit(solution)/shard_map/ppermute | solution.py:725
  5.9 0.0 collective-permute-start.1
  5.9 1.2 %collective-permute-start.2 = (f32[848,128]{1,0:T(8,128)S(1)}, f32[848,128]{1,0:T(8,128)S(1)}, u32[]{:S(2)}, u32[]{:S(2)}) collective-permute-start(f32[848,128]{1,0:T(8,128)S(1)} %get-tuple-element.45), channel_id=1, source_target_pairs={{0,1},{1,2},{2,3},{3,4},{4,5},{5,6},{6,7},{7,8},{8,9},{9,10},{10,1... | collective-permute-start | bytes 1302536 | tf_op jit(solution)/shard_map/ppermute | solution.py:725
  7.1 3.7 %collective-permute-start.3 = (f32[848,128]{1,0:T(8,128)S(1)}, f32[848,128]{1,0:T(8,128)S(1)}, u32[]{:S(2)}, u32[]{:S(2)}) collective-permute-start(f32[848,128]{1,0:T(8,128)S(1)} %get-tuple-element.46), channel_id=1, source_target_pairs={{0,15},{1,0},{2,1},{3,2},{4,3},{5,4},{6,5},{7,6},{8,7},{9,8},{10,9... | collective-permute-start | bytes 1302536 | tf_op jit(solution)/shard_map/ppermute | solution.py:725
  10.8 4.0 %shard_map.83 = (f32[16,40,8,128]{3,2,1,0:T(8,128)S(1)}, f32[16,40,8,128]{3,2,1,0:T(8,128)S(1)}, f32[16,40,8,128]{3,2,1,0:T(8,128)S(1)}, f32[16,40,8,128]{3,2,1,...) custom-call(f32[2048,128]{1,0:T(8,128)} %bitcast.29, ...), custom_call_target="tpu_custom_call" | custom-call | bytes 8388608 | tf_op jit(solution)/shard_map/pallas_call | solution.py:748
  14.9 4.1 %collective-permute-done.2.py_low = f32[848,128]{1,0:T(8,128)S(1)} collective-permute-done((f32[848,128]{1,0:T(8,128)S(1)}, f32[848,128]{1,0:T(8,128)S(1)}, u32[]{:S(2)}, u32[]{:S(2)}) %collective-permute-start.2) | collective-permute-done | bytes 434208 | tf_op jit(solution)/shard_map/ppermute | solution.py:725
  19.0 0.0 collective-permute-done.3.py_high
  19.0 4.3 %collective-permute-start.4 = (f32[448,128]{1,0:T(8,128)S(1)}, f32[448,128]{1,0:T(8,128)S(1)}, u32[]{:S(2)}, u32[]{:S(2)}) collective-permute-start(f32[448,128]{1,0:T(8,128)S(1)} %get-tuple-element.49), channel_id=1, source_target_pairs={{0,16},{16,32},{32,48},{48,64},{64,80},{80,96},{96,112},{112,0},{1... | collective-permute-start | bytes 688136 | tf_op jit(solution)/shard_map/ppermute | solution.py:725
  23.3 0.0 collective-permute-start.5
  23.3 0.0 copy-done
  23.3 2.3 %shard_map.85 = (f32[16,40,8,128]{3,2,1,0:T(8,128)S(1)}, f32[16,40,8,128]{3,2,1,0:T(8,128)S(1)}, f32[16,40,8,128]{3,2,1,0:T(8,128)S(1)}, f32[16,40,8,128]{3,2,1,...) custom-call(f32[848,128]{1,0:T(8,128)S(1)} %collective-permute-done., ...), custom_call_target="tpu_custom_call", output_to_operand_aliasing={{0}: (4, {}), {1}: (5, {}), {2}: (6, {}), {3}: (7, {})} | custom-call | bytes 8388608 | tf_op jit(solution)/shard_map/pallas_call | solution.py:748
  25.6 0.7 collective-permute-done.4.c_low
  26.3 2.5 %collective-permute-done.5.c_high = f32[448,128]{1,0:T(8,128)S(1)} collective-permute-done((f32[448,128]{1,0:T(8,128)S(1)}, f32[448,128]{1,0:T(8,128)S(1)}, u32[]{:S(2)}, u32[]{:S(2)}) %collective-permute-start.5) | collective-permute-done | bytes 229408 | tf_op jit(solution)/shard_map/ppermute | solution.py:725
  28.8 0.0 collective-permute-done.px_low
  28.8 0.0 collective-permute-done.1.px_high
  28.8 13.1 %shard_map.86 = (f32[1152,128]{1,0:T(8,128)S(1)}, f32[16,40,8,128]{3,2,1,0:T(8,128)S(1)}, f32[16,40,8,128]{3,2,1,0:T(8,128)S(1)}, f32[16,40,8,128]{3,2,1,0:T(8,1...) custom-call(f32[2816,128]{1,0:T(8,128)S(1)} %collective-permute-done, ...), custom_call_target="tpu_custom_call", output_to_operand_aliasing={{1}: (8, {}), {2}: (9, {}), {3}: (10, {}), {4}: (11, {}), {... | custom-call | tf_op jit(solution)/shard_map/pallas_call | solution.py:748
  41.9 22.4 %all_to_all.5 = f32[128,1,1152]{2,1,0:T(1,128)S(1)} all-to-all(f32[128,1,1152]{2,1,0:T(1,128)S(1)} %bitcast.27), channel_id=1, replica_groups=mesh['px'=8,'py'=16] {'px','py'}, dimensions={0} | all-to-all | bytes 1179648 | tf_op jit(solution)/shard_map/all_to_all | solution.py:840
  64.3 2.8 %shard_map.87 = (f32[8,128]{1,0:T(8,128)S(1)}, bf16[512,4096]{1,0:T(8,128)(2,1)S(1)}, f32[2048,128]{1,0:T(8,128)S(1)}, f32[512,128]{1,0:T(8,128)S(1)}, f32[512,128]{1,0:T(8,128)S(1)}) custom-call(f32[1152,128]{1,0:T(8,128)S(1)} %bitcast.26, f32[16,1024]{1,0:T(8,128)S(1)} %get-tuple-element.47.meta, bf16[1024,4096]{1,0:T(8,128)(2,1)S(1)} %get-tuple-element.51.hot), custom_call_target="tpu_custom_call" | custom-call | tf_op jit(solution)/shard_map/pallas_call | solution.py:748
  67.1 1.2 %collective-permute-start.6 = (f32[512,128]{1,0:T(8,128)S(1)}, f32[512,128]{1,0:T(8,128)S(1)}, u32[]{:S(2)}, u32[]{:S(2)}) collective-permute-start(f32[512,128]{1,0:T(8,128)S(1)} %get-tuple-element.64), channel_id=1, source_target_pairs={{0,16},{16,32},{32,48},{48,64},{64,80},{80,96},{96,112},{112,0},{1... | collective-permute-start | bytes 786440 | tf_op jit(solution)/shard_map/ppermute | solution.py:725
  68.3 0.0 collective-permute-start.7
  68.3 2.4 %shard_map.88 = (f32[2048,128]{1,0:T(8,128)S(1)}, f32[512,128]{1,0:T(8,128)S(1)}, f32[512,128]{1,0:T(8,128)S(1)}) custom-call(bf16[512,4096]{1,0:T(8,128)(2,1)S(1)} %get-tuple-element.66.lhs, bf16[1024,4096]{1,0:T(8,128)(2,1)S(1)} %get-tuple-element.51.hot, f32[2048,128]{1,0:T(8,128)S(1)} %get-tuple-element.67.own_in), custom_call_target="tpu_custom_call", output_to_operand_aliasing={{0}: (2, {})} | custom-call | bytes 8388608 | tf_op jit(solution)/shard_map/pallas_call | solution.py:748
  70.7 1.8 %collective-permute-start.8 = (f32[512,128]{1,0:T(8,128)S(1)}, f32[512,128]{1,0:T(8,128)S(1)}, u32[]{:S(2)}, u32[]{:S(2)}) collective-permute-start(f32[512,128]{1,0:T(8,128)S(1)} %get-tuple-element.68), channel_id=1, source_target_pairs={{0,16},{16,32},{32,48},{48,64},{64,80},{80,96},{96,112},{112,0},{1... | collective-permute-start | bytes 786440 | tf_op jit(solution)/shard_map/ppermute | solution.py:725
  72.5 0.8 collective-permute-start.9
  73.3 6.3 %shard_map.89 = (f32[16,40,8,128]{3,2,1,0:T(8,128)S(1)}, f32[16,40,8,128]{3,2,1,0:T(8,128)S(1)}, f32[16,40,8,128]{3,2,1,0:T(8,128)S(1)}, f32[16,40,8,128]{3,2,1,0:T(8,128)S(1)}) custom-call(f32[8,128]{1,0:T(8,128)S(1)} %get-tuple-element.74.weighted, f32[848,128]{1,0:T(8,128)S(1)} %collective-permute-done.2.py_low, ...), custom_call_target="tpu_custom_call" | custom-call | bytes 25165824 | tf_op jit(solution)/shard_map/pallas_call | solution.py:748
  79.6 0.0 collective-permute-done.6.low_0
  79.6 0.0 collective-permute-done.7.high_0
  79.6 0.0 collective-permute-done.8.low_1
  79.6 0.0 collective-permute-done.9.high_1
  79.6 7.3 %shard_map.90 = (f32[2048,128]{1,0:T(8,128)}, f32[16,40,8,128]{3,2,1,0:T(8,128)S(1)}, f32[16,40,8,128]{3,2,1,0:T(8,128)S(1)}, f32[16,40,8,128]{3,2,1,0:T(8,128)S(1)}, f32[16,40,8,128]{3,2,1,0:T(8,128)S(1)}) custom-call(f32[512,128]{1,0:T(8,128)S(1)} %collective-permute-done.6.low_0, ...), custom_call_target="tpu_custom_call", output_to_operand_aliasing={{1}: (8, {}), {2}: (9, {}), {3}: (10, {}), {4}: (11, {})} | custom-call | tf_op jit(solution)/shard_map/pallas_call | solution.py:748
  (2 shorter events, 0.0 us)
Async XLA Ops:
  2.8 20.5 %copy-start = (f32[8]{0:T(128)S(1)}, f32[8]{0:T(128)}, u32[]{:S(2)}) copy-start(f32[8]{0:T(128)} %param.15) | copy-start | bytes 100
  2.8 25.9 %collective-permute-start = (f32[2816,128]{1,0:T(8,128)S(1)}, f32[2816,128]{1,0:T(8,128)S(1)}, u32[]{:S(2)}, u32[]{:S(2)}) collective-permute-start(f32[2816,128]{1,0:T(8,128)S(1)} %get-tuple-element.43), channel_id=1, source_target_pairs={{0,16},{16,32},{32,48},{48,64},{64,80},{80,96},{96,112},{112,0},{1... | collective-permute-start | bytes 4325384 | tf_op jit(solution)/shard_map/ppermute | solution.py:725
  5.9 22.9 %collective-permute-start.1 = (f32[2816,128]{1,0:T(8,128)S(1)}, f32[2816,128]{1,0:T(8,128)S(1)}, u32[]{:S(2)}, u32[]{:S(2)}) collective-permute-start(f32[2816,128]{1,0:T(8,128)S(1)} %get-tuple-element.44), channel_id=1, source_target_pairs={{0,112},{16,0},{32,16},{48,32},{64,48},{80,64},{96,80},{112,96},{1... | collective-permute-start | bytes 4325384 | tf_op jit(solution)/shard_map/ppermute | solution.py:725
  5.9 13.1 %collective-permute-start.2 = (f32[848,128]{1,0:T(8,128)S(1)}, f32[848,128]{1,0:T(8,128)S(1)}, u32[]{:S(2)}, u32[]{:S(2)}) collective-permute-start(f32[848,128]{1,0:T(8,128)S(1)} %get-tuple-element.45), channel_id=1, source_target_pairs={{0,1},{1,2},{2,3},{3,4},{4,5},{5,6},{6,7},{7,8},{8,9},{9,10},{10,1... | collective-permute-start | bytes 1302536 | tf_op jit(solution)/shard_map/ppermute | solution.py:725
  7.1 11.9 %collective-permute-start.3 = (f32[848,128]{1,0:T(8,128)S(1)}, f32[848,128]{1,0:T(8,128)S(1)}, u32[]{:S(2)}, u32[]{:S(2)}) collective-permute-start(f32[848,128]{1,0:T(8,128)S(1)} %get-tuple-element.46), channel_id=1, source_target_pairs={{0,15},{1,0},{2,1},{3,2},{4,3},{5,4},{6,5},{7,6},{8,7},{9,8},{10,9... | collective-permute-start | bytes 1302536 | tf_op jit(solution)/shard_map/ppermute | solution.py:725
  19.0 7.3 %collective-permute-start.4 = (f32[448,128]{1,0:T(8,128)S(1)}, f32[448,128]{1,0:T(8,128)S(1)}, u32[]{:S(2)}, u32[]{:S(2)}) collective-permute-start(f32[448,128]{1,0:T(8,128)S(1)} %get-tuple-element.49), channel_id=1, source_target_pairs={{0,16},{16,32},{32,48},{48,64},{64,80},{80,96},{96,112},{112,0},{1... | collective-permute-start | bytes 688136 | tf_op jit(solution)/shard_map/ppermute | solution.py:725
  23.3 5.4 %collective-permute-start.5 = (f32[448,128]{1,0:T(8,128)S(1)}, f32[448,128]{1,0:T(8,128)S(1)}, u32[]{:S(2)}, u32[]{:S(2)}) collective-permute-start(f32[448,128]{1,0:T(8,128)S(1)} %get-tuple-element.50.after), channel_id=1, source_target_pairs={{0,112},{16,0},{32,16},{48,32},{64,48},{80,64},{96,80},{112,96},{1... | collective-permute-start | bytes 688136 | tf_op jit(solution)/shard_map/ppermute | solution.py:725
  67.1 12.5 %collective-permute-start.6 = (f32[512,128]{1,0:T(8,128)S(1)}, f32[512,128]{1,0:T(8,128)S(1)}, u32[]{:S(2)}, u32[]{:S(2)}) collective-permute-start(f32[512,128]{1,0:T(8,128)S(1)} %get-tuple-element.64), channel_id=1, source_target_pairs={{0,16},{16,32},{32,48},{48,64},{64,80},{80,96},{96,112},{112,0},{1... | collective-permute-start | bytes 786440 | tf_op jit(solution)/shard_map/ppermute | solution.py:725
  68.3 11.3 %collective-permute-start.7 = (f32[512,128]{1,0:T(8,128)S(1)}, f32[512,128]{1,0:T(8,128)S(1)}, u32[]{:S(2)}, u32[]{:S(2)}) collective-permute-start(f32[512,128]{1,0:T(8,128)S(1)} %get-tuple-element.65), channel_id=1, source_target_pairs={{0,112},{16,0},{32,16},{48,32},{64,48},{80,64},{96,80},{112,96},{1... | collective-permute-start | bytes 786440 | tf_op jit(solution)/shard_map/ppermute | solution.py:725
  70.7 8.9 %collective-permute-start.8 = (f32[512,128]{1,0:T(8,128)S(1)}, f32[512,128]{1,0:T(8,128)S(1)}, u32[]{:S(2)}, u32[]{:S(2)}) collective-permute-start(f32[512,128]{1,0:T(8,128)S(1)} %get-tuple-element.68), channel_id=1, source_target_pairs={{0,16},{16,32},{32,48},{48,64},{64,80},{80,96},{96,112},{112,0},{1... | collective-permute-start | bytes 786440 | tf_op jit(solution)/shard_map/ppermute | solution.py:725
  72.5 7.1 %collective-permute-start.9 = (f32[512,128]{1,0:T(8,128)S(1)}, f32[512,128]{1,0:T(8,128)S(1)}, u32[]{:S(2)}, u32[]{:S(2)}) collective-permute-start(f32[512,128]{1,0:T(8,128)S(1)} %get-tuple-element.69), channel_id=1, source_target_pairs={{0,112},{16,0},{32,16},{48,32},{64,48},{80,64},{96,80},{112,96},{1... | collective-permute-start | bytes 786440 | tf_op jit(solution)/shard_map/ppermute | solution.py:725

commit v11 on v9

--- a/solution.py
+++ b/solution.py
@@ -189,7 +189,7 @@
         f, acc = fluxes(y1, q, cz, x, y, n)
         y2[x, pl.ds(y, n)] = A1 * b[x, pl.ds(y, n)] - f - acc
 
-    return lines(1, 4, whole), right_own, lines(2, 4, second), lines(3, 4, third)
+    return lines(1, 2, whole), right_own, lines(2, 4, second), lines(3, 2, third)
 
 
 def middle_kernel(
@@ -425,7 +425,7 @@
         f, acc = fluxes(y2, q, cz, x, y, n)
         y3[x, pl.ds(y, n)] = A0 * src[x, pl.ds(y, n)] - f - acc
 
-    return lines(1, 4, first), lines(2, 4, second), lines(3, 4, third)
+    return lines(1, 2, first), lines(2, 4, second), lines(3, 2, third)
 
 
 def strips_kernel(

time: 87.3 us -> 87.6 us (level)
  no operation moved by 1% of the time
where the time goes in v11:
time: 87.6 us; the launch traced here: 87.5 us
  Pallas kernels  41.6 us (47%)
  blocking collectives  22.4 us (26%)
  starting transfers between devices  13.5 us (15%)
  waiting for transfers between devices  9.9 us (11%)
    pallas_call x8, Pallas kernels, call(): pl.pallas_call(kernel, out_shape=tuple(outs), in_specs=[pl.BlockSpec(memo...  41.6 us
    all_to_all x1, blocking collectives, body(): lax.all_to_all(readings.reshape(devices, 1, 9 * 128), ('px', 'py'), split...  22.4 us
    ppermute x8, starting transfers between devices, shift(): return lax.ppermute(x, axis, [(i, (i + by) % count) for i in range(count)])  13.5 us
    ppermute x8, waiting for transfers between devices, shift(): return lax.ppermute(x, axis, [(i, (i + by) % count) for i in range(count)])  9.9 us
  transfers between devices with their start and end apart: 8, of which 4 were waited for; matrix products, arithmetic and copies ran while one was open for 0% of the time, Pallas kernels for 14%

profile of v11, /device:TPU:1, one launch (start us, length us, event | category | flops | bytes accessed | tf_op | source)
XLA Modules:
  0.0 87.5 jit_solution(2919968314474353542)
XLA Ops:
  0.0 2.8 %shard_map.82 = (f32[2816,128]{1,0:T(8,128)S(1)}, f32[2816,128]{1,0:T(8,128)S(1)}, f32[848,128]{1,0:T(8,128)S(1)}, f32[848,128]{1,0:T(8,128)S(1)}, f32[16,1024]{1,0:T(8,128)S(1)}) custom-call(f32[2048,128]{1,0:T(8,128)} %bitcast.28, f32[2048,128]{1,0:T(8,128)} %bitcast.30, f32[2048,128]{1,0:T(8,128)} %bitcast.32, s32[4,1024]{1,0:T(4,128)} %nodes_hbm.1, ...), custom_call_target="tpu_custom_call" | custom-call | tf_op jit(solution)/shard_map/pallas_call | solution.py:743
  2.8 0.0 copy-start
  2.8 3.0 %collective-permute-start = (f32[2816,128]{1,0:T(8,128)S(1)}, f32[2816,128]{1,0:T(8,128)S(1)}, u32[]{:S(2)}, u32[]{:S(2)}) collective-permute-start(f32[2816,128]{1,0:T(8,128)S(1)} %get-tuple-element.39), channel_id=1, source_target_pairs={{0,16},{16,32},{32,48},{48,64},{64,80},{80,96},{96,112},{112,0},{1... | collective-permute-start | bytes 4325384 | tf_op jit(solution)/shard_map/ppermute | solution.py:720
  5.9 0.0 collective-permute-start.1
  5.9 1.2 %collective-permute-start.2 = (f32[848,128]{1,0:T(8,128)S(1)}, f32[848,128]{1,0:T(8,128)S(1)}, u32[]{:S(2)}, u32[]{:S(2)}) collective-permute-start(f32[848,128]{1,0:T(8,128)S(1)} %get-tuple-element.41), channel_id=1, source_target_pairs={{0,1},{1,2},{2,3},{3,4},{4,5},{5,6},{6,7},{7,8},{8,9},{9,10},{10,1... | collective-permute-start | bytes 1302536 | tf_op jit(solution)/shard_map/ppermute | solution.py:720
  7.1 3.7 %collective-permute-start.3 = (f32[848,128]{1,0:T(8,128)S(1)}, f32[848,128]{1,0:T(8,128)S(1)}, u32[]{:S(2)}, u32[]{:S(2)}) collective-permute-start(f32[848,128]{1,0:T(8,128)S(1)} %get-tuple-element.42), channel_id=1, source_target_pairs={{0,15},{1,0},{2,1},{3,2},{4,3},{5,4},{6,5},{7,6},{8,7},{9,8},{10,9... | collective-permute-start | bytes 1302536 | tf_op jit(solution)/shard_map/ppermute | solution.py:720
  10.8 4.0 %shard_map.83 = (f32[16,40,8,128]{3,2,1,0:T(8,128)S(1)}, f32[16,40,8,128]{3,2,1,0:T(8,128)S(1)}, f32[16,40,8,128]{3,2,1,0:T(8,128)S(1)}, f32[16,40,8,128]{3,2,1,...) custom-call(f32[2048,128]{1,0:T(8,128)} %bitcast.29, ...), custom_call_target="tpu_custom_call" | custom-call | bytes 8388608 | tf_op jit(solution)/shard_map/pallas_call | solution.py:743
  14.9 4.1 %collective-permute-done.2.py_low = f32[848,128]{1,0:T(8,128)S(1)} collective-permute-done((f32[848,128]{1,0:T(8,128)S(1)}, f32[848,128]{1,0:T(8,128)S(1)}, u32[]{:S(2)}, u32[]{:S(2)}) %collective-permute-start.2) | collective-permute-done | bytes 434208 | tf_op jit(solution)/shard_map/ppermute | solution.py:720
  19.0 0.0 collective-permute-done.3.py_high
  19.0 4.3 %collective-permute-start.4 = (f32[448,128]{1,0:T(8,128)S(1)}, f32[448,128]{1,0:T(8,128)S(1)}, u32[]{:S(2)}, u32[]{:S(2)}) collective-permute-start(f32[448,128]{1,0:T(8,128)S(1)} %get-tuple-element.45), channel_id=1, source_target_pairs={{0,16},{16,32},{32,48},{48,64},{64,80},{80,96},{96,112},{112,0},{1... | collective-permute-start | bytes 688136 | tf_op jit(solution)/shard_map/ppermute | solution.py:720
  23.3 0.0 collective-permute-start.5
  23.3 0.0 copy-done
  23.3 2.3 %shard_map.85 = (f32[16,40,8,128]{3,2,1,0:T(8,128)S(1)}, f32[16,40,8,128]{3,2,1,0:T(8,128)S(1)}, f32[16,40,8,128]{3,2,1,0:T(8,128)S(1)}, f32[16,40,8,128]{3,2,1,...) custom-call(f32[848,128]{1,0:T(8,128)S(1)} %collective-permute-done., ...), custom_call_target="tpu_custom_call", output_to_operand_aliasing={{0}: (4, {}), {1}: (5, {}), {2}: (6, {}), {3}: (7, {})} | custom-call | bytes 8388608 | tf_op jit(solution)/shard_map/pallas_call | solution.py:743
  25.6 0.7 collective-permute-done.4.c_low
  26.3 2.5 %collective-permute-done.5.c_high = f32[448,128]{1,0:T(8,128)S(1)} collective-permute-done((f32[448,128]{1,0:T(8,128)S(1)}, f32[448,128]{1,0:T(8,128)S(1)}, u32[]{:S(2)}, u32[]{:S(2)}) %collective-permute-start.5) | collective-permute-done | bytes 229408 | tf_op jit(solution)/shard_map/ppermute | solution.py:720
  28.8 0.0 collective-permute-done.px_low
  28.8 0.0 collective-permute-done.1.px_high
  28.8 13.4 %shard_map.86 = (f32[1152,128]{1,0:T(8,128)S(1)}, f32[16,40,8,128]{3,2,1,0:T(8,128)S(1)}, f32[16,40,8,128]{3,2,1,0:T(8,128)S(1)}, f32[16,40,8,128]{3,2,1,0:T(8,1...) custom-call(f32[2816,128]{1,0:T(8,128)S(1)} %collective-permute-done, ...), custom_call_target="tpu_custom_call", output_to_operand_aliasing={{1}: (8, {}), {2}: (9, {}), {3}: (10, {}), {4}: (11, {}), {... | custom-call | tf_op jit(solution)/shard_map/pallas_call | solution.py:743
  42.2 22.4 %all_to_all.5 = f32[128,1,1152]{2,1,0:T(1,128)S(1)} all-to-all(f32[128,1,1152]{2,1,0:T(1,128)S(1)} %bitcast.27), channel_id=1, replica_groups=mesh['px'=8,'py'=16] {'px','py'}, dimensions={0} | all-to-all | bytes 1179648 | tf_op jit(solution)/shard_map/all_to_all | solution.py:835
  64.6 5.5 %shard_map.87 = (f32[8,128]{1,0:T(8,128)S(1)}, f32[2048,128]{1,0:T(8,128)S(1)}, f32[1024,128]{1,0:T(8,128)S(1)}, f32[1024,128]{1,0:T(8,128)S(1)}) custom-call(f32[1152,128]{1,0:T(8,128)S(1)} %bitcast.26, f32[16,1024]{1,0:T(8,128)S(1)} %get-tuple-element.43.meta, bf16[1024,4096]{1,0:T(8,128)(2,1)S(1)} %get-tuple-element.47.hot), custom_call_target="tpu_custom_call" | custom-call | tf_op jit(solution)/shard_map/pallas_call | solution.py:743
  70.1 1.2 %collective-permute-start.6 = (f32[1024,128]{1,0:T(8,128)S(1)}, f32[1024,128]{1,0:T(8,128)S(1)}, u32[]{:S(2)}, u32[]{:S(2)}) collective-permute-start(f32[1024,128]{1,0:T(8,128)S(1)} %get-tuple-element.60), channel_id=1, source_target_pairs={{0,16},{16,32},{32,48},{48,64},{64,80},{80,96},{96,112},{112,0},{1... | collective-permute-start | bytes 1572872 | tf_op jit(solution)/shard_map/ppermute | solution.py:720
  71.4 0.0 collective-permute-start.7
  71.4 6.3 %shard_map.88 = (f32[16,40,8,128]{3,2,1,0:T(8,128)S(1)}, f32[16,40,8,128]{3,2,1,0:T(8,128)S(1)}, f32[16,40,8,128]{3,2,1,0:T(8,128)S(1)}, f32[16,40,8,128]{3,2,1,0:T(8,128)S(1)}) custom-call(f32[8,128]{1,0:T(8,128)S(1)} %get-tuple-element.66.weighted, f32[848,128]{1,0:T(8,128)S(1)} %collective-permute-done.2.py_low, ...), custom_call_target="tpu_custom_call" | custom-call | bytes 25165824 | tf_op jit(solution)/shard_map/pallas_call | solution.py:743
  77.7 0.0 collective-permute-done.6.px_low
  77.7 2.6 %collective-permute-done.7.px_high = f32[1024,128]{1,0:T(8,128)S(1)} collective-permute-done((f32[1024,128]{1,0:T(8,128)S(1)}, f32[1024,128]{1,0:T(8,128)S(1)}, u32[]{:S(2)}, u32[]{:S(2)}) %collective-permute-start.7) | collective-permute-done | bytes 524320 | tf_op jit(solution)/shard_map/ppermute | solution.py:720
  80.3 7.2 %shard_map.89 = (f32[2048,128]{1,0:T(8,128)}, f32[16,40,8,128]{3,2,1,0:T(8,128)S(1)}, f32[16,40,8,128]{3,2,1,0:T(8,128)S(1)}, f32[16,40,8,128]{3,2,1,0:T(8,128)S(1)}, f32[16,40,8,128]{3,2,1,0:T(8,128)S(1)}) custom-call(f32[1024,128]{1,0:T(8,128)S(1)} %collective-permute-done.6.px_low, ...), custom_call_target="tpu_custom_call", output_to_operand_aliasing={{1}: (6, {}), {2}: (7, {}), {3}: (8, {}), {4}: (9, {})} | custom-call | tf_op jit(solution)/shard_map/pallas_call | solution.py:743
  (2 shorter events, 0.0 us)
Async XLA Ops:
  2.8 20.5 %copy-start = (f32[8]{0:T(128)S(1)}, f32[8]{0:T(128)}, u32[]{:S(2)}) copy-start(f32[8]{0:T(128)} %param.15) | copy-start | bytes 100
  2.8 25.9 %collective-permute-start = (f32[2816,128]{1,0:T(8,128)S(1)}, f32[2816,128]{1,0:T(8,128)S(1)}, u32[]{:S(2)}, u32[]{:S(2)}) collective-permute-start(f32[2816,128]{1,0:T(8,128)S(1)} %get-tuple-element.39), channel_id=1, source_target_pairs={{0,16},{16,32},{32,48},{48,64},{64,80},{80,96},{96,112},{112,0},{1... | collective-permute-start | bytes 4325384 | tf_op jit(solution)/shard_map/ppermute | solution.py:720
  5.9 22.9 %collective-permute-start.1 = (f32[2816,128]{1,0:T(8,128)S(1)}, f32[2816,128]{1,0:T(8,128)S(1)}, u32[]{:S(2)}, u32[]{:S(2)}) collective-permute-start(f32[2816,128]{1,0:T(8,128)S(1)} %get-tuple-element.40), channel_id=1, source_target_pairs={{0,112},{16,0},{32,16},{48,32},{64,48},{80,64},{96,80},{112,96},{1... | collective-permute-start | bytes 4325384 | tf_op jit(solution)/shard_map/ppermute | solution.py:720
  5.9 13.1 %collective-permute-start.2 = (f32[848,128]{1,0:T(8,128)S(1)}, f32[848,128]{1,0:T(8,128)S(1)}, u32[]{:S(2)}, u32[]{:S(2)}) collective-permute-start(f32[848,128]{1,0:T(8,128)S(1)} %get-tuple-element.41), channel_id=1, source_target_pairs={{0,1},{1,2},{2,3},{3,4},{4,5},{5,6},{6,7},{7,8},{8,9},{9,10},{10,1... | collective-permute-start | bytes 1302536 | tf_op jit(solution)/shard_map/ppermute | solution.py:720
  7.1 11.9 %collective-permute-start.3 = (f32[848,128]{1,0:T(8,128)S(1)}, f32[848,128]{1,0:T(8,128)S(1)}, u32[]{:S(2)}, u32[]{:S(2)}) collective-permute-start(f32[848,128]{1,0:T(8,128)S(1)} %get-tuple-element.42), channel_id=1, source_target_pairs={{0,15},{1,0},{2,1},{3,2},{4,3},{5,4},{6,5},{7,6},{8,7},{9,8},{10,9... | collective-permute-start | bytes 1302536 | tf_op jit(solution)/shard_map/ppermute | solution.py:720
  19.0 7.3 %collective-permute-start.4 = (f32[448,128]{1,0:T(8,128)S(1)}, f32[448,128]{1,0:T(8,128)S(1)}, u32[]{:S(2)}, u32[]{:S(2)}) collective-permute-start(f32[448,128]{1,0:T(8,128)S(1)} %get-tuple-element.45), channel_id=1, source_target_pairs={{0,16},{16,32},{32,48},{48,64},{64,80},{80,96},{96,112},{112,0},{1... | collective-permute-start | bytes 688136 | tf_op jit(solution)/shard_map/ppermute | solution.py:720
  23.3 5.4 %collective-permute-start.5 = (f32[448,128]{1,0:T(8,128)S(1)}, f32[448,128]{1,0:T(8,128)S(1)}, u32[]{:S(2)}, u32[]{:S(2)}) collective-permute-start(f32[448,128]{1,0:T(8,128)S(1)} %get-tuple-element.46.after), channel_id=1, source_target_pairs={{0,112},{16,0},{32,16},{48,32},{64,48},{80,64},{96,80},{112,96},{1... | collective-permute-start | bytes 688136 | tf_op jit(solution)/shard_map/ppermute | solution.py:720
  70.1 7.5 %collective-permute-start.6 = (f32[1024,128]{1,0:T(8,128)S(1)}, f32[1024,128]{1,0:T(8,128)S(1)}, u32[]{:S(2)}, u32[]{:S(2)}) collective-permute-start(f32[1024,128]{1,0:T(8,128)S(1)} %get-tuple-element.60), channel_id=1, source_target_pairs={{0,16},{16,32},{32,48},{48,64},{64,80},{80,96},{96,112},{112,0},{1... | collective-permute-start | bytes 1572872 | tf_op jit(solution)/shard_map/ppermute | solution.py:720
  71.4 8.9 %collective-permute-start.7 = (f32[1024,128]{1,0:T(8,128)S(1)}, f32[1024,128]{1,0:T(8,128)S(1)}, u32[]{:S(2)}, u32[]{:S(2)}) collective-permute-start(f32[1024,128]{1,0:T(8,128)S(1)} %get-tuple-element.61), channel_id=1, source_target_pairs={{0,112},{16,0},{32,16},{48,32},{64,48},{80,64},{96,80},{112,96},{1... | collective-permute-start | bytes 1572872 | tf_op jit(solution)/shard_map/ppermute | solution.py:720
